TPU v7x, 32 devices: a whole 2x2x4 slice. The times are simulated.
32 devices in a mesh: row: 8 (over z, y), col: 4 (over x, core).
Axes of the slice: x: 2, y: 2, z: 4, core: 2. Of those that a mesh axis runs over, the one named last changes fastest.
Arguments:
- right_side: bfloat16 [256, 32, 128], P(('row', 'col')), may hold values from -6 to 6
- leaf_lower: bfloat16 [256, 128, 128], P(('row', 'col')), may hold values from -0.5 to 0.5
- leaf_upper: bfloat16 [256, 128, 128], P(('row', 'col')), may hold values from -0.5 to 0.5
- lower_blocks: bfloat16 [256, 2, 128, 1024], P(('row', 'col')), may hold values from -0.09375 to 0.09375
- upper_blocks: bfloat16 [256, 2, 1024, 128], P(('row', 'col')), may hold values from -0.125 to 0.125
- parent_rhs: bfloat16 [16, 32, 1024], P('row'), may hold values from -6 to 6
- parent_lower: bfloat16 [16, 1024, 1024], P('row', None, 'col'), may hold values from -0.1875 to 0.1875
- parent_upper: bfloat16 [16, 1024, 1024], P('row', None, 'col'), may hold values from -0.1875 to 0.1875
- targets: int32 [256, 2], P(('row', 'col')), may hold values from 0 to 3, all different within a row
Outputs:
- leaf_solution: float32 [256, 32, 128], P(('row', 'col'))
- parent_solution: float32 [16, 32, 1024], P('row', None, 'col')
Inputs may be any that keep to these rules, and one draw needn't show every extreme that they name: `targets`: each leaf lists 2 different window indices; index j below 2 names a parent of the leaf's own process row, the others one of the next row (the last row's next is the first).
All inputs are finite; a program needn't handle non-finite values.
Results may differ from a plain program's by a relative error of at most 0.0075.
Values may be sent and summed in bfloat16 or wider, within the bound.
No kernel may reach another device: no remote copies, remote signals or barrier semaphores. Data moves between devices by JAX's collectives and lax.ppermute only.
A program may use at most 128 MiB of HBM per device.

v0:
```python
import jax
import jax.numpy as jnp
from jax import lax
from jax.sharding import PartitionSpec as P


def from_behind(array, axis, by):
    peers = lax.axis_size(axis)
    return lax.ppermute(array, axis, [(i, (i + by) % peers) for i in range(peers)])


def local(
    right_side,
    leaf_lower,
    leaf_upper,
    lower_blocks,
    upper_blocks,
    parent_rhs,
    parent_lower,
    parent_upper,
    targets,
):
    highest = lax.Precision.HIGHEST
    local_parents = parent_rhs.shape[0]
    solved = jnp.einsum(
        "anw,awv->anv", right_side, leaf_lower, preferred_element_type=jnp.float32
    ).astype(jnp.bfloat16)
    terms = jnp.einsum("anw,akwv->aknv", solved, lower_blocks, preferred_element_type=jnp.float32)
    window_ids = jnp.arange(2 * local_parents, dtype=jnp.int32)
    selector = (targets[:, :, None] == window_ids[None, None, :]).astype(jnp.float32)
    partial_sums = jnp.einsum("akj,aknv->jnv", selector, terms, precision=highest)
    incoming = from_behind(partial_sums[local_parents:], "row", 1)
    totals = lax.psum(partial_sums[:local_parents] + incoming, "col")
    combined = (parent_rhs.astype(jnp.float32) - totals).astype(jnp.bfloat16)
    forward_parent = jnp.einsum(
        "tnw,twv->tnv", combined, parent_lower, preferred_element_type=jnp.float32
    ).astype(jnp.bfloat16)
    parent_solution = jnp.einsum(
        "tnw,twv->tnv",
        lax.all_gather(forward_parent, "col", axis=2, tiled=True),
        parent_upper,
        preferred_element_type=jnp.float32,
    )
    rounded = parent_solution.astype(jnp.bfloat16)
    own_full = lax.all_gather(rounded, "col", axis=2, tiled=True)
    next_full = from_behind(own_full, "row", -1)
    window = jnp.concatenate([own_full, next_full], axis=0)
    picked = jnp.einsum(
        "akj,jnv->aknv", selector.astype(jnp.bfloat16), window, preferred_element_type=jnp.float32
    ).astype(jnp.bfloat16)
    coupling = jnp.einsum(
        "aknv,akvw->anw", picked, upper_blocks, preferred_element_type=jnp.float32
    )
    reduced = (solved.astype(jnp.float32) - coupling).astype(jnp.bfloat16)
    leaf_solution = jnp.einsum(
        "anw,awv->anv", reduced, leaf_upper, preferred_element_type=jnp.float32
    )
    return (leaf_solution, parent_solution)


def solution(mesh):
    placed = (
        P(("row", "col"), None, None),
        P(("row", "col"), None, None),
        P(("row", "col"), None, None),
        P(("row", "col"), None, None, None),
        P(("row", "col"), None, None, None),
        P("row", None, None),
        P("row", None, "col"),
        P("row", None, "col"),
        P(("row", "col"), None),
    )
    return jax.shard_map(
        local,
        mesh=mesh,
        in_specs=placed,
        out_specs=(P(("row", "col"), None, None), P("row", None, "col")),
        check_vma=False,
    )
```

profile of v0, /device:TPU:0, one launch (start us, length us, event | category | flops | bytes accessed | tf_op | source)
XLA Modules:
  0.0 89.9 jit_solution(4337251285470712476)
XLA Ops:
  7.2 0.0 copy-start
  7.2 0.0 all-reduce.2.cloned.1.call-start
  7.2 1.2 %convolution_convert_fusion = bf16[8,32,128]{2,1,0:T(8,128)(2,1)S(1)} fusion(bf16[8,32,128]{2,1,0:T(8,128)(2,1)} %param.9, bf16[8,128,128]{2,1,0:T(8,128)(2,1)} %param.10), kind=kOutput, calls=%fused_computation.8 | convolution fusion | flops 8421376 | bytes 393216 | tf_op jit(solution)/shard_map/anw,awv->anv/dot_general | solution.py:25
  8.5 0.0 copy-start.4
  8.5 2.9 %fusion.13 = f32[8,32,2,1024]{3,1,2,0:T(8,128)S(1)} fusion(bf16[8,2,128,1024]{3,2,1,0:T(8,128)(2,1)} %param.12, bf16[8,32,128]{2,1,0:T(8,128)(2,1)S(1)} %convolution_convert_fusion), kind=kOutput, calls=%fused_computation.18 | convolution fusion | flops 134217728 | bytes 6356992 | tf_op jit(solution)/shard_map/anw,akwv->aknv/dot_general | solution.py:28
  11.4 0.0 copy-start.3
  11.4 0.0 copy-start.1
  11.4 0.0 copy-start.2
  11.4 2.1 %fusion.3 = f32[4,32,1024]{2,0,1:T(4,128)S(1)} fusion(f32[8,32,2,1024]{3,1,2,0:T(8,128)S(1)} %fusion.13, s32[8,2]{0,1:T(2,128)S(1)} %copy-done.4), kind=kOutput, calls=%fused_computation.4 | convolution fusion | flops 25165888 | bytes 2621504 | tf_op jit(solution)/shard_map/akj,aknv->jnv/dot_general | solution.py:31
  13.5 0.1 slice.9
  13.6 3.0 %collective-permute-start = (f32[2,32,1024]{2,0,1:T(2,128)S(1)}, f32[2,32,1024]{2,0,1:T(2,128)S(1)}, u32[]{:S(2)}, u32[]{:S(2)}) collective-permute-start(f32[2,32,1024]{2,0,1:T(2,128)S(1)} %slice.9), channel_id=1, source_target_pairs={{0,4},{4,8},{8,12},{12,16},{16,20},{20,24},{24,28},{28,0},{1,5},{5... | collective-permute-start | bytes 786440 | tf_op jit(solution)/shard_map/ppermute | solution.py:9
  16.6 9.3 %collective-permute-done = f32[2,32,1024]{2,0,1:T(2,128)S(1)} collective-permute-done((f32[2,32,1024]{2,0,1:T(2,128)S(1)}, f32[2,32,1024]{2,0,1:T(2,128)S(1)}, u32[]{:S(2)}, u32[]{:S(2)}) %collective-permute-start) | collective-permute-done | bytes 262176 | tf_op jit(solution)/shard_map/ppermute | solution.py:9
  26.0 0.9 slice_add_fusion
  26.9 0.0 all-reduce.2.cloned.1.call-update
  26.9 30.6 %all-reduce.2.cloned.1.call-done = f32[2,32,1024]{2,0,1:T(2,128)} async-done(((f32[2,32,1024]{2,0,1:T(2,128)}), f32[2,32,1024]{2,0,1:T(2,128)}) %all-reduce.2.cloned.1.call-update) | async-done | bytes 262160 | tf_op jit(solution)/shard_map/psum | solution.py:33
  57.4 1.1 %subtract_convert_fusion = bf16[2,32,1024]{2,0,1:T(2,128)(2,1)S(1)} fusion(f32[2,32,1024]{2,0,1:T(2,128)} %all-reduce.2.cloned.1.call-done, bf16[2,32,1024]{2,1,0:T(8,128)(2,1)S(1)} %copy-done.3), kind=kLoop, calls=%fused_computation.15 | loop fusion | flops 196608 | bytes 524288 | tf_op jit(solution)/shard_map/convert_element_type | solution.py:34
  58.6 0.3 convolution_convert_fusion.1
  58.9 5.4 %all_gather.6 = bf16[2,32,1024]{2,1,0:T(8,128)(2,1)S(1)} all-gather(bf16[2,32,256]{2,1,0:T(8,128)(2,1)S(1)} %convolution_convert_fusion.1), channel_id=1, replica_groups=mesh['row'=8,'col'=4] {'col'}, dimensions={2}, use_global_device_ids=true | all-gather | bytes 163840 | tf_op jit(solution)/shard_map/all_gather | solution.py:40
  64.3 0.9 %fusion.21 = (bf16[2,32,256]{2,1,0:T(8,128)(2,1)S(1)}, f32[2,32,256]{2,1,0:T(8,128)}) fusion(bf16[2,32,1024]{2,1,0:T(8,128)(2,1)S(1)} %all_gather.6, bf16[2,1024,256]{2,1,0:T(8,128)(2,1)S(1)} %copy-done), kind=kOutput, calls=%fused_computation.26 | convolution fusion | flops 33570816 | bytes 1277952 | tf_op jit(solution)/shard_map/tnw,twv->tnv/dot_general | solution.py:38
  65.2 5.4 %all_gather.7 = bf16[2,32,1024]{2,1,0:T(8,128)(2,1)S(1)} all-gather(bf16[2,32,256]{2,1,0:T(8,128)(2,1)S(1)} %get-tuple-element.2), channel_id=1, replica_groups=mesh['row'=8,'col'=4] {'col'}, dimensions={2}, use_global_device_ids=true | all-gather | bytes 163840 | tf_op jit(solution)/shard_map/all_gather | solution.py:45
  70.6 4.2 %collective-permute-start.1 = (bf16[2,32,1024]{2,1,0:T(8,128)(2,1)S(1)}, bf16[2,32,1024]{2,1,0:T(8,128)(2,1)S(1)}, u32[]{:S(2)}, u32[]{:S(2)}) collective-permute-start(bf16[2,32,1024]{2,1,0:T(8,128)(2,1)S(1)} %all_gather.7), channel_id=1, source_target_pairs={{0,28},{4,0},{8,4},{12,8},{16,12},{20,16},{24,20},{28,24},{1,29},{... | collective-permute-start | bytes 393224 | tf_op jit(solution)/shard_map/ppermute | solution.py:9
  74.8 3.3 %collective-permute-done.1 = bf16[2,32,1024]{2,1,0:T(8,128)(2,1)S(1)} collective-permute-done((bf16[2,32,1024]{2,1,0:T(8,128)(2,1)S(1)}, bf16[2,32,1024]{2,1,0:T(8,128)(2,1)S(1)}, u32[]{:S(2)}, u32[]{:S(2)}) %collective-permute-start.1) | collective-permute-done | bytes 131104 | tf_op jit(solution)/shard_map/ppermute | solution.py:9
  78.1 0.5 fusion.9
  78.6 4.4 %fusion.8 = f32[8,32,128]{2,1,0:T(8,128)} fusion(bf16[8,128,128]{2,1,0:T(8,128)(2,1)S(1)} %copy-done.2, bf16[8,2,1024,128]{3,2,1,0:T(8,128)(2,1)} %param.13, bf16[8,2,32,1024]{3,0,2,1:T(8,128)(2,1)S(1)} %fusion.9, bf16[8,32,128]{2,1,0:T(8,128)(2,1)S(1)} %convolution_convert_fusion), kind=kOutput, calls=%fused_computation.9 | convolution fusion | flops 142704640 | bytes 5701632 | tf_op jit(solution)/shard_map/anw,awv->anv/dot_general | solution.py:55
  (6 shorter events, 0.0 us)
Async XLA Ops:
  7.2 57.1 %copy-start = (bf16[2,1024,256]{2,1,0:T(8,128)(2,1)S(1)}, bf16[2,1024,256]{2,1,0:T(8,128)(2,1)}, u32[]{:S(2)}) copy-start(bf16[2,1024,256]{2,1,0:T(8,128)(2,1)} %param.16) | copy-start | bytes 3145732
  7.2 50.3 %all-reduce.2.cloned.1.call-start = ((), (), s32[]{:S(2)}) async-start(), calls=%async_computation | async-start | bytes 524288 | tf_op jit(solution)/shard_map/psum | solution.py:33
  8.5 2.9 %copy-start.4 = (s32[8,2]{0,1:T(2,128)S(1)}, s32[8,2]{0,1:T(2,128)}, u32[]{:S(2)}) copy-start(s32[8,2]{0,1:T(2,128)} %param.17) | copy-start | bytes 196
  11.4 46.1 %copy-start.3 = (bf16[2,32,1024]{2,1,0:T(8,128)(2,1)S(1)}, bf16[2,32,1024]{2,1,0:T(8,128)(2,1)}, u32[]{:S(2)}) copy-start(bf16[2,32,1024]{2,1,0:T(8,128)(2,1)} %param.14) | copy-start | bytes 393220
  11.4 47.2 %copy-start.1 = (bf16[2,1024,256]{2,1,0:T(8,128)(2,1)S(1)}, bf16[2,1024,256]{2,1,0:T(8,128)(2,1)}, u32[]{:S(2)}) copy-start(bf16[2,1024,256]{2,1,0:T(8,128)(2,1)} %param.15) | copy-start | bytes 3145732
  11.4 67.3 %copy-start.2 = (bf16[8,128,128]{2,1,0:T(8,128)(2,1)S(1)}, bf16[8,128,128]{2,1,0:T(8,128)(2,1)}, u32[]{:S(2)}) copy-start(bf16[8,128,128]{2,1,0:T(8,128)(2,1)} %param.11) | copy-start | bytes 786436
  13.6 12.4 %collective-permute-start = (f32[2,32,1024]{2,0,1:T(2,128)S(1)}, f32[2,32,1024]{2,0,1:T(2,128)S(1)}, u32[]{:S(2)}, u32[]{:S(2)}) collective-permute-start(f32[2,32,1024]{2,0,1:T(2,128)S(1)} %slice.9), channel_id=1, source_target_pairs={{0,4},{4,8},{8,12},{12,16},{16,20},{20,24},{24,28},{28,0},{1,5},{5... | collective-permute-start | bytes 786440 | tf_op jit(solution)/shard_map/ppermute | solution.py:9
  70.6 7.5 %collective-permute-start.1 = (bf16[2,32,1024]{2,1,0:T(8,128)(2,1)S(1)}, bf16[2,32,1024]{2,1,0:T(8,128)(2,1)S(1)}, u32[]{:S(2)}, u32[]{:S(2)}) collective-permute-start(bf16[2,32,1024]{2,1,0:T(8,128)(2,1)S(1)} %all_gather.7), channel_id=1, source_target_pairs={{0,28},{4,0},{8,4},{12,8},{16,12},{20,16},{24,20},{28,24},{1,29},{... | collective-permute-start | bytes 393224 | tf_op jit(solution)/shard_map/ppermute | solution.py:9
Sparse Core Ops, SparseCore 0:
  27.0 30.3 all-reduce.1
where the time goes:
time: 90.1 us; the launch traced here: 89.9 us
  waiting for transfers between devices  43.2 us (48%)
  between operations  14.1 us (16%)
  matrix products  12.2 us (14%)
  blocking collectives  10.8 us (12%)
  starting transfers between devices  7.3 us (8%)
  other arithmetic  2.03 us (2%)
    psum x1, waiting for transfers between devices, local(): totals = lax.psum(partial_sums[:local_parents] + incoming, 'col')  30.6 us
    ppermute x2, waiting for transfers between devices, from_behind(): lax.ppermute(array, axis, [(i, (i + by) % peers) for i in range(peers)])  12.6 us
    ppermute x2, starting transfers between devices, from_behind(): lax.ppermute(array, axis, [(i, (i + by) % peers) for i in range(peers)])  7.26 us
    all_gather x1, blocking collectives, local(): lax.all_gather(forward_parent, 'col', axis=2, tiled=True)  5.42 us
    all_gather x1, blocking collectives, local(): own_full = lax.all_gather(rounded, 'col', axis=2, tiled=True)  5.41 us
    dot_general x1, matrix products, local(): jnp.einsum('anw,awv->anv', reduced, leaf_upper, preferred_element_type=jn...  4.38 us
    dot_general x1, matrix products, local(): jnp.einsum('anw,akwv->aknv', solved, lower_blocks, preferred_element_type...  2.89 us
    dot_general x1, matrix products, local(): jnp.einsum('akj,aknv->jnv', selector, terms, precision=highest)  2.07 us
  transfers between devices with their start and end apart: 3, of which 3 were waited for; matrix products, arithmetic and copies ran while one was open for 0% of the time, Pallas kernels for 0%

commit v1 on v0

v1 whole, which is shorter than its diff:
```python
import functools

import jax
import jax.numpy as jnp
from jax import lax
from jax.experimental import pallas as pl
from jax.experimental.pallas import tpu as pltpu
from jax.sharding import PartitionSpec as P

CORES = 2
F32 = jnp.float32
BF16 = jnp.bfloat16
VMEM = pl.BlockSpec(memory_space=pltpu.VMEM)
SMEM = pl.BlockSpec(memory_space=pltpu.SMEM)
ANY = pl.BlockSpec(memory_space=pl.ANY)


def dot(a, b):
    return jnp.dot(a, b, preferred_element_type=F32)


def send(array, rows, cols, by_row, by_chip, flip):
    chips = cols // CORES
    pairs = []
    for row in range(rows):
        for col in range(cols):
            chip, core = col // CORES, col % CORES
            to = ((chip + by_chip) % chips) * CORES + (core ^ flip)
            pairs.append((row * cols + col, ((row + by_row) % rows) * cols + to))
    return lax.ppermute(array, ("row", "col"), pairs)


def forward_kernel(where, targets, rhs_hbm, lower_hbm, blocks_hbm, solved_ref, keep_ref, send_ref, rhs, lower, blocks, acc, sems):
    leaves, k, width, wide = blocks.shape
    nrhs = rhs.shape[1]
    first = [
        pltpu.make_async_copy(rhs_hbm, rhs, sems.at[0]),
        pltpu.make_async_copy(lower_hbm, lower, sems.at[1]),
    ]
    copies = [pltpu.make_async_copy(blocks_hbm.at[a], blocks.at[a], sems.at[2 + a]) for a in range(leaves)]
    for copy in first + copies:
        copy.start()
    core = where[0]
    slots = (core, 2 + core, 1 - core, 3 - core)
    for copy in first:
        copy.wait()
    solved = [dot(rhs[a], lower[a]).astype(BF16) for a in range(leaves)]
    for a in range(leaves):
        solved_ref[a] = solved[a]
    step = 2
    for a0 in range(0, leaves, step):
        for a in range(a0, a0 + step):
            copies[a].wait()
        lhs = jnp.concatenate(
            [
                jnp.concatenate(
                    [
                        jnp.where(targets[a, i] == slot, solved[a], jnp.zeros_like(solved[a]))
                        for a in range(a0, a0 + step)
                        for i in range(k)
                    ],
                    axis=1,
                )
                for slot in slots
            ],
            axis=0,
        )
        part = dot(lhs, blocks[pl.ds(a0, step)].reshape(step * k * width, wide))
        if a0 == 0:
            acc[...] = part
        elif a0 + step < leaves:
            acc[...] += part
        else:
            total = acc[...] + part
            keep_ref[...] = total[: 2 * nrhs].reshape(2, nrhs, wide)
            send_ref[...] = total[2 * nrhs :].astype(BF16).reshape(2, nrhs, wide)


def parent_kernel(pieces, incoming, where, keep, came, rhs, lower, lower_other, upper, *rest):
    rest = list(rest)
    others = [rest.pop(0) for _ in range(pieces)]
    sums = [rest.pop(0) for _ in range(incoming)]
    full_ref, half_ref, forward = rest
    core, chip = where[0], where[1]
    chips = pieces + 1
    chips = (pieces + 1) // CORES
    cut = lower.shape[2]
    update = keep[0] + came[0].astype(F32)
    for term in sums:
        update = update + term[...].astype(F32)
    combined = (rhs[core].astype(F32) - update).astype(BF16)
    mine = pl.multiple_of(core * cut, cut)
    theirs = pl.multiple_of((1 - core) * cut, cut)
    forward[:, pl.ds(mine, cut)] = dot(combined, lower[core]).astype(BF16)
    forward[:, pl.ds(theirs, cut)] = dot(combined, lower_other[...]).astype(BF16)
    depth = forward.shape[1]
    lhs = forward[...]
    rows = pl.ds(pl.multiple_of(chip * depth, depth), depth)
    piece = 0
    for by in range(chips):
        for flip in range(CORES):
            source = lax.rem(chip + chips - by, chips) * CORES + (core if flip == 0 else 1 - core)
            if by == 0 and flip == 0:
                block = upper[core, rows, :]
            else:
                block = others[piece][...]
                piece += 1
            part = dot(lhs, block)
            at = pl.ds(pl.multiple_of(source * cut, cut), cut)
            full_ref[:, at] = part
            half_ref[:, at] = part.astype(BF16)


def backward_kernel(where, targets, solved, own, mine, theirs, blocks_hbm, upper, leaf_ref, parent_ref, window, blocks, sems):
    leaves, k, wide, width = blocks.shape
    copies = [pltpu.make_async_copy(blocks_hbm.at[a], blocks.at[a], sems.at[a]) for a in range(leaves)]
    for copy in copies:
        copy.start()
    core, chip = where[0], where[1]
    for level in range(2):
        window[2 * level + core] = mine[level]
        window[2 * level + 1 - core] = theirs[level]
    cut = parent_ref.shape[2]
    at = pl.ds(pl.multiple_of((chip * CORES + core) * cut, cut), cut)
    parent_ref[core] = own[:, at]
    parent_ref[1 - core] = theirs[0, :, at].astype(F32)
    for a in range(leaves):
        copies[a].wait()
        lhs = jnp.concatenate([window[targets[a, i]] for i in range(k)], axis=1)
        coupling = dot(lhs, blocks[a].reshape(k * wide, width))
        reduced = (solved[a].astype(F32) - coupling).astype(BF16)
        leaf_ref[a] = dot(reduced, upper[a])


def local(
    right_side, leaf_lower, leaf_upper, lower_blocks, upper_blocks, parent_rhs, parent_lower, parent_upper, targets
):
    rows, cols = lax.axis_size("row"), lax.axis_size("col")
    chips = cols // CORES
    here = lax.axis_index("col")
    core, chip = here % CORES, here // CORES
    where = jnp.stack([core, chip]).astype(jnp.int32)
    go = functools.partial(send, rows=rows, cols=cols)
    leaves, k, width, wide = lower_blocks.shape
    nrhs = right_side.shape[1]
    cut = parent_lower.shape[2]
    depth = cut * CORES

    upper_view = parent_upper.reshape(2, chips, depth, cut)
    lower_other = go(lax.dynamic_index_in_dim(parent_lower, 1 - core, 0, False), by_row=0, by_chip=0, flip=1)
    pieces = []
    for by in range(chips):
        for flip in range(CORES):
            if by == 0 and flip == 0:
                continue
            block = lax.dynamic_slice(
                upper_view, (core ^ flip, (chip + by) % chips, 0, 0), (1, 1, depth, cut)
            ).reshape(depth, cut)
            pieces.append(go(block, by_row=0, by_chip=by, flip=flip))

    solved, keep, give = pl.pallas_call(
        forward_kernel,
        in_specs=[SMEM, SMEM, ANY, ANY, ANY],
        out_specs=[VMEM, VMEM, VMEM],
        out_shape=[
            jax.ShapeDtypeStruct((leaves, nrhs, width), BF16),
            jax.ShapeDtypeStruct((2, nrhs, wide), F32),
            jax.ShapeDtypeStruct((2, nrhs, wide), BF16),
        ],
        scratch_shapes=[
            pltpu.VMEM(right_side.shape, BF16),
            pltpu.VMEM(leaf_lower.shape, BF16),
            pltpu.VMEM(lower_blocks.shape, BF16),
            pltpu.VMEM((4 * nrhs, wide), F32),
            pltpu.SemaphoreType.DMA((2 + leaves,)),
        ],
        compiler_params=pltpu.CompilerParams(vmem_limit_bytes=24 << 20),
        cost_estimate=pl.CostEstimate(flops=1 << 29, bytes_accessed=5 << 20, transcendentals=0),
        name="forward",
    )(where, targets, right_side, leaf_lower, lower_blocks)

    came = go(give, by_row=0, by_chip=0, flip=1)
    chip_sum = (keep + came.astype(F32)).astype(BF16)
    sums = [go(chip_sum[1], by_row=1, by_chip=by, flip=0) for by in range(chips)]
    sums += [go(chip_sum[0], by_row=0, by_chip=by, flip=0) for by in range(1, chips)]

    full, half = pl.pallas_call(
        functools.partial(parent_kernel, len(pieces), len(sums)),
        in_specs=[SMEM] + [VMEM] * (6 + len(pieces) + len(sums)),
        out_specs=[VMEM, VMEM],
        out_shape=[jax.ShapeDtypeStruct((nrhs, wide), F32), jax.ShapeDtypeStruct((nrhs, wide), BF16)],
        scratch_shapes=[pltpu.VMEM((nrhs, depth), BF16)],
        compiler_params=pltpu.CompilerParams(vmem_limit_bytes=24 << 20),
        cost_estimate=pl.CostEstimate(flops=1 << 27, bytes_accessed=4 << 20, transcendentals=0),
        name="parent",
    )(where, keep, came, parent_rhs, parent_lower, lower_other, parent_upper, *pieces, *sums)

    nexts = [go(half, by_row=-1, by_chip=by, flip=0) for by in range(chips)]
    own = full
    for by in range(1, chips):
        own = own + go(half, by_row=0, by_chip=by, flip=0).astype(F32)
    after = functools.reduce(jnp.add, [term.astype(F32) for term in nexts])
    mine = jnp.stack([own, after]).astype(BF16)
    theirs = go(mine, by_row=0, by_chip=0, flip=1)

    return pl.pallas_call(
        backward_kernel,
        in_specs=[SMEM, SMEM, VMEM, VMEM, VMEM, VMEM, ANY, VMEM],
        out_specs=[VMEM, VMEM],
        out_shape=[
            jax.ShapeDtypeStruct((leaves, nrhs, width), F32),
            jax.ShapeDtypeStruct((2, nrhs, cut), F32),
        ],
        scratch_shapes=[
            pltpu.VMEM((4, nrhs, wide), BF16),
            pltpu.VMEM(upper_blocks.shape, BF16),
            pltpu.SemaphoreType.DMA((leaves,)),
        ],
        compiler_params=pltpu.CompilerParams(vmem_limit_bytes=24 << 20),
        cost_estimate=pl.CostEstimate(flops=1 << 28, bytes_accessed=5 << 20, transcendentals=0),
        name="backward",
    )(where, targets, solved, own, mine, theirs, upper_blocks, leaf_upper)


def solution(mesh):
    placed = (
        P(("row", "col"), None, None),
        P(("row", "col"), None, None),
        P(("row", "col"), None, None),
        P(("row", "col"), None, None, None),
        P(("row", "col"), None, None, None),
        P("row", None, None),
        P("row", None, "col"),
        P("row", None, "col"),
        P(("row", "col"), None),
    )
    return jax.shard_map(
        local,
        mesh=mesh,
        in_specs=placed,
        out_specs=(P(("row", "col"), None, None), P("row", None, "col")),
        check_vma=False,
    )
```

time: 90.1 us -> 48.7 us (0.54)
  waiting for transfers between devices: 43.2 us -> 21.8 us
  between operations: 14.1 us -> 0.74 us
  matrix products: 12.2 us -> 0 us
  blocking collectives: 10.8 us -> 0 us
  Pallas kernels: 0 us -> 8.21 us
  local copies, waits for them, and re-layouts: 0.17 us -> 5.65 us
  starting transfers between devices: 7.3 us -> 11.9 us
  other arithmetic: 2.03 us -> 0.16 us
    psum x1 -> x0, waiting for transfers between devices: 30.6 us -> none  [local(): totals = lax.psum(partial_sums[:local_parents] + incoming, 'col')]
    dot_general x7 -> x0, matrix products: 12.2 us -> none  [the longest x1 4.38 us: local(): jnp.einsum('anw,awv->anv', reduced, leaf_upper, preferred_element_type=jn...]
    all_gather x2 -> x0, blocking collectives: 10.8 us -> none  [the longest x1 5.42 us: local(): lax.all_gather(forward_parent, 'col', axis=2, tiled=True)]
    ppermute x2 -> x12, waiting for transfers between devices: 12.6 us -> 21.8 us  [send(): return lax.ppermute(array, ('row', 'col'), pairs)]
    pallas_call x0 -> x3, Pallas kernels: none -> 8.21 us  [the longest x1 4.27 us: local(): pl.pallas_call(backward_kernel, in_specs=[SMEM, SMEM, VMEM, VMEM, VMEM, V...]
    unnamed x10 -> x17, local copies, waits for them, and re-layouts: 0.03 us -> 4.75 us
    ppermute x2 -> x12, starting transfers between devices: 7.26 us -> 11.9 us  [send(): return lax.ppermute(array, ('row', 'col'), pairs)]
    convert_element_type x1, other arithmetic: 1.13 us -> 0.03 us  [local(): chip_sum = (keep + came.astype(F32)).astype(BF16)]
  transfers between devices with their start and end apart: 3 -> 12, of which waited for: 3 -> 6; matrix products, arithmetic and copies ran while one was open for 0% -> 2% of each run, Pallas kernels for 0% -> 0%
where the time goes in v1:
time: 48.7 us; the launch traced here: 48.5 us
  waiting for transfers between devices  21.8 us (45%)
  starting transfers between devices  11.9 us (24%)
  Pallas kernels  8.21 us (17%)
  local copies, waits for them, and re-layouts  5.65 us (12%)
  between operations  0.74 us (2%)
    ppermute x12, waiting for transfers between devices, send(): return lax.ppermute(array, ('row', 'col'), pairs)  21.8 us
    ppermute x12, starting transfers between devices, send(): return lax.ppermute(array, ('row', 'col'), pairs)  11.9 us
    unnamed x17, local copies, waits for them, and re-layouts  4.75 us
    pallas_call x1, Pallas kernels, local(): pl.pallas_call(backward_kernel, in_specs=[SMEM, SMEM, VMEM, VMEM, VMEM, V...  4.27 us
    pallas_call x1, Pallas kernels, local(): pl.pallas_call(forward_kernel, in_specs=[SMEM, SMEM, ANY, ANY, ANY], out_...  2.85 us
    pallas_call x1, Pallas kernels, local(): pl.pallas_call(functools.partial(parent_kernel, len(pieces), len(sums)),...  1.08 us
  transfers between devices with their start and end apart: 12, of which 6 were waited for; matrix products, arithmetic and copies ran while one was open for 2% of the time, Pallas kernels for 0%

profile of v1, /device:TPU:0, one launch (start us, length us, event | category | flops | bytes accessed | tf_op | source)
XLA Modules:
  0.0 48.5 jit_solution(11953835405607444121)
XLA Ops:
  0.6 0.8 %copy.12.targets = s32[8,2]{1,0:T(8,128)S(1)} copy(s32[8,2]{0,1:T(2,128)} %param.17) | data formatting | bytes 128 | tf_op args[8]
  1.4 0.1 pad_add_fusion.where
  1.5 2.2 %copy-done = bf16[8,2,128,1024]{3,2,1,0:T(8,128)(2,1)S(1)} copy-done((bf16[8,2,128,1024]{3,2,1,0:T(8,128)(2,1)S(1)}, bf16[8,2,128,1024]{3,2,1,0:T(8,128)(2,1)}, u32[]{:S(2)}) %copy-start) | copy-done | bytes 4194328
  3.7 0.9 %copy-done.4 = bf16[8,128,128]{2,1,0:T(8,128)(2,1)S(1)} copy-done((bf16[8,128,128]{2,1,0:T(8,128)(2,1)S(1)}, bf16[8,128,128]{2,1,0:T(8,128)(2,1)}, u32[]{:S(2)}) %copy-start.4) | copy-done | bytes 262168
  4.6 0.8 %copy-done.7 = bf16[8,32,128]{2,1,0:T(8,128)(2,1)S(1)} copy-done((bf16[8,32,128]{2,1,0:T(8,128)(2,1)S(1)}, bf16[8,32,128]{2,1,0:T(8,128)(2,1)}, u32[]{:S(2)}) %copy-start.7) | copy-done | bytes 65560
  5.5 2.9 %forward.1 = (bf16[8,32,128]{2,1,0:T(8,128)(2,1)S(1)}, f32[2,32,1024]{2,1,0:T(8,128)S(1)}, bf16[2,32,1024]{2,1,0:T(8,128)(2,1)}) custom-call(s32[2]{0:T(128)S(1)} %pad_add_fusion.where, s32[8,2]{1,0:T(8,128)S(1)} %copy.12.targets, bf16[8,32,128]{2,1,0:T(8,128)(2,1)S(1)} %copy-done.7, bf16[8,128,128]{2,1,0:T(8,128)(2,1)S(1)} %copy-done.4, ...), custom_call_target="tpu_custom_call" | custom-call | flops 536870912 | bytes 5242880 | tf_op jit(solution)/shard_map/forward/pallas_call | solution.py:161
  8.3 0.5 %collective-permute-start = (bf16[2,32,1024]{2,1,0:T(8,128)(2,1)}, bf16[2,32,1024]{2,1,0:T(8,128)(2,1)S(1)}, u32[]{:S(2)}, u32[]{:S(2)}) collective-permute-start(bf16[2,32,1024]{2,1,0:T(8,128)(2,1)} %get-tuple-element.9), channel_id=1, source_target_pairs={{0,1},{1,0},{2,3},{3,2},{4,5},{5,4},{6,7},{7,6},{8,9},{9,8},{10,11... | collective-permute-start | bytes 393224 | tf_op jit(solution)/shard_map/ppermute | solution.py:30
  8.8 0.8 %dynamic-slice_bitcast_fusion = bf16[1024,256]{1,0:T(8,128)(2,1)} fusion(bf16[2,1024,256]{2,1,0:T(8,128)(2,1)S(1)} %copy-done.3, s32[]{:T(128)S(6)} %select_n.41), kind=kLoop, calls=%fused_computation | loop fusion | bytes 1048580 | tf_op jit(solution)/shard_map/jit(dynamic_index_in_dim)/squeeze | solution.py:150
  9.8 0.5 %collective-permute-start.2 = (bf16[512,256]{1,0:T(8,128)(2,1)S(1)}, bf16[512,256]{1,0:T(8,128)(2,1)S(1)}, u32[]{:S(2)}, u32[]{:S(2)}) collective-permute-start(bf16[512,256]{1,0:T(8,128)(2,1)S(1)} %get-tuple-element.16), channel_id=1, source_target_pairs={{0,1},{1,0},{2,3},{3,2},{4,5},{5,4},{6,7},{7,6},{8,9},{9,8},{10,11... | collective-permute-start | bytes 786440 | tf_op jit(solution)/shard_map/ppermute | solution.py:30
  10.3 2.6 %collective-permute-start.3 = (bf16[512,256]{1,0:T(8,128)(2,1)S(1)}, bf16[512,256]{1,0:T(8,128)(2,1)S(1)}, u32[]{:S(2)}, u32[]{:S(2)}) collective-permute-start(bf16[512,256]{1,0:T(8,128)(2,1)S(1)} %get-tuple-element.15), channel_id=1, source_target_pairs={{0,2},{1,3},{2,0},{3,1},{4,6},{5,7},{6,4},{7,5},{8,10},{9,11},{10,... | collective-permute-start | bytes 786440 | tf_op jit(solution)/shard_map/ppermute | solution.py:30
  12.9 0.1 collective-permute-start.4
  13.0 1.8 %collective-permute-start.5 = (bf16[32,1024]{1,0:T(8,128)(2,1)S(1)}, bf16[32,1024]{1,0:T(8,128)(2,1)S(1)}, u32[]{:S(2)}, u32[]{:S(2)}) collective-permute-start(bf16[32,1024]{1,0:T(8,128)(2,1)S(1)} %get-tuple-element.18), channel_id=1, source_target_pairs={{0,4},{1,5},{2,6},{3,7},{4,8},{5,9},{6,10},{7,11},{8,12},{9,13},{1... | collective-permute-start | bytes 196616 | tf_op jit(solution)/shard_map/ppermute | solution.py:30
  14.8 5.6 %collective-permute-done.5.rest_3_ = bf16[32,1024]{1,0:T(8,128)(2,1)S(1)} collective-permute-done((bf16[32,1024]{1,0:T(8,128)(2,1)S(1)}, bf16[32,1024]{1,0:T(8,128)(2,1)S(1)}, u32[]{:S(2)}, u32[]{:S(2)}) %collective-permute-start.5) | collective-permute-done | bytes 65568 | tf_op jit(solution)/shard_map/ppermute | solution.py:30
  20.5 7.9 %collective-permute-done.6.rest_4_ = bf16[32,1024]{1,0:T(8,128)(2,1)S(1)} collective-permute-done((bf16[32,1024]{1,0:T(8,128)(2,1)S(1)}, bf16[32,1024]{1,0:T(8,128)(2,1)S(1)}, u32[]{:S(2)}, u32[]{:S(2)}) %collective-permute-start.6) | collective-permute-done | bytes 65568 | tf_op jit(solution)/shard_map/ppermute | solution.py:30
  28.3 1.5 %collective-permute-start.7 = (bf16[32,1024]{1,0:T(8,128)(2,1)S(1)}, bf16[32,1024]{1,0:T(8,128)(2,1)S(1)}, u32[]{:S(2)}, u32[]{:S(2)}) collective-permute-start(bf16[32,1024]{1,0:T(8,128)(2,1)S(1)} %get-tuple-element.17), channel_id=1, source_target_pairs={{0,2},{1,3},{2,0},{3,1},{4,6},{5,7},{6,4},{7,5},{8,10},{9,11},{10,... | collective-permute-start | bytes 196616 | tf_op jit(solution)/shard_map/ppermute | solution.py:30
  29.8 2.8 %collective-permute-done.7.rest_5_ = bf16[32,1024]{1,0:T(8,128)(2,1)S(1)} collective-permute-done((bf16[32,1024]{1,0:T(8,128)(2,1)S(1)}, bf16[32,1024]{1,0:T(8,128)(2,1)S(1)}, u32[]{:S(2)}, u32[]{:S(2)}) %collective-permute-start.7) | collective-permute-done | bytes 65568 | tf_op jit(solution)/shard_map/ppermute | solution.py:30
  32.6 1.1 %parent.1 = (f32[32,1024]{1,0:T(8,128)S(1)}, bf16[32,1024]{1,0:T(8,128)(2,1)S(1)}) custom-call(s32[2]{0:T(128)S(1)} %pad_add_fusion.where, f32[2,32,1024]{2,1,0:T(8,128)S(1)} %get-tuple-element.8.keep, bf16[2,32,1024]{2,1,0:T(8,128)(2,1)S(1)} %collective-permute-done.came, bf16[2,32,1024]{2,1,0:T(8,128)(2,1)S(1)} %copy-done.6, ...), custom_call_target="tpu_custom_call" | custom-call | flops 134217728 | bytes 4194304 | tf_op jit(solution)/shard_map/parent/pallas_call | solution.py:187
  33.7 1.6 %collective-permute-start.8 = (bf16[32,1024]{1,0:T(8,128)(2,1)S(1)}, bf16[32,1024]{1,0:T(8,128)(2,1)S(1)}, u32[]{:S(2)}, u32[]{:S(2)}) collective-permute-start(bf16[32,1024]{1,0:T(8,128)(2,1)S(1)} %get-tuple-element.11), channel_id=1, source_target_pairs={{0,2},{1,3},{2,0},{3,1},{4,6},{5,7},{6,4},{7,5},{8,10},{9,11},{10,... | collective-permute-start | bytes 196616 | tf_op jit(solution)/shard_map/ppermute | solution.py:30
  35.3 3.2 %collective-permute-start.10 = (bf16[32,1024]{1,0:T(8,128)(2,1)S(1)}, bf16[32,1024]{1,0:T(8,128)(2,1)S(1)}, u32[]{:S(2)}, u32[]{:S(2)}) collective-permute-start(bf16[32,1024]{1,0:T(8,128)(2,1)S(1)} %get-tuple-element.11), channel_id=1, source_target_pairs={{0,30},{1,31},{2,28},{3,29},{4,2},{5,3},{6,0},{7,1},{8,6},{9,7},{1... | collective-permute-start | bytes 196616 | tf_op jit(solution)/shard_map/ppermute | solution.py:30
  38.6 1.9 %collective-permute-done.10 = bf16[32,1024]{1,0:T(8,128)(2,1)S(1)} collective-permute-done((bf16[32,1024]{1,0:T(8,128)(2,1)S(1)}, bf16[32,1024]{1,0:T(8,128)(2,1)S(1)}, u32[]{:S(2)}, u32[]{:S(2)}) %collective-permute-start.10) | collective-permute-done | bytes 65568 | tf_op jit(solution)/shard_map/ppermute | solution.py:30
  40.4 2.3 %collective-permute-done.9 = bf16[32,1024]{1,0:T(8,128)(2,1)S(1)} collective-permute-done((bf16[32,1024]{1,0:T(8,128)(2,1)S(1)}, bf16[32,1024]{1,0:T(8,128)(2,1)S(1)}, u32[]{:S(2)}, u32[]{:S(2)}) %collective-permute-start.9) | collective-permute-done | bytes 65568 | tf_op jit(solution)/shard_map/ppermute | solution.py:30
  42.8 0.1 collective-permute-start.11
  42.9 1.3 %collective-permute-done.11.theirs = bf16[2,32,1024]{2,1,0:T(8,128)(2,1)S(1)} collective-permute-done((bf16[2,32,1024]{2,1,0:T(8,128)(2,1)S(1)}, bf16[2,32,1024]{2,1,0:T(8,128)(2,1)S(1)}, u32[]{:S(2)}, u32[]{:S(2)}) %collective-permute-start.11) | collective-permute-done | bytes 131104 | tf_op jit(solution)/shard_map/ppermute | solution.py:30
  44.2 4.3 %backward.1 = (f32[8,32,128]{2,1,0:T(8,128)}, f32[2,32,256]{2,1,0:T(8,128)}) custom-call(s32[2]{0:T(128)S(1)} %pad_add_fusion.where, s32[8,2]{1,0:T(8,128)S(1)} %copy.12.targets, bf16[8,32,128]{2,1,0:T(8,128)(2,1)S(1)} %get-tuple-element.7.solved, f32[32,1024]{1,0:T(8,128)S(1)} %get-tuple-element.13.own, bf16[2,32,1024]{2,1,0:T(8,128)(2,1)S(1)} %pad_maximum_fusion.mine, ...), custom_call_target="tpu_custom_call" | custom-call | flops 268435456 | bytes 5242880 | tf_op jit(solution)/shard_map/backward/pallas_call | solution.py:206
  (28 shorter events, 0.3 us)
Async XLA Ops:
  1.5 2.2 %copy-start = (bf16[8,2,128,1024]{3,2,1,0:T(8,128)(2,1)S(1)}, bf16[8,2,128,1024]{3,2,1,0:T(8,128)(2,1)}, u32[]{:S(2)}) copy-start(bf16[8,2,128,1024]{3,2,1,0:T(8,128)(2,1)} %blocks_hbm.2) | copy-start | bytes 12582916
  3.7 0.9 %copy-start.4 = (bf16[8,128,128]{2,1,0:T(8,128)(2,1)S(1)}, bf16[8,128,128]{2,1,0:T(8,128)(2,1)}, u32[]{:S(2)}) copy-start(bf16[8,128,128]{2,1,0:T(8,128)(2,1)} %lower_hbm.1) | copy-start | bytes 786436
  4.6 0.8 %copy-start.7 = (bf16[8,32,128]{2,1,0:T(8,128)(2,1)S(1)}, bf16[8,32,128]{2,1,0:T(8,128)(2,1)}, u32[]{:S(2)}) copy-start(bf16[8,32,128]{2,1,0:T(8,128)(2,1)} %rhs_hbm.1) | copy-start | bytes 196612
  5.5 3.4 %copy-start.3 = (bf16[2,1024,256]{2,1,0:T(8,128)(2,1)S(1)}, bf16[2,1024,256]{2,1,0:T(8,128)(2,1)}, u32[]{:S(2)}) copy-start(bf16[2,1024,256]{2,1,0:T(8,128)(2,1)} %lower.1) | copy-start | bytes 3145732
  5.5 4.3 %copy-start.2 = (bf16[2,1024,256]{2,1,0:T(8,128)(2,1)S(1)}, bf16[2,1024,256]{2,1,0:T(8,128)(2,1)}, u32[]{:S(2)}) copy-start(bf16[2,1024,256]{2,1,0:T(8,128)(2,1)} %upper.2) | copy-start | bytes 3145732
  5.5 27.2 %copy-start.6 = (bf16[2,32,1024]{2,1,0:T(8,128)(2,1)S(1)}, bf16[2,32,1024]{2,1,0:T(8,128)(2,1)}, u32[]{:S(2)}) copy-start(bf16[2,32,1024]{2,1,0:T(8,128)(2,1)} %rhs.1) | copy-start | bytes 393220
  8.3 4.6 %collective-permute-start = (bf16[2,32,1024]{2,1,0:T(8,128)(2,1)}, bf16[2,32,1024]{2,1,0:T(8,128)(2,1)S(1)}, u32[]{:S(2)}, u32[]{:S(2)}) collective-permute-start(bf16[2,32,1024]{2,1,0:T(8,128)(2,1)} %get-tuple-element.9), channel_id=1, source_target_pairs={{0,1},{1,0},{2,3},{3,2},{4,5},{5,4},{6,7},{7,6},{8,9},{9,8},{10,11... | collective-permute-start | bytes 393224 | tf_op jit(solution)/shard_map/ppermute | solution.py:30
  8.8 35.4 %copy-start.5 = (bf16[8,128,128]{2,1,0:T(8,128)(2,1)S(1)}, bf16[8,128,128]{2,1,0:T(8,128)(2,1)}, u32[]{:S(2)}) copy-start(bf16[8,128,128]{2,1,0:T(8,128)(2,1)} %upper.3) | copy-start | bytes 786436
  9.7 22.9 %collective-permute-start.1 = (bf16[1024,256]{1,0:T(8,128)(2,1)}, bf16[1024,256]{1,0:T(8,128)(2,1)S(1)}, u32[]{:S(2)}, u32[]{:S(2)}) collective-permute-start(bf16[1024,256]{1,0:T(8,128)(2,1)} %dynamic-slice_bitcast_fusion), channel_id=1, source_target_pairs={{0,1},{1,0},{2,3},{3,2},{4,5},{5,4},{6,7},{7,6},{8,9},{9,8},{10,11... | collective-permute-start | bytes 1572872 | tf_op jit(solution)/shard_map/ppermute | solution.py:30
  9.7 34.5 %copy-start.1 = (bf16[8,2,1024,128]{3,2,1,0:T(8,128)(2,1)S(1)}, bf16[8,2,1024,128]{3,2,1,0:T(8,128)(2,1)}, u32[]{:S(2)}) copy-start(bf16[8,2,1024,128]{3,2,1,0:T(8,128)(2,1)} %blocks_hbm.3) | copy-start | bytes 12582916
  9.8 22.8 %collective-permute-start.2 = (bf16[512,256]{1,0:T(8,128)(2,1)S(1)}, bf16[512,256]{1,0:T(8,128)(2,1)S(1)}, u32[]{:S(2)}, u32[]{:S(2)}) collective-permute-start(bf16[512,256]{1,0:T(8,128)(2,1)S(1)} %get-tuple-element.16), channel_id=1, source_target_pairs={{0,1},{1,0},{2,3},{3,2},{4,5},{5,4},{6,7},{7,6},{8,9},{9,8},{10,11... | collective-permute-start | bytes 786440 | tf_op jit(solution)/shard_map/ppermute | solution.py:30
  10.3 22.3 %collective-permute-start.3 = (bf16[512,256]{1,0:T(8,128)(2,1)S(1)}, bf16[512,256]{1,0:T(8,128)(2,1)S(1)}, u32[]{:S(2)}, u32[]{:S(2)}) collective-permute-start(bf16[512,256]{1,0:T(8,128)(2,1)S(1)} %get-tuple-element.15), channel_id=1, source_target_pairs={{0,2},{1,3},{2,0},{3,1},{4,6},{5,7},{6,4},{7,5},{8,10},{9,11},{10,... | collective-permute-start | bytes 786440 | tf_op jit(solution)/shard_map/ppermute | solution.py:30
  12.9 19.7 %collective-permute-start.4 = (bf16[512,256]{1,0:T(8,128)(2,1)S(1)}, bf16[512,256]{1,0:T(8,128)(2,1)S(1)}, u32[]{:S(2)}, u32[]{:S(2)}) collective-permute-start(bf16[512,256]{1,0:T(8,128)(2,1)S(1)} %get-tuple-element.14), channel_id=1, source_target_pairs={{0,3},{1,2},{2,1},{3,0},{4,7},{5,6},{6,5},{7,4},{8,11},{9,10},{10,... | collective-permute-start | bytes 786440 | tf_op jit(solution)/shard_map/ppermute | solution.py:30
  13.0 7.4 %collective-permute-start.5 = (bf16[32,1024]{1,0:T(8,128)(2,1)S(1)}, bf16[32,1024]{1,0:T(8,128)(2,1)S(1)}, u32[]{:S(2)}, u32[]{:S(2)}) collective-permute-start(bf16[32,1024]{1,0:T(8,128)(2,1)S(1)} %get-tuple-element.18), channel_id=1, source_target_pairs={{0,4},{1,5},{2,6},{3,7},{4,8},{5,9},{6,10},{7,11},{8,12},{9,13},{1... | collective-permute-start | bytes 196616 | tf_op jit(solution)/shard_map/ppermute | solution.py:30
  20.5 7.9 %collective-permute-start.6 = (bf16[32,1024]{1,0:T(8,128)(2,1)S(1)}, bf16[32,1024]{1,0:T(8,128)(2,1)S(1)}, u32[]{:S(2)}, u32[]{:S(2)}) collective-permute-start(bf16[32,1024]{1,0:T(8,128)(2,1)S(1)} %get-tuple-element.18), channel_id=1, source_target_pairs={{0,6},{1,7},{2,4},{3,5},{4,10},{5,11},{6,8},{7,9},{8,14},{9,15},{1... | collective-permute-start | bytes 196616 | tf_op jit(solution)/shard_map/ppermute | solution.py:30
  28.3 4.3 %collective-permute-start.7 = (bf16[32,1024]{1,0:T(8,128)(2,1)S(1)}, bf16[32,1024]{1,0:T(8,128)(2,1)S(1)}, u32[]{:S(2)}, u32[]{:S(2)}) collective-permute-start(bf16[32,1024]{1,0:T(8,128)(2,1)S(1)} %get-tuple-element.17), channel_id=1, source_target_pairs={{0,2},{1,3},{2,0},{3,1},{4,6},{5,7},{6,4},{7,5},{8,10},{9,11},{10,... | collective-permute-start | bytes 196616 | tf_op jit(solution)/shard_map/ppermute | solution.py:30
  33.7 4.8 %collective-permute-start.8 = (bf16[32,1024]{1,0:T(8,128)(2,1)S(1)}, bf16[32,1024]{1,0:T(8,128)(2,1)S(1)}, u32[]{:S(2)}, u32[]{:S(2)}) collective-permute-start(bf16[32,1024]{1,0:T(8,128)(2,1)S(1)} %get-tuple-element.11), channel_id=1, source_target_pairs={{0,2},{1,3},{2,0},{3,1},{4,6},{5,7},{6,4},{7,5},{8,10},{9,11},{10,... | collective-permute-start | bytes 196616 | tf_op jit(solution)/shard_map/ppermute | solution.py:30
  35.3 5.2 %collective-permute-start.10 = (bf16[32,1024]{1,0:T(8,128)(2,1)S(1)}, bf16[32,1024]{1,0:T(8,128)(2,1)S(1)}, u32[]{:S(2)}, u32[]{:S(2)}) collective-permute-start(bf16[32,1024]{1,0:T(8,128)(2,1)S(1)} %get-tuple-element.11), channel_id=1, source_target_pairs={{0,30},{1,31},{2,28},{3,29},{4,2},{5,3},{6,0},{7,1},{8,6},{9,7},{1... | collective-permute-start | bytes 196616 | tf_op jit(solution)/shard_map/ppermute | solution.py:30
  38.5 4.3 %collective-permute-start.9 = (bf16[32,1024]{1,0:T(8,128)(2,1)S(1)}, bf16[32,1024]{1,0:T(8,128)(2,1)S(1)}, u32[]{:S(2)}, u32[]{:S(2)}) collective-permute-start(bf16[32,1024]{1,0:T(8,128)(2,1)S(1)} %get-tuple-element.11), channel_id=1, source_target_pairs={{0,28},{1,29},{2,30},{3,31},{4,0},{5,1},{6,2},{7,3},{8,4},{9,5},{1... | collective-permute-start | bytes 196616 | tf_op jit(solution)/shard_map/ppermute | solution.py:30
  42.8 1.4 %collective-permute-start.11 = (bf16[2,32,1024]{2,1,0:T(8,128)(2,1)S(1)}, bf16[2,32,1024]{2,1,0:T(8,128)(2,1)S(1)}, u32[]{:S(2)}, u32[]{:S(2)}) collective-permute-start(bf16[2,32,1024]{2,1,0:T(8,128)(2,1)S(1)} %pad_maximum_fusion.mine), channel_id=1, source_target_pairs={{0,1},{1,0},{2,3},{3,2},{4,5},{5,4},{6,7},{7,6},{8,9},{9,8},{10,11... | collective-permute-start | bytes 393224 | tf_op jit(solution)/shard_map/ppermute | solution.py:30

commit v2 on v1

v2 whole, which is shorter than its diff:
```python
import functools

import jax
import jax.numpy as jnp
from jax import lax
from jax.experimental import pallas as pl
from jax.experimental.pallas import tpu as pltpu
from jax.sharding import PartitionSpec as P

CORES = 2
F32 = jnp.float32
BF16 = jnp.bfloat16
VMEM = pl.BlockSpec(memory_space=pltpu.VMEM)
SMEM = pl.BlockSpec(memory_space=pltpu.SMEM)
HBM = pl.BlockSpec(memory_space=pltpu.HBM)


def dot(a, b):
    return jnp.dot(a, b, preferred_element_type=F32)


def in_hbm(*arrays):
    return [pltpu.with_memory_space_constraint(array, pltpu.HBM) for array in arrays]


def in_vmem(*arrays):
    return [pltpu.with_memory_space_constraint(array, pltpu.VMEM) for array in arrays]


def place():
    here = lax.axis_index("col")
    return lax.rem(here, CORES), lax.div(here, CORES)


def send(array, rows, cols, by_row, by_chip, flip):
    chips = cols // CORES
    pairs = []
    for row in range(rows):
        for col in range(cols):
            chip, core = col // CORES, col % CORES
            to = ((chip + by_chip) % chips) * CORES + (core ^ flip)
            pairs.append((row * cols + col, ((row + by_row) % rows) * cols + to))
    return lax.ppermute(array, ("row", "col"), pairs)


def forward_kernel(chips, targets_hbm, rhs_hbm, lower_hbm, blocks_hbm, parent_lower, parent_upper, *rest):
    solved_ref, keep_ref, give_ref, across_ref, *piece_refs = rest[: 4 + CORES * (chips - 1)]
    targets, rhs, lower, blocks, acc, sems = rest[4 + CORES * (chips - 1) :]
    leaves, k, width, wide = blocks.shape
    nrhs = rhs.shape[1]
    depth = wide // chips
    core, chip = place()
    other = 1 - core
    first = [
        pltpu.make_async_copy(targets_hbm, targets, sems.at[0]),
        pltpu.make_async_copy(rhs_hbm, rhs, sems.at[1]),
        pltpu.make_async_copy(lower_hbm, lower, sems.at[2]),
    ]
    copies = [pltpu.make_async_copy(blocks_hbm.at[a], blocks.at[a], sems.at[3 + a]) for a in range(leaves)]

    def rows(by):
        return pl.ds(pl.multiple_of(lax.rem(chip + by, chips) * depth, depth), depth)

    moves = []
    for by in range(1, chips):
        for flip in range(CORES):
            moves.append((parent_upper.at[core if flip == 0 else other, rows(by), :], piece_refs[len(moves)]))
    moves.append((parent_lower.at[other], across_ref.at[pl.ds(0, wide)]))
    moves.append((parent_upper.at[other, rows(0), :], across_ref.at[pl.ds(wide, depth)]))
    last = [pltpu.make_async_copy(a, b, sems.at[3 + leaves + i]) for i, (a, b) in enumerate(moves)]
    for copy in first + copies + last:
        copy.start()
    slots = (core, 2 + core, other, 2 + other)
    for copy in first:
        copy.wait()
    solved = [dot(rhs[a], lower[a]).astype(BF16) for a in range(leaves)]
    for a in range(leaves):
        solved_ref[a] = solved[a]
    step = 2
    for a0 in range(0, leaves, step):
        lhs = jnp.concatenate(
            [
                jnp.concatenate(
                    [
                        jnp.where(targets[i, a] == slot, solved[a], jnp.zeros_like(solved[a]))
                        for a in range(a0, a0 + step)
                        for i in range(k)
                    ],
                    axis=1,
                )
                for slot in slots
            ],
            axis=0,
        )
        for a in range(a0, a0 + step):
            copies[a].wait()
        part = dot(lhs, blocks[pl.ds(a0, step)].reshape(step * k * width, wide))
        if a0 == 0:
            acc[...] = part
        elif a0 + step < leaves:
            acc[...] += part
        else:
            total = acc[...] + part
            keep_ref[...] = total[: 2 * nrhs].reshape(2, nrhs, wide)
            give_ref[...] = total[2 * nrhs :].astype(BF16).reshape(2, nrhs, wide)
    for copy in last:
        copy.wait()


def parent_kernel(chips, keep, came, rhs, lower, upper, across, *rest):
    pieces = rest[: CORES * (chips - 1)]
    sums = rest[len(pieces) : len(pieces) + 2 * chips - 1]
    full_ref, half_ref, forward = rest[len(pieces) + len(sums) :]
    core, chip = place()
    other = 1 - core
    wide = lower.shape[1]
    cut = lower.shape[2]
    depth = forward.shape[1]
    update = keep[0] + came[0].astype(F32)
    for term in sums:
        update = update + term[...].astype(F32)
    combined = (rhs[core].astype(F32) - update).astype(BF16)
    forward[:, pl.ds(pl.multiple_of(core * cut, cut), cut)] = dot(combined, lower[core]).astype(BF16)
    forward[:, pl.ds(pl.multiple_of(other * cut, cut), cut)] = dot(combined, across[pl.ds(0, wide)]).astype(BF16)
    lhs = forward[...]
    rows = pl.ds(pl.multiple_of(chip * depth, depth), depth)
    blocks = [(0, core, upper[core, rows, :]), (0, other, across[pl.ds(wide, depth)])]
    for by in range(1, chips):
        for flip in range(CORES):
            blocks.append((by, core if flip == 0 else other, pieces[len(blocks) - CORES][...]))
    for by, source_core, block in blocks:
        source = lax.rem(chip + chips - by, chips) * CORES + source_core
        part = dot(lhs, block)
        at = pl.ds(pl.multiple_of(source * cut, cut), cut)
        full_ref[:, at] = part
        half_ref[:, at] = part.astype(BF16)


def backward_kernel(targets, solved, own, mine, theirs, blocks, upper, leaf_ref, parent_ref, window):
    leaves, k, wide, width = blocks.shape
    core, chip = place()
    for level in range(2):
        window[2 * level + core] = mine[level]
        window[2 * level + 1 - core] = theirs[level]
    cut = parent_ref.shape[2]
    at = pl.ds(pl.multiple_of((chip * CORES + core) * cut, cut), cut)
    parent_ref[core] = own[:, at]
    parent_ref[1 - core] = theirs[0, :, at].astype(F32)
    for a in range(leaves):
        lhs = jnp.concatenate([window[targets[i, a]] for i in range(k)], axis=1)
        coupling = dot(lhs, blocks[a].reshape(k * wide, width))
        reduced = (solved[a].astype(F32) - coupling).astype(BF16)
        leaf_ref[a] = dot(reduced, upper[a])


def local(
    right_side, leaf_lower, leaf_upper, lower_blocks, upper_blocks, parent_rhs, parent_lower, parent_upper, targets
):
    rows, cols = lax.axis_size("row"), lax.axis_size("col")
    chips = cols // CORES
    go = functools.partial(send, rows=rows, cols=cols)
    leaves, k, width, wide = lower_blocks.shape
    nrhs = right_side.shape[1]
    cut = parent_lower.shape[2]
    depth = cut * CORES
    listed = targets.T

    n_pieces = CORES * (chips - 1)
    solved, keep, give, across, *pieces = pl.pallas_call(
        functools.partial(forward_kernel, chips),
        in_specs=[HBM] * 6,
        out_specs=[VMEM] * (4 + n_pieces),
        out_shape=[
            jax.ShapeDtypeStruct((leaves, nrhs, width), BF16),
            jax.ShapeDtypeStruct((2, nrhs, wide), F32),
            jax.ShapeDtypeStruct((2, nrhs, wide), BF16),
            jax.ShapeDtypeStruct((wide + depth, cut), BF16),
        ]
        + [jax.ShapeDtypeStruct((depth, cut), BF16)] * n_pieces,
        scratch_shapes=[
            pltpu.SMEM(listed.shape, jnp.int32),
            pltpu.VMEM(right_side.shape, BF16),
            pltpu.VMEM(leaf_lower.shape, BF16),
            pltpu.VMEM(lower_blocks.shape, BF16),
            pltpu.VMEM((4 * nrhs, wide), F32),
            pltpu.SemaphoreType.DMA((3 + leaves + n_pieces + 2,)),
        ],
        compiler_params=pltpu.CompilerParams(vmem_limit_bytes=24 << 20),
        cost_estimate=pl.CostEstimate(flops=1 << 29, bytes_accessed=5 << 20, transcendentals=0),
        name="forward",
    )(*in_hbm(listed, right_side, leaf_lower, lower_blocks, parent_lower, parent_upper))

    came = go(give, by_row=0, by_chip=0, flip=1)
    across = go(across, by_row=0, by_chip=0, flip=1)
    pieces = [
        go(piece, by_row=0, by_chip=1 + i // CORES, flip=i % CORES) for i, piece in enumerate(pieces)
    ]
    came, across = lax.optimization_barrier((came, across))
    chip_sum = (keep + came.astype(F32)).astype(BF16)
    sums = [go(chip_sum[1], by_row=1, by_chip=by, flip=0) for by in range(chips)]
    sums += [go(chip_sum[0], by_row=0, by_chip=by, flip=0) for by in range(1, chips)]

    full, half = pl.pallas_call(
        functools.partial(parent_kernel, chips),
        in_specs=[VMEM] * (6 + n_pieces + len(sums)),
        out_specs=[VMEM, VMEM],
        out_shape=[jax.ShapeDtypeStruct((nrhs, wide), F32), jax.ShapeDtypeStruct((nrhs, wide), BF16)],
        scratch_shapes=[pltpu.VMEM((nrhs, depth), BF16)],
        compiler_params=pltpu.CompilerParams(vmem_limit_bytes=24 << 20),
        cost_estimate=pl.CostEstimate(flops=1 << 27, bytes_accessed=4 << 20, transcendentals=0),
        name="parent",
    )(keep, came, parent_rhs, parent_lower, parent_upper, across, *pieces, *sums)

    nexts = [go(half, by_row=-1, by_chip=by, flip=0) for by in range(chips)]
    own = full
    for by in range(1, chips):
        own = own + go(half, by_row=0, by_chip=by, flip=0).astype(F32)
    after = functools.reduce(jnp.add, [term.astype(F32) for term in nexts])
    mine = jnp.stack([own, after]).astype(BF16)
    theirs = go(mine, by_row=0, by_chip=0, flip=1)

    return pl.pallas_call(
        backward_kernel,
        in_specs=[SMEM] + [VMEM] * 6,
        out_specs=[VMEM, VMEM],
        out_shape=[
            jax.ShapeDtypeStruct((leaves, nrhs, width), F32),
            jax.ShapeDtypeStruct((2, nrhs, cut), F32),
        ],
        scratch_shapes=[pltpu.VMEM((4, nrhs, wide), BF16)],
        compiler_params=pltpu.CompilerParams(vmem_limit_bytes=24 << 20),
        cost_estimate=pl.CostEstimate(flops=1 << 28, bytes_accessed=5 << 20, transcendentals=0),
        name="backward",
    )(listed, solved, own, mine, theirs, upper_blocks, leaf_upper)


def solution(mesh):
    placed = (
        P(("row", "col"), None, None),
        P(("row", "col"), None, None),
        P(("row", "col"), None, None),
        P(("row", "col"), None, None, None),
        P(("row", "col"), None, None, None),
        P("row", None, None),
        P("row", None, "col"),
        P("row", None, "col"),
        P(("row", "col"), None),
    )
    return jax.shard_map(
        local,
        mesh=mesh,
        in_specs=placed,
        out_specs=(P(("row", "col"), None, None), P("row", None, "col")),
        check_vma=False,
    )
```

time: 48.7 us -> 37.3 us (0.77)
  waiting for transfers between devices: 21.8 us -> 14.1 us
  local copies, waits for them, and re-layouts: 5.65 us -> 0.04 us
  starting transfers between devices: 11.9 us -> 15.8 us
  Pallas kernels: 8.21 us -> 6.35 us
    ppermute x12 -> x11, waiting for transfers between devices: 21.8 us -> 14.1 us  [send(): return lax.ppermute(array, ('row', 'col'), pairs)]
    unnamed x17 -> x12, local copies, waits for them, and re-layouts: 4.75 us -> 0.03 us
    ppermute x12 -> x11, starting transfers between devices: 11.9 us -> 15.8 us  [send(): return lax.ppermute(array, ('row', 'col'), pairs)]
    pallas_call x3, Pallas kernels: 8.21 us -> 6.35 us  [the longest x1 2.92 us: local(): pl.pallas_call(functools.partial(forward_kernel, chips), in_specs=[HBM] *...]
    squeeze x1 -> x0, local copies, waits for them, and re-layouts: 0.84 us -> none  [local(): lax.dynamic_index_in_dim(parent_lower, 1 - core, 0, False)]
  transfers between devices with their start and end apart: 12 -> 11, of which waited for: 6 -> 7; matrix products, arithmetic and copies ran while one was open for 2% -> 0% of each run, Pallas kernels for 0% -> 0%
where the time goes in v2:
time: 37.3 us; the launch traced here: 37.1 us
  starting transfers between devices  15.8 us (42%)
  waiting for transfers between devices  14.1 us (38%)
  Pallas kernels  6.35 us (17%)
  between operations  0.76 us (2%)
    ppermute x11, starting transfers between devices, send(): return lax.ppermute(array, ('row', 'col'), pairs)  15.8 us
    ppermute x11, waiting for transfers between devices, send(): return lax.ppermute(array, ('row', 'col'), pairs)  14.1 us
    pallas_call x1, Pallas kernels, local(): pl.pallas_call(functools.partial(forward_kernel, chips), in_specs=[HBM] *...  2.92 us
    pallas_call x1, Pallas kernels, local(): pl.pallas_call(backward_kernel, in_specs=[SMEM] + [VMEM] * 6, out_specs=[...  2.89 us
  transfers between devices with their start and end apart: 11, of which 7 were waited for; matrix products, arithmetic and copies ran while one was open for 0% of the time, Pallas kernels for 0%

profile of v2, /device:TPU:0, one launch (start us, length us, event | category | flops | bytes accessed | tf_op | source)
XLA Modules:
  0.0 37.1 jit_solution(12617888078267182748)
XLA Ops:
  0.7 2.9 %forward.1 = (bf16[8,32,128]{2,1,0:T(8,128)(2,1)S(1)}, f32[2,32,1024]{2,1,0:T(8,128)S(1)}, bf16[2,32,1024]{2,1,0:T(8,128)(2,1)S(1)}, bf16[1536,256]{1,0:T(8,128)...) custom-call(s32[2,8]{1,0:T(2,128)} %bitcast.9, bf16[8,32,128]{2,1,0:T(8,128)(2,1)} %rhs_hbm.1, ...), custom_call_target="tpu_custom_call" | custom-call | flops 536870912 | bytes 5242880 | tf_op jit(solution)/shard_map/forward/pallas_call | solution.py:169
  3.6 0.0 copy-start
  3.6 0.0 copy-start.3
  3.6 0.0 copy-start.5
  3.6 0.5 %collective-permute-start.1 = (bf16[1536,256]{1,0:T(8,128)(2,1)S(1)}, bf16[1536,256]{1,0:T(8,128)(2,1)S(1)}, u32[]{:S(2)}, u32[]{:S(2)}) collective-permute-start(bf16[1536,256]{1,0:T(8,128)(2,1)S(1)} %get-tuple-element.15), channel_id=1, source_target_pairs={{0,1},{1,0},{2,3},{3,2},{4,5},{5,4},{6,7},{7,6},{8,9},{9,8},{10,11... | collective-permute-start | bytes 2359304 | tf_op jit(solution)/shard_map/ppermute | solution.py:43
  4.1 0.1 collective-permute-start
  4.2 2.9 %collective-permute-start.2 = (bf16[512,256]{1,0:T(8,128)(2,1)S(1)}, bf16[512,256]{1,0:T(8,128)(2,1)S(1)}, u32[]{:S(2)}, u32[]{:S(2)}) collective-permute-start(bf16[512,256]{1,0:T(8,128)(2,1)S(1)} %get-tuple-element.18), channel_id=1, source_target_pairs={{0,2},{1,3},{2,0},{3,1},{4,6},{5,7},{6,4},{7,5},{8,10},{9,11},{10,... | collective-permute-start | bytes 786440 | tf_op jit(solution)/shard_map/ppermute | solution.py:43
  7.1 0.0 collective-permute-start.3
  7.1 0.0 collective-permute-done.came
  7.2 2.0 %collective-permute-start.6 = (bf16[32,1024]{1,0:T(8,128)(2,1)S(1)}, bf16[32,1024]{1,0:T(8,128)(2,1)S(1)}, u32[]{:S(2)}, u32[]{:S(2)}) collective-permute-start(bf16[32,1024]{1,0:T(8,128)(2,1)S(1)} %get-tuple-element.24), channel_id=1, source_target_pairs={{0,2},{1,3},{2,0},{3,1},{4,6},{5,7},{6,4},{7,5},{8,10},{9,11},{10,... | collective-permute-start | bytes 196616 | tf_op jit(solution)/shard_map/ppermute | solution.py:43
  9.2 1.5 %collective-permute-start.5 = (bf16[32,1024]{1,0:T(8,128)(2,1)S(1)}, bf16[32,1024]{1,0:T(8,128)(2,1)S(1)}, u32[]{:S(2)}, u32[]{:S(2)}) collective-permute-start(bf16[32,1024]{1,0:T(8,128)(2,1)S(1)} %get-tuple-element.25), channel_id=1, source_target_pairs={{0,6},{1,7},{2,4},{3,5},{4,10},{5,11},{6,8},{7,9},{8,14},{9,15},{1... | collective-permute-start | bytes 196616 | tf_op jit(solution)/shard_map/ppermute | solution.py:43
  10.7 1.5 %collective-permute-start.4 = (bf16[32,1024]{1,0:T(8,128)(2,1)S(1)}, bf16[32,1024]{1,0:T(8,128)(2,1)S(1)}, u32[]{:S(2)}, u32[]{:S(2)}) collective-permute-start(bf16[32,1024]{1,0:T(8,128)(2,1)S(1)} %get-tuple-element.25), channel_id=1, source_target_pairs={{0,4},{1,5},{2,6},{3,7},{4,8},{5,9},{6,10},{7,11},{8,12},{9,13},{1... | collective-permute-start | bytes 196616 | tf_op jit(solution)/shard_map/ppermute | solution.py:43
  12.2 2.0 %collective-permute-done.2.rest_0_ = bf16[512,256]{1,0:T(8,128)(2,1)S(1)} collective-permute-done((bf16[512,256]{1,0:T(8,128)(2,1)S(1)}, bf16[512,256]{1,0:T(8,128)(2,1)S(1)}, u32[]{:S(2)}, u32[]{:S(2)}) %collective-permute-start.2) | collective-permute-done | bytes 262176 | tf_op jit(solution)/shard_map/ppermute | solution.py:43
  14.2 5.2 %collective-permute-done.3.rest_1_ = bf16[512,256]{1,0:T(8,128)(2,1)S(1)} collective-permute-done((bf16[512,256]{1,0:T(8,128)(2,1)S(1)}, bf16[512,256]{1,0:T(8,128)(2,1)S(1)}, u32[]{:S(2)}, u32[]{:S(2)}) %collective-permute-start.3) | collective-permute-done | bytes 262176 | tf_op jit(solution)/shard_map/ppermute | solution.py:43
  19.4 1.8 %collective-permute-done.6.rest_4_ = bf16[32,1024]{1,0:T(8,128)(2,1)S(1)} collective-permute-done((bf16[32,1024]{1,0:T(8,128)(2,1)S(1)}, bf16[32,1024]{1,0:T(8,128)(2,1)S(1)}, u32[]{:S(2)}, u32[]{:S(2)}) %collective-permute-start.6) | collective-permute-done | bytes 65568 | tf_op jit(solution)/shard_map/ppermute | solution.py:43
  21.3 0.1 collective-permute-done.5.rest_3_
  21.4 0.5 %parent.1 = (f32[32,1024]{1,0:T(8,128)S(1)}, bf16[32,1024]{1,0:T(8,128)(2,1)S(1)}) custom-call(f32[2,32,1024]{2,1,0:T(8,128)S(1)} %get-tuple-element.13.keep, bf16[2,32,1024]{2,1,0:T(8,128)(2,1)S(1)} %collective-permute-done.came, bf16[2,32,1024]{2,1,0:T(8,128)(2,1)S(1)} %copy-done.4, bf16[2,1024,256]{2,1,0:T(8,128)(2,1)S(1)} %copy-done.1, ...), custom_call_target="tpu_custom_call" | custom-call | flops 134217728 | bytes 4194304 | tf_op jit(solution)/shard_map/parent/pallas_call | solution.py:203
  21.9 6.5 %collective-permute-start.9 = (bf16[32,1024]{1,0:T(8,128)(2,1)S(1)}, bf16[32,1024]{1,0:T(8,128)(2,1)S(1)}, u32[]{:S(2)}, u32[]{:S(2)}) collective-permute-start(bf16[32,1024]{1,0:T(8,128)(2,1)S(1)} %get-tuple-element.21), channel_id=1, source_target_pairs={{0,30},{1,31},{2,28},{3,29},{4,2},{5,3},{6,0},{7,1},{8,6},{9,7},{1... | collective-permute-start | bytes 196616 | tf_op jit(solution)/shard_map/ppermute | solution.py:43
  28.5 0.6 %collective-permute-start.7 = (bf16[32,1024]{1,0:T(8,128)(2,1)S(1)}, bf16[32,1024]{1,0:T(8,128)(2,1)S(1)}, u32[]{:S(2)}, u32[]{:S(2)}) collective-permute-start(bf16[32,1024]{1,0:T(8,128)(2,1)S(1)} %get-tuple-element.21), channel_id=1, source_target_pairs={{0,2},{1,3},{2,0},{3,1},{4,6},{5,7},{6,4},{7,5},{8,10},{9,11},{10,... | collective-permute-start | bytes 196616 | tf_op jit(solution)/shard_map/ppermute | solution.py:43
  29.1 1.3 %collective-permute-done.9 = bf16[32,1024]{1,0:T(8,128)(2,1)S(1)} collective-permute-done((bf16[32,1024]{1,0:T(8,128)(2,1)S(1)}, bf16[32,1024]{1,0:T(8,128)(2,1)S(1)}, u32[]{:S(2)}, u32[]{:S(2)}) %collective-permute-start.9) | collective-permute-done | bytes 65568 | tf_op jit(solution)/shard_map/ppermute | solution.py:43
  30.4 2.4 %collective-permute-done.8 = bf16[32,1024]{1,0:T(8,128)(2,1)S(1)} collective-permute-done((bf16[32,1024]{1,0:T(8,128)(2,1)S(1)}, bf16[32,1024]{1,0:T(8,128)(2,1)S(1)}, u32[]{:S(2)}, u32[]{:S(2)}) %collective-permute-start.8) | collective-permute-done | bytes 65568 | tf_op jit(solution)/shard_map/ppermute | solution.py:43
  32.8 0.1 collective-permute-start.10
  32.9 1.3 %collective-permute-done.10.theirs = bf16[2,32,1024]{2,1,0:T(8,128)(2,1)S(1)} collective-permute-done((bf16[2,32,1024]{2,1,0:T(8,128)(2,1)S(1)}, bf16[2,32,1024]{2,1,0:T(8,128)(2,1)S(1)}, u32[]{:S(2)}, u32[]{:S(2)}) %collective-permute-start.10) | collective-permute-done | bytes 131104 | tf_op jit(solution)/shard_map/ppermute | solution.py:43
  34.2 2.9 %backward.1 = (f32[8,32,128]{2,1,0:T(8,128)}, f32[2,32,256]{2,1,0:T(8,128)}) custom-call(s32[2,8]{1,0:T(2,128)S(1)} %bitcast.10, bf16[8,32,128]{2,1,0:T(8,128)(2,1)S(1)} %get-tuple-element.12.solved, f32[32,1024]{1,0:T(8,128)S(1)} %get-tuple-element.23.own, bf16[2,32,1024]{2,1,0:T(8,128)(2,1)S(1)} %pad_maximum_fusion.mine, ...), custom_call_target="tpu_custom_call" | custom-call | flops 268435456 | bytes 5242880 | tf_op jit(solution)/shard_map/backward/pallas_call | solution.py:222
  (18 shorter events, 0.1 us)
Async XLA Ops:
  0.6 20.7 %copy-start.2 = (bf16[2,1024,256]{2,1,0:T(8,128)(2,1)S(1)}, bf16[2,1024,256]{2,1,0:T(8,128)(2,1)}, u32[]{:S(2)}) copy-start(bf16[2,1024,256]{2,1,0:T(8,128)(2,1)} %upper.2) | copy-start | bytes 3145732
  0.6 20.7 %copy-start.1 = (bf16[2,1024,256]{2,1,0:T(8,128)(2,1)S(1)}, bf16[2,1024,256]{2,1,0:T(8,128)(2,1)}, u32[]{:S(2)}) copy-start(bf16[2,1024,256]{2,1,0:T(8,128)(2,1)} %lower.1) | copy-start | bytes 3145732
  0.7 20.7 %copy-start.4 = (bf16[2,32,1024]{2,1,0:T(8,128)(2,1)S(1)}, bf16[2,32,1024]{2,1,0:T(8,128)(2,1)}, u32[]{:S(2)}) copy-start(bf16[2,32,1024]{2,1,0:T(8,128)(2,1)} %rhs.1) | copy-start | bytes 393220
  3.6 30.7 %copy-start = (bf16[8,2,1024,128]{3,2,1,0:T(8,128)(2,1)S(1)}, bf16[8,2,1024,128]{3,2,1,0:T(8,128)(2,1)}, u32[]{:S(2)}) copy-start(bf16[8,2,1024,128]{3,2,1,0:T(8,128)(2,1)} %blocks.1) | copy-start | bytes 12582916
  3.6 30.6 %copy-start.3 = (bf16[8,128,128]{2,1,0:T(8,128)(2,1)S(1)}, bf16[8,128,128]{2,1,0:T(8,128)(2,1)}, u32[]{:S(2)}) copy-start(bf16[8,128,128]{2,1,0:T(8,128)(2,1)} %upper.3) | copy-start | bytes 786436
  3.6 30.6 %copy-start.5 = (s32[8,2]{0,1:T(2,128)S(1)}, s32[8,2]{0,1:T(2,128)}, u32[]{:S(2)}) copy-start(s32[8,2]{0,1:T(2,128)} %param.17) | copy-start | bytes 196
  3.6 3.5 %collective-permute-start.1 = (bf16[1536,256]{1,0:T(8,128)(2,1)S(1)}, bf16[1536,256]{1,0:T(8,128)(2,1)S(1)}, u32[]{:S(2)}, u32[]{:S(2)}) collective-permute-start(bf16[1536,256]{1,0:T(8,128)(2,1)S(1)} %get-tuple-element.15), channel_id=1, source_target_pairs={{0,1},{1,0},{2,3},{3,2},{4,5},{5,4},{6,7},{7,6},{8,9},{9,8},{10,11... | collective-permute-start | bytes 2359304 | tf_op jit(solution)/shard_map/ppermute | solution.py:43
  4.1 3.0 %collective-permute-start = (bf16[2,32,1024]{2,1,0:T(8,128)(2,1)S(1)}, bf16[2,32,1024]{2,1,0:T(8,128)(2,1)S(1)}, u32[]{:S(2)}, u32[]{:S(2)}) collective-permute-start(bf16[2,32,1024]{2,1,0:T(8,128)(2,1)S(1)} %get-tuple-element.14), channel_id=1, source_target_pairs={{0,1},{1,0},{2,3},{3,2},{4,5},{5,4},{6,7},{7,6},{8,9},{9,8},{10,11... | collective-permute-start | bytes 393224 | tf_op jit(solution)/shard_map/ppermute | solution.py:43
  4.2 10.0 %collective-permute-start.2 = (bf16[512,256]{1,0:T(8,128)(2,1)S(1)}, bf16[512,256]{1,0:T(8,128)(2,1)S(1)}, u32[]{:S(2)}, u32[]{:S(2)}) collective-permute-start(bf16[512,256]{1,0:T(8,128)(2,1)S(1)} %get-tuple-element.18), channel_id=1, source_target_pairs={{0,2},{1,3},{2,0},{3,1},{4,6},{5,7},{6,4},{7,5},{8,10},{9,11},{10,... | collective-permute-start | bytes 786440 | tf_op jit(solution)/shard_map/ppermute | solution.py:43
  7.1 12.3 %collective-permute-start.3 = (bf16[512,256]{1,0:T(8,128)(2,1)S(1)}, bf16[512,256]{1,0:T(8,128)(2,1)S(1)}, u32[]{:S(2)}, u32[]{:S(2)}) collective-permute-start(bf16[512,256]{1,0:T(8,128)(2,1)S(1)} %get-tuple-element.19), channel_id=1, source_target_pairs={{0,3},{1,2},{2,1},{3,0},{4,7},{5,6},{6,5},{7,4},{8,11},{9,10},{10,... | collective-permute-start | bytes 786440 | tf_op jit(solution)/shard_map/ppermute | solution.py:43
  7.2 14.1 %collective-permute-start.6 = (bf16[32,1024]{1,0:T(8,128)(2,1)S(1)}, bf16[32,1024]{1,0:T(8,128)(2,1)S(1)}, u32[]{:S(2)}, u32[]{:S(2)}) collective-permute-start(bf16[32,1024]{1,0:T(8,128)(2,1)S(1)} %get-tuple-element.24), channel_id=1, source_target_pairs={{0,2},{1,3},{2,0},{3,1},{4,6},{5,7},{6,4},{7,5},{8,10},{9,11},{10,... | collective-permute-start | bytes 196616 | tf_op jit(solution)/shard_map/ppermute | solution.py:43
  9.2 12.2 %collective-permute-start.5 = (bf16[32,1024]{1,0:T(8,128)(2,1)S(1)}, bf16[32,1024]{1,0:T(8,128)(2,1)S(1)}, u32[]{:S(2)}, u32[]{:S(2)}) collective-permute-start(bf16[32,1024]{1,0:T(8,128)(2,1)S(1)} %get-tuple-element.25), channel_id=1, source_target_pairs={{0,6},{1,7},{2,4},{3,5},{4,10},{5,11},{6,8},{7,9},{8,14},{9,15},{1... | collective-permute-start | bytes 196616 | tf_op jit(solution)/shard_map/ppermute | solution.py:43
  10.7 10.7 %collective-permute-start.4 = (bf16[32,1024]{1,0:T(8,128)(2,1)S(1)}, bf16[32,1024]{1,0:T(8,128)(2,1)S(1)}, u32[]{:S(2)}, u32[]{:S(2)}) collective-permute-start(bf16[32,1024]{1,0:T(8,128)(2,1)S(1)} %get-tuple-element.25), channel_id=1, source_target_pairs={{0,4},{1,5},{2,6},{3,7},{4,8},{5,9},{6,10},{7,11},{8,12},{9,13},{1... | collective-permute-start | bytes 196616 | tf_op jit(solution)/shard_map/ppermute | solution.py:43
  21.9 8.5 %collective-permute-start.9 = (bf16[32,1024]{1,0:T(8,128)(2,1)S(1)}, bf16[32,1024]{1,0:T(8,128)(2,1)S(1)}, u32[]{:S(2)}, u32[]{:S(2)}) collective-permute-start(bf16[32,1024]{1,0:T(8,128)(2,1)S(1)} %get-tuple-element.21), channel_id=1, source_target_pairs={{0,30},{1,31},{2,28},{3,29},{4,2},{5,3},{6,0},{7,1},{8,6},{9,7},{1... | collective-permute-start | bytes 196616 | tf_op jit(solution)/shard_map/ppermute | solution.py:43
  28.5 4.3 %collective-permute-start.8 = (bf16[32,1024]{1,0:T(8,128)(2,1)S(1)}, bf16[32,1024]{1,0:T(8,128)(2,1)S(1)}, u32[]{:S(2)}, u32[]{:S(2)}) collective-permute-start(bf16[32,1024]{1,0:T(8,128)(2,1)S(1)} %get-tuple-element.21), channel_id=1, source_target_pairs={{0,28},{1,29},{2,30},{3,31},{4,0},{5,1},{6,2},{7,3},{8,4},{9,5},{1... | collective-permute-start | bytes 196616 | tf_op jit(solution)/shard_map/ppermute | solution.py:43
  28.5 4.3 %collective-permute-start.7 = (bf16[32,1024]{1,0:T(8,128)(2,1)S(1)}, bf16[32,1024]{1,0:T(8,128)(2,1)S(1)}, u32[]{:S(2)}, u32[]{:S(2)}) collective-permute-start(bf16[32,1024]{1,0:T(8,128)(2,1)S(1)} %get-tuple-element.21), channel_id=1, source_target_pairs={{0,2},{1,3},{2,0},{3,1},{4,6},{5,7},{6,4},{7,5},{8,10},{9,11},{10,... | collective-permute-start | bytes 196616 | tf_op jit(solution)/shard_map/ppermute | solution.py:43
  32.8 1.4 %collective-permute-start.10 = (bf16[2,32,1024]{2,1,0:T(8,128)(2,1)S(1)}, bf16[2,32,1024]{2,1,0:T(8,128)(2,1)S(1)}, u32[]{:S(2)}, u32[]{:S(2)}) collective-permute-start(bf16[2,32,1024]{2,1,0:T(8,128)(2,1)S(1)} %pad_maximum_fusion.mine), channel_id=1, source_target_pairs={{0,1},{1,0},{2,3},{3,2},{4,5},{5,4},{6,7},{7,6},{8,9},{9,8},{10,11... | collective-permute-start | bytes 393224 | tf_op jit(solution)/shard_map/ppermute | solution.py:43

commit v3 on v2

v3 whole, which is shorter than its diff:
```python
import functools

import jax
import jax.numpy as jnp
from jax import lax
from jax.experimental import pallas as pl
from jax.experimental.pallas import tpu as pltpu
from jax.sharding import PartitionSpec as P

CORES = 2
F32 = jnp.float32
BF16 = jnp.bfloat16
VMEM = pl.BlockSpec(memory_space=pltpu.VMEM)
SMEM = pl.BlockSpec(memory_space=pltpu.SMEM)
HBM = pl.BlockSpec(memory_space=pltpu.HBM)


def dot(a, b):
    return jnp.dot(a, b, preferred_element_type=F32)


def in_hbm(*arrays):
    return [pltpu.with_memory_space_constraint(array, pltpu.HBM) for array in arrays]


def in_vmem(*arrays):
    return [pltpu.with_memory_space_constraint(array, pltpu.VMEM) for array in arrays]


def place():
    here = lax.axis_index("col")
    return lax.rem(here, CORES), lax.div(here, CORES)


def send(array, rows, cols, by_row, by_chip, flip):
    chips = cols // CORES
    pairs = []
    for row in range(rows):
        for col in range(cols):
            chip, core = col // CORES, col % CORES
            to = ((chip + by_chip) % chips) * CORES + (core ^ flip)
            pairs.append((row * cols + col, ((row + by_row) % rows) * cols + to))
    return lax.ppermute(array, ("row", "col"), pairs)


def forward_kernel(targets_hbm, rhs_hbm, lower_hbm, blocks_hbm, parent_lower, parent_upper, *rest):
    solved_ref, keep_ref, give_ref, across_ref, targets, rhs, lower, blocks, acc, sems = rest
    leaves, k, width, wide = blocks.shape
    nrhs = rhs.shape[1]
    core, _ = place()
    other = 1 - core
    first = [
        pltpu.make_async_copy(targets_hbm, targets, sems.at[0]),
        pltpu.make_async_copy(rhs_hbm, rhs, sems.at[1]),
        pltpu.make_async_copy(lower_hbm, lower, sems.at[2]),
    ]
    copies = [pltpu.make_async_copy(blocks_hbm.at[a], blocks.at[a], sems.at[3 + a]) for a in range(leaves)]
    last = [
        pltpu.make_async_copy(parent_lower.at[other], across_ref.at[0], sems.at[3 + leaves]),
        pltpu.make_async_copy(parent_upper.at[other], across_ref.at[1], sems.at[4 + leaves]),
    ]
    for copy in first + copies + last:
        copy.start()
    slots = (core, 2 + core, other, 2 + other)
    for copy in first:
        copy.wait()
    solved = [dot(rhs[a], lower[a]).astype(BF16) for a in range(leaves)]
    for a in range(leaves):
        solved_ref[a] = solved[a]
    step = 2
    for a0 in range(0, leaves, step):
        lhs = jnp.concatenate(
            [
                jnp.concatenate(
                    [
                        jnp.where(targets[i, a] == slot, solved[a], jnp.zeros_like(solved[a]))
                        for a in range(a0, a0 + step)
                        for i in range(k)
                    ],
                    axis=1,
                )
                for slot in slots
            ],
            axis=0,
        )
        for a in range(a0, a0 + step):
            copies[a].wait()
        part = dot(lhs, blocks[pl.ds(a0, step)].reshape(step * k * width, wide))
        if a0 == 0:
            acc[...] = part
        elif a0 + step < leaves:
            acc[...] += part
        else:
            total = acc[...] + part
            keep_ref[...] = total[: 2 * nrhs].reshape(2, nrhs, wide)
            give_ref[...] = total[2 * nrhs :].astype(BF16).reshape(2, nrhs, wide)
    for copy in last:
        copy.wait()


def parent_forward_kernel(keep, came, rhs, lower, across, *rest):
    sums, half_ref = rest[:-1], rest[-1]
    core, _ = place()
    other = 1 - core
    cut = lower.shape[2]
    update = keep[0] + came[0].astype(F32)
    for term in sums:
        update = update + term[...].astype(F32)
    combined = (rhs[core].astype(F32) - update).astype(BF16)
    half_ref[:, pl.ds(pl.multiple_of(core * cut, cut), cut)] = dot(combined, lower[core]).astype(BF16)
    half_ref[:, pl.ds(pl.multiple_of(other * cut, cut), cut)] = dot(combined, across[0]).astype(BF16)


def parent_backward_kernel(upper, across, *rest):
    halves, (full_ref, half_ref, forward) = rest[:-3], rest[-3:]
    chips = len(halves)
    core, chip = place()
    other = 1 - core
    cut = upper.shape[2]
    depth = halves[0].shape[1]
    for by, half in enumerate(halves):
        source = lax.rem(chip + chips - by, chips)
        forward[:, pl.ds(pl.multiple_of(source * depth, depth), depth)] = half[...]
    for at, block in ((core, upper[core]), (other, across[1])):
        part = dot(forward[...], block)
        at = pl.ds(pl.multiple_of(at * cut, cut), cut)
        full_ref[:, at] = part
        half_ref[:, at] = part.astype(BF16)


def backward_kernel(targets, solved, own, mine, theirs, blocks, upper, leaf_ref, parent_ref, window):
    leaves, k, wide, width = blocks.shape
    chips, depth = mine.shape[1], mine.shape[3]
    core, chip = place()
    for by in range(chips):
        source = lax.rem(chip + chips - by, chips)
        at = pl.ds(pl.multiple_of(source * depth, depth), depth)
        for level in range(2):
            window[2 * level + core, :, at] = mine[level, by]
            window[2 * level + 1 - core, :, at] = theirs[level, by]
    cut = parent_ref.shape[2]
    at = pl.ds(pl.multiple_of(core * cut, cut), cut)
    parent_ref[core] = own[:, at]
    parent_ref[1 - core] = theirs[0, 0, :, at].astype(F32)
    for a in range(leaves):
        lhs = jnp.concatenate([window[targets[i, a]] for i in range(k)], axis=1)
        coupling = dot(lhs, blocks[a].reshape(k * wide, width))
        reduced = (solved[a].astype(F32) - coupling).astype(BF16)
        leaf_ref[a] = dot(reduced, upper[a])


def local(
    right_side, leaf_lower, leaf_upper, lower_blocks, upper_blocks, parent_rhs, parent_lower, parent_upper, targets
):
    rows, cols = lax.axis_size("row"), lax.axis_size("col")
    chips = cols // CORES
    go = functools.partial(send, rows=rows, cols=cols)
    leaves, k, width, wide = lower_blocks.shape
    nrhs = right_side.shape[1]
    cut = parent_lower.shape[2]
    depth = cut * CORES
    listed = targets.T

    solved, keep, give, across = pl.pallas_call(
        forward_kernel,
        in_specs=[HBM] * 6,
        out_specs=[VMEM] * 4,
        out_shape=[
            jax.ShapeDtypeStruct((leaves, nrhs, width), BF16),
            jax.ShapeDtypeStruct((2, nrhs, wide), F32),
            jax.ShapeDtypeStruct((2, nrhs, wide), BF16),
            jax.ShapeDtypeStruct((2, wide, cut), BF16),
        ],
        scratch_shapes=[
            pltpu.SMEM(listed.shape, jnp.int32),
            pltpu.VMEM(right_side.shape, BF16),
            pltpu.VMEM(leaf_lower.shape, BF16),
            pltpu.VMEM(lower_blocks.shape, BF16),
            pltpu.VMEM((4 * nrhs, wide), F32),
            pltpu.SemaphoreType.DMA((5 + leaves,)),
        ],
        compiler_params=pltpu.CompilerParams(vmem_limit_bytes=24 << 20),
        cost_estimate=pl.CostEstimate(flops=1 << 29, bytes_accessed=5 << 20, transcendentals=0),
        name="forward",
    )(*in_hbm(listed, right_side, leaf_lower, lower_blocks, parent_lower, parent_upper))

    came = go(give, by_row=0, by_chip=0, flip=1)
    came, across = lax.optimization_barrier((came, across))
    across = go(across, by_row=0, by_chip=0, flip=1)
    chip_sum = (keep + came.astype(F32)).astype(BF16)
    sums = [go(chip_sum[1], by_row=1, by_chip=by, flip=0) for by in range(chips)]
    sums += [go(chip_sum[0], by_row=0, by_chip=by, flip=0) for by in range(1, chips)]

    half = pl.pallas_call(
        parent_forward_kernel,
        in_specs=[VMEM] * (5 + len(sums)),
        out_specs=VMEM,
        out_shape=jax.ShapeDtypeStruct((nrhs, depth), BF16),
        compiler_params=pltpu.CompilerParams(vmem_limit_bytes=16 << 20),
        cost_estimate=pl.CostEstimate(flops=1 << 25, bytes_accessed=2 << 20, transcendentals=0),
        name="parent_forward",
    )(keep, came, parent_rhs, parent_lower, across, *sums)
    halves = [half] + [go(half, by_row=0, by_chip=by, flip=0) for by in range(1, chips)]

    full, half = pl.pallas_call(
        parent_backward_kernel,
        in_specs=[VMEM] * (2 + chips),
        out_specs=[VMEM, VMEM],
        out_shape=[jax.ShapeDtypeStruct((nrhs, depth), F32), jax.ShapeDtypeStruct((nrhs, depth), BF16)],
        scratch_shapes=[pltpu.VMEM((nrhs, wide), BF16)],
        compiler_params=pltpu.CompilerParams(vmem_limit_bytes=16 << 20),
        cost_estimate=pl.CostEstimate(flops=1 << 25, bytes_accessed=2 << 20, transcendentals=0),
        name="parent_backward",
    )(parent_upper, across, *halves)

    nexts = [go(half, by_row=-1, by_chip=by, flip=0) for by in range(chips)]
    owns = [half] + [go(half, by_row=0, by_chip=by, flip=0) for by in range(1, chips)]
    mine = jnp.stack([jnp.stack(owns), jnp.stack(nexts)])
    theirs = go(mine, by_row=0, by_chip=0, flip=1)

    return pl.pallas_call(
        backward_kernel,
        in_specs=[SMEM] + [VMEM] * 6,
        out_specs=[VMEM, VMEM],
        out_shape=[
            jax.ShapeDtypeStruct((leaves, nrhs, width), F32),
            jax.ShapeDtypeStruct((2, nrhs, cut), F32),
        ],
        scratch_shapes=[pltpu.VMEM((4, nrhs, wide), BF16)],
        compiler_params=pltpu.CompilerParams(vmem_limit_bytes=24 << 20),
        cost_estimate=pl.CostEstimate(flops=1 << 28, bytes_accessed=5 << 20, transcendentals=0),
        name="backward",
    )(listed, solved, full, mine, theirs, upper_blocks, leaf_upper)


def solution(mesh):
    placed = (
        P(("row", "col"), None, None),
        P(("row", "col"), None, None),
        P(("row", "col"), None, None),
        P(("row", "col"), None, None, None),
        P(("row", "col"), None, None, None),
        P("row", None, None),
        P("row", None, "col"),
        P("row", None, "col"),
        P(("row", "col"), None),
    )
    return jax.shard_map(
        local,
        mesh=mesh,
        in_specs=placed,
        out_specs=(P(("row", "col"), None, None), P("row", None, "col")),
        check_vma=False,
    )
```

time: 37.3 us -> 33.3 us (0.89)
  starting transfers between devices: 15.8 us -> 12.8 us
  waiting for transfers between devices: 14.1 us -> 13.3 us
    ppermute x11 -> x10, starting transfers between devices: 15.8 us -> 12.8 us  [send(): return lax.ppermute(array, ('row', 'col'), pairs)]
    ppermute x11 -> x10, waiting for transfers between devices: 14.1 us -> 13.3 us  [send(): return lax.ppermute(array, ('row', 'col'), pairs)]
    pallas_call x2 -> x3, Pallas kernels: 3.46 us -> 3.39 us  [the longest x1 2.84 us: local(): pl.pallas_call(forward_kernel, in_specs=[HBM] * 6, out_specs=[VMEM] * 4,...]
  transfers between devices with their start and end apart: 11 -> 10, of which waited for: 7 -> 8; matrix products, arithmetic and copies ran while one was open for 0% -> 0% of each run, Pallas kernels for 0% -> 0%
where the time goes in v3:
time: 33.3 us; the launch traced here: 33.2 us
  waiting for transfers between devices  13.3 us (40%)
  starting transfers between devices  12.8 us (38%)
  Pallas kernels  6.28 us (19%)
  between operations  0.76 us (2%)
    ppermute x10, waiting for transfers between devices, send(): return lax.ppermute(array, ('row', 'col'), pairs)  13.3 us
    ppermute x10, starting transfers between devices, send(): return lax.ppermute(array, ('row', 'col'), pairs)  12.8 us
    pallas_call x1, Pallas kernels, local(): pl.pallas_call(backward_kernel, in_specs=[SMEM] + [VMEM] * 6, out_specs=[...  2.9 us
    pallas_call x1, Pallas kernels, local(): pl.pallas_call(forward_kernel, in_specs=[HBM] * 6, out_specs=[VMEM] * 4,...  2.84 us
  transfers between devices with their start and end apart: 10, of which 8 were waited for; matrix products, arithmetic and copies ran while one was open for 0% of the time, Pallas kernels for 0%

profile of v3, /device:TPU:0, one launch (start us, length us, event | category | flops | bytes accessed | tf_op | source)
XLA Modules:
  0.0 33.2 jit_solution(12845486290160252732)
XLA Ops:
  0.7 2.8 %forward.1 = (bf16[8,32,128]{2,1,0:T(8,128)(2,1)S(1)}, f32[2,32,1024]{2,1,0:T(8,128)S(1)}, bf16[2,32,1024]{2,1,0:T(8,128)(2,1)S(1)}, bf16[2,1024,256]{2,1,0:T(8,128)(2,1)S(1)}) custom-call(s32[2,8]{1,0:T(2,128)} %bitcast.14, bf16[8,32,128]{2,1,0:T(8,128)(2,1)} %rhs_hbm.1, bf16[8,128,128]{2,1,0:T(8,128)(2,1)} %lower_hbm.1, ...), custom_call_target="tpu_custom_call" | custom-call | flops 536870912 | bytes 5242880 | tf_op jit(solution)/shard_map/forward/pallas_call | solution.py:164
  3.5 0.0 copy-start
  3.5 0.0 copy-start.5
  3.5 0.5 %collective-permute-start = (bf16[2,32,1024]{2,1,0:T(8,128)(2,1)S(1)}, bf16[2,32,1024]{2,1,0:T(8,128)(2,1)S(1)}, u32[]{:S(2)}, u32[]{:S(2)}) collective-permute-start(bf16[2,32,1024]{2,1,0:T(8,128)(2,1)S(1)} %get-tuple-element.11), channel_id=1, source_target_pairs={{0,1},{1,0},{2,3},{3,2},{4,5},{5,4},{6,7},{7,6},{8,9},{9,8},{10,11... | collective-permute-start | bytes 393224 | tf_op jit(solution)/shard_map/ppermute | solution.py:43
  4.1 1.0 %collective-permute-done.came = bf16[2,32,1024]{2,1,0:T(8,128)(2,1)S(1)} collective-permute-done((bf16[2,32,1024]{2,1,0:T(8,128)(2,1)S(1)}, bf16[2,32,1024]{2,1,0:T(8,128)(2,1)S(1)}, u32[]{:S(2)}, u32[]{:S(2)}) %collective-permute-start) | collective-permute-done | bytes 131104 | tf_op jit(solution)/shard_map/ppermute | solution.py:43
  5.0 0.4 %collective-permute-start.1 = (bf16[2,1024,256]{2,1,0:T(8,128)(2,1)S(1)}, bf16[2,1024,256]{2,1,0:T(8,128)(2,1)S(1)}, u32[]{:S(2)}, u32[]{:S(2)}) collective-permute-start(bf16[2,1024,256]{2,1,0:T(8,128)(2,1)S(1)} %get-tuple-element.13), channel_id=1, source_target_pairs={{0,1},{1,0},{2,3},{3,2},{4,5},{5,4},{6,7},{7,6},{8,9},{9,8},{10,11... | collective-permute-start | bytes 3145736 | tf_op jit(solution)/shard_map/ppermute | solution.py:43
  5.5 2.7 %collective-permute-start.2 = (bf16[32,1024]{1,0:T(8,128)(2,1)S(1)}, bf16[32,1024]{1,0:T(8,128)(2,1)S(1)}, u32[]{:S(2)}, u32[]{:S(2)}) collective-permute-start(bf16[32,1024]{1,0:T(8,128)(2,1)S(1)} %get-tuple-element.19), channel_id=1, source_target_pairs={{0,4},{1,5},{2,6},{3,7},{4,8},{5,9},{6,10},{7,11},{8,12},{9,13},{1... | collective-permute-start | bytes 196616 | tf_op jit(solution)/shard_map/ppermute | solution.py:43
  8.2 2.4 %collective-permute-start.3 = (bf16[32,1024]{1,0:T(8,128)(2,1)S(1)}, bf16[32,1024]{1,0:T(8,128)(2,1)S(1)}, u32[]{:S(2)}, u32[]{:S(2)}) collective-permute-start(bf16[32,1024]{1,0:T(8,128)(2,1)S(1)} %get-tuple-element.19), channel_id=1, source_target_pairs={{0,6},{1,7},{2,4},{3,5},{4,10},{5,11},{6,8},{7,9},{8,14},{9,15},{1... | collective-permute-start | bytes 196616 | tf_op jit(solution)/shard_map/ppermute | solution.py:43
  10.6 0.5 %collective-permute-start.4 = (bf16[32,1024]{1,0:T(8,128)(2,1)S(1)}, bf16[32,1024]{1,0:T(8,128)(2,1)S(1)}, u32[]{:S(2)}, u32[]{:S(2)}) collective-permute-start(bf16[32,1024]{1,0:T(8,128)(2,1)S(1)} %get-tuple-element.18), channel_id=1, source_target_pairs={{0,2},{1,3},{2,0},{3,1},{4,6},{5,7},{6,4},{7,5},{8,10},{9,11},{10,... | collective-permute-start | bytes 196616 | tf_op jit(solution)/shard_map/ppermute | solution.py:43
  11.2 2.7 %collective-permute-done.2.rest_0_ = bf16[32,1024]{1,0:T(8,128)(2,1)S(1)} collective-permute-done((bf16[32,1024]{1,0:T(8,128)(2,1)S(1)}, bf16[32,1024]{1,0:T(8,128)(2,1)S(1)}, u32[]{:S(2)}, u32[]{:S(2)}) %collective-permute-start.2) | collective-permute-done | bytes 65568 | tf_op jit(solution)/shard_map/ppermute | solution.py:43
  13.8 2.4 %collective-permute-done.3.rest_1_ = bf16[32,1024]{1,0:T(8,128)(2,1)S(1)} collective-permute-done((bf16[32,1024]{1,0:T(8,128)(2,1)S(1)}, bf16[32,1024]{1,0:T(8,128)(2,1)S(1)}, u32[]{:S(2)}, u32[]{:S(2)}) %collective-permute-start.3) | collective-permute-done | bytes 65568 | tf_op jit(solution)/shard_map/ppermute | solution.py:43
  16.2 0.3 parent_forward.1.rest_0_
  16.5 1.4 %collective-permute-start.5 = (bf16[32,512]{1,0:T(8,128)(2,1)S(1)}, bf16[32,512]{1,0:T(8,128)(2,1)S(1)}, u32[]{:S(2)}, u32[]{:S(2)}) collective-permute-start(bf16[32,512]{1,0:T(8,128)(2,1)S(1)} %parent_forward.1.rest_0_), channel_id=1, source_target_pairs={{0,2},{1,3},{2,0},{3,1},{4,6},{5,7},{6,4},{7,5},{8,10},{9,11},{10,... | collective-permute-start | bytes 98312 | tf_op jit(solution)/shard_map/ppermute | solution.py:43
  18.0 2.5 %collective-permute-done.5.rest_1_ = bf16[32,512]{1,0:T(8,128)(2,1)S(1)} collective-permute-done((bf16[32,512]{1,0:T(8,128)(2,1)S(1)}, bf16[32,512]{1,0:T(8,128)(2,1)S(1)}, u32[]{:S(2)}, u32[]{:S(2)}) %collective-permute-start.5) | collective-permute-done | bytes 32800 | tf_op jit(solution)/shard_map/ppermute | solution.py:43
  20.5 0.3 parent_backward.1
  20.8 3.1 %collective-permute-start.8 = (bf16[32,512]{1,0:T(8,128)(2,1)S(1)}, bf16[32,512]{1,0:T(8,128)(2,1)S(1)}, u32[]{:S(2)}, u32[]{:S(2)}) collective-permute-start(bf16[32,512]{1,0:T(8,128)(2,1)S(1)} %get-tuple-element.17), channel_id=1, source_target_pairs={{0,30},{1,31},{2,28},{3,29},{4,2},{5,3},{6,0},{7,1},{8,6},{9,7},{1... | collective-permute-start | bytes 98312 | tf_op jit(solution)/shard_map/ppermute | solution.py:43
  23.9 1.0 %collective-permute-start.7 = (bf16[32,512]{1,0:T(8,128)(2,1)S(1)}, bf16[32,512]{1,0:T(8,128)(2,1)S(1)}, u32[]{:S(2)}, u32[]{:S(2)}) collective-permute-start(bf16[32,512]{1,0:T(8,128)(2,1)S(1)} %get-tuple-element.17), channel_id=1, source_target_pairs={{0,28},{1,29},{2,30},{3,31},{4,0},{5,1},{6,2},{7,3},{8,4},{9,5},{1... | collective-permute-start | bytes 98312 | tf_op jit(solution)/shard_map/ppermute | solution.py:43
  24.9 0.5 %collective-permute-start.6 = (bf16[32,512]{1,0:T(8,128)(2,1)S(1)}, bf16[32,512]{1,0:T(8,128)(2,1)S(1)}, u32[]{:S(2)}, u32[]{:S(2)}) collective-permute-start(bf16[32,512]{1,0:T(8,128)(2,1)S(1)} %get-tuple-element.17), channel_id=1, source_target_pairs={{0,2},{1,3},{2,0},{3,1},{4,6},{5,7},{6,4},{7,5},{8,10},{9,11},{10,... | collective-permute-start | bytes 98312 | tf_op jit(solution)/shard_map/ppermute | solution.py:43
  25.5 0.3 collective-permute-done.8
  25.8 2.0 %collective-permute-done.7 = bf16[32,512]{1,0:T(8,128)(2,1)S(1)} collective-permute-done((bf16[32,512]{1,0:T(8,128)(2,1)S(1)}, bf16[32,512]{1,0:T(8,128)(2,1)S(1)}, u32[]{:S(2)}, u32[]{:S(2)}) %collective-permute-start.7) | collective-permute-done | bytes 32800 | tf_op jit(solution)/shard_map/ppermute | solution.py:43
  27.8 1.0 %collective-permute-done.6 = bf16[32,512]{1,0:T(8,128)(2,1)S(1)} collective-permute-done((bf16[32,512]{1,0:T(8,128)(2,1)S(1)}, bf16[32,512]{1,0:T(8,128)(2,1)S(1)}, u32[]{:S(2)}, u32[]{:S(2)}) %collective-permute-start.6) | collective-permute-done | bytes 32800 | tf_op jit(solution)/shard_map/ppermute | solution.py:43
  28.9 0.1 collective-permute-start.9
  29.0 1.3 %collective-permute-done.9.theirs = bf16[2,2,32,512]{3,2,1,0:T(8,128)(2,1)S(1)} collective-permute-done((bf16[2,2,32,512]{3,2,1,0:T(8,128)(2,1)S(1)}, bf16[2,2,32,512]{3,2,1,0:T(8,128)(2,1)S(1)}, u32[]{:S(2)}, u32[]{:S(2)}) %collective-permute-start.9) | collective-permute-done | bytes 131104 | tf_op jit(solution)/shard_map/ppermute | solution.py:43
  30.3 2.9 %backward.1 = (f32[8,32,128]{2,1,0:T(8,128)}, f32[2,32,256]{2,1,0:T(8,128)}) custom-call(s32[2,8]{1,0:T(2,128)S(1)} %bitcast.15, bf16[8,32,128]{2,1,0:T(8,128)(2,1)S(1)} %get-tuple-element.10.solved, f32[32,512]{1,0:T(8,128)S(1)} %get-tuple-element.16.own, bf16[2,2,32,512]{3,2,1,0:T(8,128)(2,1)S(1)} %pad_maximum_fusion.mine, ...), custom_call_target="tpu_custom_call" | custom-call | flops 268435456 | bytes 5242880 | tf_op jit(solution)/shard_map/backward/pallas_call | solution.py:221
  (17 shorter events, 0.1 us)
Async XLA Ops:
  0.6 15.6 %copy-start.2 = (bf16[2,1024,256]{2,1,0:T(8,128)(2,1)S(1)}, bf16[2,1024,256]{2,1,0:T(8,128)(2,1)}, u32[]{:S(2)}) copy-start(bf16[2,1024,256]{2,1,0:T(8,128)(2,1)} %lower.1) | copy-start | bytes 3145732
  0.6 15.6 %copy-start.4 = (bf16[2,32,1024]{2,1,0:T(8,128)(2,1)S(1)}, bf16[2,32,1024]{2,1,0:T(8,128)(2,1)}, u32[]{:S(2)}) copy-start(bf16[2,32,1024]{2,1,0:T(8,128)(2,1)} %rhs.1) | copy-start | bytes 393220
  0.7 19.9 %copy-start.1 = (bf16[2,1024,256]{2,1,0:T(8,128)(2,1)S(1)}, bf16[2,1024,256]{2,1,0:T(8,128)(2,1)}, u32[]{:S(2)}) copy-start(bf16[2,1024,256]{2,1,0:T(8,128)(2,1)} %upper.2) | copy-start | bytes 3145732
  3.5 26.8 %copy-start = (bf16[8,2,1024,128]{3,2,1,0:T(8,128)(2,1)S(1)}, bf16[8,2,1024,128]{3,2,1,0:T(8,128)(2,1)}, u32[]{:S(2)}) copy-start(bf16[8,2,1024,128]{3,2,1,0:T(8,128)(2,1)} %blocks.1) | copy-start | bytes 12582916
  3.5 26.8 %copy-start.3 = (bf16[8,128,128]{2,1,0:T(8,128)(2,1)S(1)}, bf16[8,128,128]{2,1,0:T(8,128)(2,1)}, u32[]{:S(2)}) copy-start(bf16[8,128,128]{2,1,0:T(8,128)(2,1)} %upper.3) | copy-start | bytes 786436
  3.5 26.8 %copy-start.5 = (s32[8,2]{0,1:T(2,128)S(1)}, s32[8,2]{0,1:T(2,128)}, u32[]{:S(2)}) copy-start(s32[8,2]{0,1:T(2,128)} %param.17) | copy-start | bytes 196
  3.5 1.5 %collective-permute-start = (bf16[2,32,1024]{2,1,0:T(8,128)(2,1)S(1)}, bf16[2,32,1024]{2,1,0:T(8,128)(2,1)S(1)}, u32[]{:S(2)}, u32[]{:S(2)}) collective-permute-start(bf16[2,32,1024]{2,1,0:T(8,128)(2,1)S(1)} %get-tuple-element.11), channel_id=1, source_target_pairs={{0,1},{1,0},{2,3},{3,2},{4,5},{5,4},{6,7},{7,6},{8,9},{9,8},{10,11... | collective-permute-start | bytes 393224 | tf_op jit(solution)/shard_map/ppermute | solution.py:43
  5.0 11.2 %collective-permute-start.1 = (bf16[2,1024,256]{2,1,0:T(8,128)(2,1)S(1)}, bf16[2,1024,256]{2,1,0:T(8,128)(2,1)S(1)}, u32[]{:S(2)}, u32[]{:S(2)}) collective-permute-start(bf16[2,1024,256]{2,1,0:T(8,128)(2,1)S(1)} %get-tuple-element.13), channel_id=1, source_target_pairs={{0,1},{1,0},{2,3},{3,2},{4,5},{5,4},{6,7},{7,6},{8,9},{9,8},{10,11... | collective-permute-start | bytes 3145736 | tf_op jit(solution)/shard_map/ppermute | solution.py:43
  5.5 8.4 %collective-permute-start.2 = (bf16[32,1024]{1,0:T(8,128)(2,1)S(1)}, bf16[32,1024]{1,0:T(8,128)(2,1)S(1)}, u32[]{:S(2)}, u32[]{:S(2)}) collective-permute-start(bf16[32,1024]{1,0:T(8,128)(2,1)S(1)} %get-tuple-element.19), channel_id=1, source_target_pairs={{0,4},{1,5},{2,6},{3,7},{4,8},{5,9},{6,10},{7,11},{8,12},{9,13},{1... | collective-permute-start | bytes 196616 | tf_op jit(solution)/shard_map/ppermute | solution.py:43
  8.2 8.0 %collective-permute-start.3 = (bf16[32,1024]{1,0:T(8,128)(2,1)S(1)}, bf16[32,1024]{1,0:T(8,128)(2,1)S(1)}, u32[]{:S(2)}, u32[]{:S(2)}) collective-permute-start(bf16[32,1024]{1,0:T(8,128)(2,1)S(1)} %get-tuple-element.19), channel_id=1, source_target_pairs={{0,6},{1,7},{2,4},{3,5},{4,10},{5,11},{6,8},{7,9},{8,14},{9,15},{1... | collective-permute-start | bytes 196616 | tf_op jit(solution)/shard_map/ppermute | solution.py:43
  10.6 5.6 %collective-permute-start.4 = (bf16[32,1024]{1,0:T(8,128)(2,1)S(1)}, bf16[32,1024]{1,0:T(8,128)(2,1)S(1)}, u32[]{:S(2)}, u32[]{:S(2)}) collective-permute-start(bf16[32,1024]{1,0:T(8,128)(2,1)S(1)} %get-tuple-element.18), channel_id=1, source_target_pairs={{0,2},{1,3},{2,0},{3,1},{4,6},{5,7},{6,4},{7,5},{8,10},{9,11},{10,... | collective-permute-start | bytes 196616 | tf_op jit(solution)/shard_map/ppermute | solution.py:43
  16.5 4.0 %collective-permute-start.5 = (bf16[32,512]{1,0:T(8,128)(2,1)S(1)}, bf16[32,512]{1,0:T(8,128)(2,1)S(1)}, u32[]{:S(2)}, u32[]{:S(2)}) collective-permute-start(bf16[32,512]{1,0:T(8,128)(2,1)S(1)} %parent_forward.1.rest_0_), channel_id=1, source_target_pairs={{0,2},{1,3},{2,0},{3,1},{4,6},{5,7},{6,4},{7,5},{8,10},{9,11},{10,... | collective-permute-start | bytes 98312 | tf_op jit(solution)/shard_map/ppermute | solution.py:43
  20.8 5.0 %collective-permute-start.8 = (bf16[32,512]{1,0:T(8,128)(2,1)S(1)}, bf16[32,512]{1,0:T(8,128)(2,1)S(1)}, u32[]{:S(2)}, u32[]{:S(2)}) collective-permute-start(bf16[32,512]{1,0:T(8,128)(2,1)S(1)} %get-tuple-element.17), channel_id=1, source_target_pairs={{0,30},{1,31},{2,28},{3,29},{4,2},{5,3},{6,0},{7,1},{8,6},{9,7},{1... | collective-permute-start | bytes 98312 | tf_op jit(solution)/shard_map/ppermute | solution.py:43
  23.9 3.9 %collective-permute-start.7 = (bf16[32,512]{1,0:T(8,128)(2,1)S(1)}, bf16[32,512]{1,0:T(8,128)(2,1)S(1)}, u32[]{:S(2)}, u32[]{:S(2)}) collective-permute-start(bf16[32,512]{1,0:T(8,128)(2,1)S(1)} %get-tuple-element.17), channel_id=1, source_target_pairs={{0,28},{1,29},{2,30},{3,31},{4,0},{5,1},{6,2},{7,3},{8,4},{9,5},{1... | collective-permute-start | bytes 98312 | tf_op jit(solution)/shard_map/ppermute | solution.py:43
  24.9 3.9 %collective-permute-start.6 = (bf16[32,512]{1,0:T(8,128)(2,1)S(1)}, bf16[32,512]{1,0:T(8,128)(2,1)S(1)}, u32[]{:S(2)}, u32[]{:S(2)}) collective-permute-start(bf16[32,512]{1,0:T(8,128)(2,1)S(1)} %get-tuple-element.17), channel_id=1, source_target_pairs={{0,2},{1,3},{2,0},{3,1},{4,6},{5,7},{6,4},{7,5},{8,10},{9,11},{10,... | collective-permute-start | bytes 98312 | tf_op jit(solution)/shard_map/ppermute | solution.py:43
  28.9 1.4 %collective-permute-start.9 = (bf16[2,2,32,512]{3,2,1,0:T(8,128)(2,1)S(1)}, bf16[2,2,32,512]{3,2,1,0:T(8,128)(2,1)S(1)}, u32[]{:S(2)}, u32[]{:S(2)}) collective-permute-start(bf16[2,2,32,512]{3,2,1,0:T(8,128)(2,1)S(1)} %pad_maximum_fusion.mine), channel_id=1, source_target_pairs={{0,1},{1,0},{2,3},{3,2},{4,5},{5,4},{6,7},{7,6},{8,9},{9,8},{10,11... | collective-permute-start | bytes 393224 | tf_op jit(solution)/shard_map/ppermute | solution.py:43

commit v4 on v3

v4 whole, which is shorter than its diff:
```python
import functools

import jax
import jax.numpy as jnp
from jax import lax
from jax.experimental import pallas as pl
from jax.experimental.pallas import tpu as pltpu
from jax.sharding import PartitionSpec as P

CORES = 2
F32 = jnp.float32
BF16 = jnp.bfloat16
VMEM = pl.BlockSpec(memory_space=pltpu.VMEM)
HBM = pl.BlockSpec(memory_space=pltpu.HBM)


def dot(a, b):
    return jnp.dot(a, b, preferred_element_type=F32)


def in_hbm(*arrays):
    return [pltpu.with_memory_space_constraint(array, pltpu.HBM) for array in arrays]


def place():
    here = lax.axis_index("col")
    chip, core = lax.div(here, CORES), lax.rem(here, CORES)
    return chip, core, lax.rem(chip + core, CORES)


def send(array, rows, cols, by_row, by_chip, other):
    chips = cols // CORES
    pairs = []
    for row in range(rows):
        for col in range(cols):
            chip, core = col // CORES, col % CORES
            to_chip = (chip + by_chip) % chips
            to_core = (chip + core + to_chip + other) % CORES
            pairs.append((row * cols + col, ((row + by_row) % rows) * cols + to_chip * CORES + to_core))
    return lax.ppermute(array, ("row", "col"), pairs)


def columns(index, size):
    return pl.ds(pl.multiple_of(index * size, size), size)


def forward_kernel(targets_hbm, rhs_hbm, lower_hbm, blocks_hbm, solved_ref, keep_ref, give_ref, targets, rhs, lower, blocks, acc, sems):
    leaves, k, width, wide = blocks.shape
    nrhs = rhs.shape[1]
    _, _, parent = place()
    first = [
        pltpu.make_async_copy(targets_hbm, targets, sems.at[0]),
        pltpu.make_async_copy(rhs_hbm, rhs, sems.at[1]),
        pltpu.make_async_copy(lower_hbm, lower, sems.at[2]),
    ]
    copies = [pltpu.make_async_copy(blocks_hbm.at[a], blocks.at[a], sems.at[3 + a]) for a in range(leaves)]
    for copy in first + copies:
        copy.start()
    windows = (parent, 2 + parent, 3 - parent, 1 - parent)
    for copy in first:
        copy.wait()
    solved = [dot(rhs[a], lower[a]).astype(BF16) for a in range(leaves)]
    for a in range(leaves):
        solved_ref[a] = solved[a]
    for a in range(leaves):
        lhs = jnp.concatenate(
            [
                jnp.concatenate(
                    [jnp.where(targets[i, a] == window, solved[a], jnp.zeros_like(solved[a])) for i in range(k)], axis=1
                )
                for window in windows
            ],
            axis=0,
        )
        copies[a].wait()
        part = dot(lhs, blocks[a].reshape(k * width, wide))
        if a == 0:
            acc[...] = part
        elif a + 1 < leaves:
            acc[...] += part
        else:
            total = acc[...] + part
            keep_ref[...] = total[: 3 * nrhs].reshape(3, nrhs, wide)
            give_ref[...] = total[nrhs:].astype(BF16).reshape(3, nrhs, wide)


def parent_forward_kernel(keep, came, rhs, lower, across, *rest):
    sums, half_ref = rest[:-1], rest[-1]
    _, core, parent = place()
    cut = lower.shape[2]
    update = keep[0] + came[2].astype(F32)
    for term in sums:
        update = update + term[...].astype(F32)
    combined = (rhs[parent].astype(F32) - update).astype(BF16)
    half_ref[:, columns(core, cut)] = dot(combined, lower[parent]).astype(BF16)
    half_ref[:, columns(1 - core, cut)] = dot(combined, across[0]).astype(BF16)


def parent_backward_kernel(upper, across, *rest):
    halves, (full_ref, half_ref, forward) = rest[:-3], rest[-3:]
    chips = len(halves)
    chip, core, parent = place()
    cut = upper.shape[2]
    for by, half in enumerate(halves):
        forward[:, columns(lax.rem(chip + chips - by, chips), half.shape[1])] = half[...]
    for at, block in ((core, upper[parent]), (1 - core, across[1])):
        part = dot(forward[...], block)
        full_ref[:, columns(at, cut)] = part
        half_ref[:, columns(at, cut)] = part.astype(BF16)


def backward_kernel(flows, targets, solved, own, mine, theirs, blocks, upper, leaf_ref, parent_ref, window):
    leaves, k, wide, width = blocks.shape
    depth = mine.shape[2]
    chips = wide // depth
    chip, core, parent = place()
    for i, (level, by) in enumerate(flows):
        at = columns(lax.rem(chip + chips - by, chips), depth)
        of = lax.rem(parent + level * (by + 1), CORES)
        window[CORES * level + of, :, at] = mine[i]
        window[CORES * level + 1 - of, :, at] = theirs[i]
    cut = parent_ref.shape[2]
    parent_ref[parent] = own[:, columns(core, cut)]
    parent_ref[1 - parent] = theirs[flows.index((0, 0)), :, columns(core, cut)].astype(F32)
    listed = targets[...]
    couplings = [
        functools.reduce(jnp.add, [dot(window[listed[i, a]], blocks[a, i]) for i in range(k)]) for a in range(leaves)
    ]
    for a in range(leaves):
        reduced = (solved[a].astype(F32) - couplings[a]).astype(BF16)
        leaf_ref[a] = dot(reduced, upper[a])


def local(
    right_side, leaf_lower, leaf_upper, lower_blocks, upper_blocks, parent_rhs, parent_lower, parent_upper, targets
):
    rows, cols = lax.axis_size("row"), lax.axis_size("col")
    chips = cols // CORES
    go = functools.partial(send, rows=rows, cols=cols)
    leaves, k, width, wide = lower_blocks.shape
    nrhs = right_side.shape[1]
    cut = parent_lower.shape[2]
    depth = cut * CORES
    listed = targets.T

    solved, keep, give = pl.pallas_call(
        forward_kernel,
        in_specs=[HBM] * 4,
        out_specs=[VMEM] * 3,
        out_shape=[
            jax.ShapeDtypeStruct((leaves, nrhs, width), BF16),
            jax.ShapeDtypeStruct((3, nrhs, wide), F32),
            jax.ShapeDtypeStruct((3, nrhs, wide), BF16),
        ],
        scratch_shapes=[
            pltpu.SMEM(listed.shape, jnp.int32),
            pltpu.VMEM(right_side.shape, BF16),
            pltpu.VMEM(leaf_lower.shape, BF16),
            pltpu.VMEM(lower_blocks.shape, BF16),
            pltpu.VMEM((4 * nrhs, wide), F32),
            pltpu.SemaphoreType.DMA((3 + leaves,)),
        ],
        compiler_params=pltpu.CompilerParams(vmem_limit_bytes=24 << 20),
        cost_estimate=pl.CostEstimate(flops=1 << 29, bytes_accessed=5 << 20, transcendentals=0),
        name="forward",
    )(*in_hbm(listed, right_side, leaf_lower, lower_blocks))

    give, lower_after, upper_after = lax.optimization_barrier((give, parent_lower, parent_upper))
    came = go(give, by_row=0, by_chip=0, other=1)
    _, _, parent = place()
    across = jnp.stack([lax.dynamic_index_in_dim(x, 1 - parent, 0, False) for x in (lower_after, upper_after)])
    came, across = lax.optimization_barrier((came, across))
    across = go(across, by_row=0, by_chip=0, other=1)
    own_sum = (keep[0] + came[2].astype(F32)).astype(BF16)
    next_sums = [(keep[1] + came[1].astype(F32)).astype(BF16), (keep[2] + came[0].astype(F32)).astype(BF16)]
    sums = [go(next_sums[(by + 1) % CORES], by_row=1, by_chip=by, other=(by + 1) % CORES) for by in range(chips)]
    sums += [go(own_sum, by_row=0, by_chip=by, other=0) for by in range(1, chips)]

    half = pl.pallas_call(
        parent_forward_kernel,
        in_specs=[VMEM] * (5 + len(sums)),
        out_specs=VMEM,
        out_shape=jax.ShapeDtypeStruct((nrhs, depth), BF16),
        compiler_params=pltpu.CompilerParams(vmem_limit_bytes=16 << 20),
        cost_estimate=pl.CostEstimate(flops=1 << 25, bytes_accessed=2 << 20, transcendentals=0),
        name="parent_forward",
    )(keep, came, parent_rhs, lower_after, across, *sums)
    halves = [half] + [go(half, by_row=0, by_chip=by, other=0) for by in range(1, chips)]

    full, half = pl.pallas_call(
        parent_backward_kernel,
        in_specs=[VMEM] * (2 + chips),
        out_specs=[VMEM, VMEM],
        out_shape=[jax.ShapeDtypeStruct((nrhs, depth), F32), jax.ShapeDtypeStruct((nrhs, depth), BF16)],
        scratch_shapes=[pltpu.VMEM((nrhs, wide), BF16)],
        compiler_params=pltpu.CompilerParams(vmem_limit_bytes=16 << 20),
        cost_estimate=pl.CostEstimate(flops=1 << 25, bytes_accessed=2 << 20, transcendentals=0),
        name="parent_backward",
    )(upper_after, across, *halves)

    flows = [(0, 0)] + [(1, by) for by in reversed(range(chips))] + [(0, by) for by in range(1, chips)]
    mine = jnp.stack(
        [
            half if flow == (0, 0) else go(half, by_row=-flow[0], by_chip=flow[1], other=flow[0] * (flow[1] + 1) % CORES)
            for flow in flows
        ]
    )
    theirs = go(mine, by_row=0, by_chip=0, other=1)

    return pl.pallas_call(
        functools.partial(backward_kernel, flows),
        in_specs=[VMEM] * 7,
        out_specs=[VMEM, VMEM],
        out_shape=[
            jax.ShapeDtypeStruct((leaves, nrhs, width), F32),
            jax.ShapeDtypeStruct((2, nrhs, cut), F32),
        ],
        scratch_shapes=[pltpu.VMEM((4, nrhs, wide), BF16)],
        compiler_params=pltpu.CompilerParams(vmem_limit_bytes=24 << 20),
        cost_estimate=pl.CostEstimate(flops=1 << 28, bytes_accessed=5 << 20, transcendentals=0),
        name="backward",
    )(listed, solved, full, mine, theirs, upper_blocks, leaf_upper)


def solution(mesh):
    placed = (
        P(("row", "col"), None, None),
        P(("row", "col"), None, None),
        P(("row", "col"), None, None),
        P(("row", "col"), None, None, None),
        P(("row", "col"), None, None, None),
        P("row", None, None),
        P("row", None, "col"),
        P("row", None, "col"),
        P(("row", "col"), None),
    )
    return jax.shard_map(
        local,
        mesh=mesh,
        in_specs=placed,
        out_specs=(P(("row", "col"), None, None), P("row", None, "col")),
        check_vma=False,
    )
```

time: 33.3 us -> 30.3 us (0.910)
  Pallas kernels: 6.28 us -> 4.84 us
  waiting for transfers between devices: 13.3 us -> 12 us
  starting transfers between devices: 12.8 us -> 12.3 us
    pallas_call x2, Pallas kernels: 5.74 us -> 4.32 us  [the longest x1 2.74 us: local(): pl.pallas_call(forward_kernel, in_specs=[HBM] * 4, out_specs=[VMEM] * 3,...]
    ppermute x10, waiting for transfers between devices: 13.3 us -> 12 us  [send(): return lax.ppermute(array, ('row', 'col'), pairs)]
    ppermute x10, starting transfers between devices: 12.8 us -> 12.3 us  [send(): return lax.ppermute(array, ('row', 'col'), pairs)]
  transfers between devices with their start and end apart: 10 -> 10, of which waited for: 8 -> 7; matrix products, arithmetic and copies ran while one was open for 0% -> 1% of each run, Pallas kernels for 0% -> 0%
where the time goes in v4:
time: 30.3 us; the launch traced here: 30.2 us
  starting transfers between devices  12.3 us (41%)
  waiting for transfers between devices  12 us (40%)
  Pallas kernels  4.84 us (16%)
  between operations  0.74 us (2%)
    ppermute x10, starting transfers between devices, send(): return lax.ppermute(array, ('row', 'col'), pairs)  12.3 us
    ppermute x10, waiting for transfers between devices, send(): return lax.ppermute(array, ('row', 'col'), pairs)  12 us
    pallas_call x1, Pallas kernels, local(): pl.pallas_call(forward_kernel, in_specs=[HBM] * 4, out_specs=[VMEM] * 3,...  2.74 us
    pallas_call x1, Pallas kernels, local(): pl.pallas_call(functools.partial(backward_kernel, flows), in_specs=[VMEM]...  1.58 us
  transfers between devices with their start and end apart: 10, of which 7 were waited for; matrix products, arithmetic and copies ran while one was open for 1% of the time, Pallas kernels for 0%

profile of v4, /device:TPU:0, one launch (start us, length us, event | category | flops | bytes accessed | tf_op | source)
XLA Modules:
  0.0 30.2 jit_solution(17214543444943651394)
XLA Ops:
  0.7 2.7 %forward.1 = (bf16[8,32,128]{2,1,0:T(8,128)(2,1)S(1)}, f32[3,32,1024]{2,1,0:T(8,128)S(1)}, bf16[3,32,1024]{2,1,0:T(8,128)(2,1)S(1)}) custom-call(s32[2,8]{1,0:T(2,128)} %bitcast.12, bf16[8,32,128]{2,1,0:T(8,128)(2,1)} %rhs_hbm.1, bf16[8,128,128]{2,1,0:T(8,128)(2,1)} %lower_hbm.1, bf16[8,2,128,1024]{3,2,1,0:T(8,128)(2,1)} %blocks_hbm.1), custom_call_target="tpu_custom_call" | custom-call | flops 536870912 | bytes 5242880 | tf_op jit(solution)/shard_map/forward/pallas_call | solution.py:146
  3.4 0.5 %collective-permute-start = (bf16[3,32,1024]{2,1,0:T(8,128)(2,1)S(1)}, bf16[3,32,1024]{2,1,0:T(8,128)(2,1)S(1)}, u32[]{:S(2)}, u32[]{:S(2)}) collective-permute-start(bf16[3,32,1024]{2,1,0:T(8,128)(2,1)S(1)} %get-tuple-element.15), channel_id=1, source_target_pairs={{0,1},{1,0},{2,3},{3,2},{4,5},{5,4},{6,7},{7,6},{8,9},{9,8},{10,11... | collective-permute-start | bytes 589832 | tf_op jit(solution)/shard_map/ppermute | solution.py:40
  3.9 0.1 constant_dynamic-slice_fusion
  4.0 0.0 copy-start.3
  4.0 0.1 pad_maximum_fusion
  4.1 0.8 %collective-permute-done.came = bf16[3,32,1024]{2,1,0:T(8,128)(2,1)S(1)} collective-permute-done((bf16[3,32,1024]{2,1,0:T(8,128)(2,1)S(1)}, bf16[3,32,1024]{2,1,0:T(8,128)(2,1)S(1)}, u32[]{:S(2)}, u32[]{:S(2)}) %collective-permute-start) | collective-permute-done | bytes 196640 | tf_op jit(solution)/shard_map/ppermute | solution.py:40
  5.0 0.4 %collective-permute-start.1 = (bf16[2,1024,256]{2,1,0:T(8,128)(2,1)S(1)}, bf16[2,1024,256]{2,1,0:T(8,128)(2,1)S(1)}, u32[]{:S(2)}, u32[]{:S(2)}) collective-permute-start(bf16[2,1024,256]{2,1,0:T(8,128)(2,1)S(1)} %pad_maximum_fusion), channel_id=1, source_target_pairs={{0,1},{1,0},{2,3},{3,2},{4,5},{5,4},{6,7},{7,6},{8,9},{9,8},{10,11... | collective-permute-start | bytes 3145736 | tf_op jit(solution)/shard_map/ppermute | solution.py:40
  5.4 2.7 %collective-permute-start.2 = (bf16[32,1024]{1,0:T(8,128)(2,1)S(1)}, bf16[32,1024]{1,0:T(8,128)(2,1)S(1)}, u32[]{:S(2)}, u32[]{:S(2)}) collective-permute-start(bf16[32,1024]{1,0:T(8,128)(2,1)S(1)} %get-tuple-element.24), channel_id=1, source_target_pairs={{0,5},{1,4},{2,7},{3,6},{4,9},{5,8},{6,11},{7,10},{8,13},{9,12},{1... | collective-permute-start | bytes 196616 | tf_op jit(solution)/shard_map/ppermute | solution.py:40
  8.1 2.2 %collective-permute-start.3 = (bf16[32,1024]{1,0:T(8,128)(2,1)S(1)}, bf16[32,1024]{1,0:T(8,128)(2,1)S(1)}, u32[]{:S(2)}, u32[]{:S(2)}) collective-permute-start(bf16[32,1024]{1,0:T(8,128)(2,1)S(1)} %get-tuple-element.23), channel_id=1, source_target_pairs={{0,7},{1,6},{2,5},{3,4},{4,11},{5,10},{6,9},{7,8},{8,15},{9,14},{1... | collective-permute-start | bytes 196616 | tf_op jit(solution)/shard_map/ppermute | solution.py:40
  10.3 0.5 %collective-permute-start.4 = (bf16[32,1024]{1,0:T(8,128)(2,1)S(1)}, bf16[32,1024]{1,0:T(8,128)(2,1)S(1)}, u32[]{:S(2)}, u32[]{:S(2)}) collective-permute-start(bf16[32,1024]{1,0:T(8,128)(2,1)S(1)} %get-tuple-element.22), channel_id=1, source_target_pairs={{0,3},{1,2},{2,1},{3,0},{4,7},{5,6},{6,5},{7,4},{8,11},{9,10},{10,... | collective-permute-start | bytes 196616 | tf_op jit(solution)/shard_map/ppermute | solution.py:40
  10.8 2.7 %collective-permute-done.2.rest_0_ = bf16[32,1024]{1,0:T(8,128)(2,1)S(1)} collective-permute-done((bf16[32,1024]{1,0:T(8,128)(2,1)S(1)}, bf16[32,1024]{1,0:T(8,128)(2,1)S(1)}, u32[]{:S(2)}, u32[]{:S(2)}) %collective-permute-start.2) | collective-permute-done | bytes 65568 | tf_op jit(solution)/shard_map/ppermute | solution.py:40
  13.5 2.4 %collective-permute-done.3.rest_1_ = bf16[32,1024]{1,0:T(8,128)(2,1)S(1)} collective-permute-done((bf16[32,1024]{1,0:T(8,128)(2,1)S(1)}, bf16[32,1024]{1,0:T(8,128)(2,1)S(1)}, u32[]{:S(2)}, u32[]{:S(2)}) %collective-permute-start.3) | collective-permute-done | bytes 65568 | tf_op jit(solution)/shard_map/ppermute | solution.py:40
  15.9 0.3 parent_forward.1.rest_0_
  16.2 1.2 %collective-permute-start.5 = (bf16[32,512]{1,0:T(8,128)(2,1)S(1)}, bf16[32,512]{1,0:T(8,128)(2,1)S(1)}, u32[]{:S(2)}, u32[]{:S(2)}) collective-permute-start(bf16[32,512]{1,0:T(8,128)(2,1)S(1)} %parent_forward.1.rest_0_), channel_id=1, source_target_pairs={{0,3},{1,2},{2,1},{3,0},{4,7},{5,6},{6,5},{7,4},{8,11},{9,10},{10,... | collective-permute-start | bytes 98312 | tf_op jit(solution)/shard_map/ppermute | solution.py:40
  17.4 2.2 %collective-permute-done.5.rest_1_ = bf16[32,512]{1,0:T(8,128)(2,1)S(1)} collective-permute-done((bf16[32,512]{1,0:T(8,128)(2,1)S(1)}, bf16[32,512]{1,0:T(8,128)(2,1)S(1)}, u32[]{:S(2)}, u32[]{:S(2)}) %collective-permute-start.5) | collective-permute-done | bytes 32800 | tf_op jit(solution)/shard_map/ppermute | solution.py:40
  19.6 0.3 parent_backward.1
  19.9 2.9 %collective-permute-start.6 = (bf16[32,512]{1,0:T(8,128)(2,1)S(1)}, bf16[32,512]{1,0:T(8,128)(2,1)S(1)}, u32[]{:S(2)}, u32[]{:S(2)}) collective-permute-start(bf16[32,512]{1,0:T(8,128)(2,1)S(1)} %get-tuple-element.21), channel_id=1, source_target_pairs={{0,31},{1,30},{2,29},{3,28},{4,3},{5,2},{6,1},{7,0},{8,7},{9,6},{1... | collective-permute-start | bytes 98312 | tf_op jit(solution)/shard_map/ppermute | solution.py:40
  22.7 1.1 %collective-permute-start.7 = (bf16[32,512]{1,0:T(8,128)(2,1)S(1)}, bf16[32,512]{1,0:T(8,128)(2,1)S(1)}, u32[]{:S(2)}, u32[]{:S(2)}) collective-permute-start(bf16[32,512]{1,0:T(8,128)(2,1)S(1)} %get-tuple-element.21), channel_id=1, source_target_pairs={{0,29},{1,28},{2,31},{3,30},{4,1},{5,0},{6,3},{7,2},{8,5},{9,4},{1... | collective-permute-start | bytes 98312 | tf_op jit(solution)/shard_map/ppermute | solution.py:40
  23.8 0.7 %collective-permute-start.8 = (bf16[32,512]{1,0:T(8,128)(2,1)S(1)}, bf16[32,512]{1,0:T(8,128)(2,1)S(1)}, u32[]{:S(2)}, u32[]{:S(2)}) collective-permute-start(bf16[32,512]{1,0:T(8,128)(2,1)S(1)} %get-tuple-element.21), channel_id=1, source_target_pairs={{0,3},{1,2},{2,1},{3,0},{4,7},{5,6},{6,5},{7,4},{8,11},{9,10},{10,... | collective-permute-start | bytes 98312 | tf_op jit(solution)/shard_map/ppermute | solution.py:40
  24.5 1.7 %collective-permute-done.7 = bf16[32,512]{1,0:T(8,128)(2,1)S(1)} collective-permute-done((bf16[32,512]{1,0:T(8,128)(2,1)S(1)}, bf16[32,512]{1,0:T(8,128)(2,1)S(1)}, u32[]{:S(2)}, u32[]{:S(2)}) %collective-permute-start.7) | collective-permute-done | bytes 32800 | tf_op jit(solution)/shard_map/ppermute | solution.py:40
  26.2 1.0 %collective-permute-done.8 = bf16[32,512]{1,0:T(8,128)(2,1)S(1)} collective-permute-done((bf16[32,512]{1,0:T(8,128)(2,1)S(1)}, bf16[32,512]{1,0:T(8,128)(2,1)S(1)}, u32[]{:S(2)}, u32[]{:S(2)}) %collective-permute-start.8) | collective-permute-done | bytes 32800 | tf_op jit(solution)/shard_map/ppermute | solution.py:40
  27.2 0.2 collective-permute-start.9
  27.4 1.2 %collective-permute-done.9.theirs = bf16[4,32,512]{2,1,0:T(8,128)(2,1)S(1)} collective-permute-done((bf16[4,32,512]{2,1,0:T(8,128)(2,1)S(1)}, bf16[4,32,512]{2,1,0:T(8,128)(2,1)S(1)}, u32[]{:S(2)}, u32[]{:S(2)}) %collective-permute-start.9) | collective-permute-done | bytes 131104 | tf_op jit(solution)/shard_map/ppermute | solution.py:40
  28.6 1.6 %backward.1 = (f32[8,32,128]{2,1,0:T(8,128)}, f32[2,32,256]{2,1,0:T(8,128)}) custom-call(s32[2,8]{1,0:T(2,128)S(1)} %bitcast.13, bf16[8,32,128]{2,1,0:T(8,128)(2,1)S(1)} %get-tuple-element.12.solved, f32[32,512]{1,0:T(8,128)S(1)} %get-tuple-element.20.own, bf16[4,32,512]{2,1,0:T(8,128)(2,1)S(1)} %pad_maximum_fusion.1.mine, ...), custom_call_target="tpu_custom_call" | custom-call | flops 268435456 | bytes 5242880 | tf_op jit(solution)/shard_map/backward/pallas_call | solution.py:210
  (16 shorter events, 0.1 us)
Async XLA Ops:
  0.6 3.3 %copy-start.1 = (bf16[2,1024,256]{2,1,0:T(8,128)(2,1)S(1)}, bf16[2,1024,256]{2,1,0:T(8,128)(2,1)}, u32[]{:S(2)}) copy-start(bf16[2,1024,256]{2,1,0:T(8,128)(2,1)} %lower) | copy-start | bytes 3145732
  0.6 3.3 %copy-start.2 = (bf16[2,1024,256]{2,1,0:T(8,128)(2,1)S(1)}, bf16[2,1024,256]{2,1,0:T(8,128)(2,1)}, u32[]{:S(2)}) copy-start(bf16[2,1024,256]{2,1,0:T(8,128)(2,1)} %upper.1) | copy-start | bytes 3145732
  0.7 15.2 %copy-start.4 = (bf16[2,32,1024]{2,1,0:T(8,128)(2,1)S(1)}, bf16[2,32,1024]{2,1,0:T(8,128)(2,1)}, u32[]{:S(2)}) copy-start(bf16[2,32,1024]{2,1,0:T(8,128)(2,1)} %rhs.1) | copy-start | bytes 393220
  3.4 1.6 %collective-permute-start = (bf16[3,32,1024]{2,1,0:T(8,128)(2,1)S(1)}, bf16[3,32,1024]{2,1,0:T(8,128)(2,1)S(1)}, u32[]{:S(2)}, u32[]{:S(2)}) collective-permute-start(bf16[3,32,1024]{2,1,0:T(8,128)(2,1)S(1)} %get-tuple-element.15), channel_id=1, source_target_pairs={{0,1},{1,0},{2,3},{3,2},{4,5},{5,4},{6,7},{7,6},{8,9},{9,8},{10,11... | collective-permute-start | bytes 589832 | tf_op jit(solution)/shard_map/ppermute | solution.py:40
  4.0 24.6 %copy-start = (bf16[8,2,1024,128]{3,2,1,0:T(8,128)(2,1)S(1)}, bf16[8,2,1024,128]{3,2,1,0:T(8,128)(2,1)}, u32[]{:S(2)}) copy-start(bf16[8,2,1024,128]{3,2,1,0:T(8,128)(2,1)} %blocks.1) | copy-start | bytes 12582916
  4.0 24.6 %copy-start.3 = (bf16[8,128,128]{2,1,0:T(8,128)(2,1)S(1)}, bf16[8,128,128]{2,1,0:T(8,128)(2,1)}, u32[]{:S(2)}) copy-start(bf16[8,128,128]{2,1,0:T(8,128)(2,1)} %upper.2) | copy-start | bytes 786436
  4.0 24.5 %copy-start.5 = (s32[8,2]{0,1:T(2,128)S(1)}, s32[8,2]{0,1:T(2,128)}, u32[]{:S(2)}) copy-start(s32[8,2]{0,1:T(2,128)} %param.17) | copy-start | bytes 196
  5.0 10.9 %collective-permute-start.1 = (bf16[2,1024,256]{2,1,0:T(8,128)(2,1)S(1)}, bf16[2,1024,256]{2,1,0:T(8,128)(2,1)S(1)}, u32[]{:S(2)}, u32[]{:S(2)}) collective-permute-start(bf16[2,1024,256]{2,1,0:T(8,128)(2,1)S(1)} %pad_maximum_fusion), channel_id=1, source_target_pairs={{0,1},{1,0},{2,3},{3,2},{4,5},{5,4},{6,7},{7,6},{8,9},{9,8},{10,11... | collective-permute-start | bytes 3145736 | tf_op jit(solution)/shard_map/ppermute | solution.py:40
  5.4 8.0 %collective-permute-start.2 = (bf16[32,1024]{1,0:T(8,128)(2,1)S(1)}, bf16[32,1024]{1,0:T(8,128)(2,1)S(1)}, u32[]{:S(2)}, u32[]{:S(2)}) collective-permute-start(bf16[32,1024]{1,0:T(8,128)(2,1)S(1)} %get-tuple-element.24), channel_id=1, source_target_pairs={{0,5},{1,4},{2,7},{3,6},{4,9},{5,8},{6,11},{7,10},{8,13},{9,12},{1... | collective-permute-start | bytes 196616 | tf_op jit(solution)/shard_map/ppermute | solution.py:40
  8.1 7.8 %collective-permute-start.3 = (bf16[32,1024]{1,0:T(8,128)(2,1)S(1)}, bf16[32,1024]{1,0:T(8,128)(2,1)S(1)}, u32[]{:S(2)}, u32[]{:S(2)}) collective-permute-start(bf16[32,1024]{1,0:T(8,128)(2,1)S(1)} %get-tuple-element.23), channel_id=1, source_target_pairs={{0,7},{1,6},{2,5},{3,4},{4,11},{5,10},{6,9},{7,8},{8,15},{9,14},{1... | collective-permute-start | bytes 196616 | tf_op jit(solution)/shard_map/ppermute | solution.py:40
  10.3 5.6 %collective-permute-start.4 = (bf16[32,1024]{1,0:T(8,128)(2,1)S(1)}, bf16[32,1024]{1,0:T(8,128)(2,1)S(1)}, u32[]{:S(2)}, u32[]{:S(2)}) collective-permute-start(bf16[32,1024]{1,0:T(8,128)(2,1)S(1)} %get-tuple-element.22), channel_id=1, source_target_pairs={{0,3},{1,2},{2,1},{3,0},{4,7},{5,6},{6,5},{7,4},{8,11},{9,10},{10,... | collective-permute-start | bytes 196616 | tf_op jit(solution)/shard_map/ppermute | solution.py:40
  16.2 3.4 %collective-permute-start.5 = (bf16[32,512]{1,0:T(8,128)(2,1)S(1)}, bf16[32,512]{1,0:T(8,128)(2,1)S(1)}, u32[]{:S(2)}, u32[]{:S(2)}) collective-permute-start(bf16[32,512]{1,0:T(8,128)(2,1)S(1)} %parent_forward.1.rest_0_), channel_id=1, source_target_pairs={{0,3},{1,2},{2,1},{3,0},{4,7},{5,6},{6,5},{7,4},{8,11},{9,10},{10,... | collective-permute-start | bytes 98312 | tf_op jit(solution)/shard_map/ppermute | solution.py:40
  19.9 4.6 %collective-permute-start.6 = (bf16[32,512]{1,0:T(8,128)(2,1)S(1)}, bf16[32,512]{1,0:T(8,128)(2,1)S(1)}, u32[]{:S(2)}, u32[]{:S(2)}) collective-permute-start(bf16[32,512]{1,0:T(8,128)(2,1)S(1)} %get-tuple-element.21), channel_id=1, source_target_pairs={{0,31},{1,30},{2,29},{3,28},{4,3},{5,2},{6,1},{7,0},{8,7},{9,6},{1... | collective-permute-start | bytes 98312 | tf_op jit(solution)/shard_map/ppermute | solution.py:40
  22.7 3.4 %collective-permute-start.7 = (bf16[32,512]{1,0:T(8,128)(2,1)S(1)}, bf16[32,512]{1,0:T(8,128)(2,1)S(1)}, u32[]{:S(2)}, u32[]{:S(2)}) collective-permute-start(bf16[32,512]{1,0:T(8,128)(2,1)S(1)} %get-tuple-element.21), channel_id=1, source_target_pairs={{0,29},{1,28},{2,31},{3,30},{4,1},{5,0},{6,3},{7,2},{8,5},{9,4},{1... | collective-permute-start | bytes 98312 | tf_op jit(solution)/shard_map/ppermute | solution.py:40
  23.8 3.3 %collective-permute-start.8 = (bf16[32,512]{1,0:T(8,128)(2,1)S(1)}, bf16[32,512]{1,0:T(8,128)(2,1)S(1)}, u32[]{:S(2)}, u32[]{:S(2)}) collective-permute-start(bf16[32,512]{1,0:T(8,128)(2,1)S(1)} %get-tuple-element.21), channel_id=1, source_target_pairs={{0,3},{1,2},{2,1},{3,0},{4,7},{5,6},{6,5},{7,4},{8,11},{9,10},{10,... | collective-permute-start | bytes 98312 | tf_op jit(solution)/shard_map/ppermute | solution.py:40
  27.2 1.4 %collective-permute-start.9 = (bf16[4,32,512]{2,1,0:T(8,128)(2,1)S(1)}, bf16[4,32,512]{2,1,0:T(8,128)(2,1)S(1)}, u32[]{:S(2)}, u32[]{:S(2)}) collective-permute-start(bf16[4,32,512]{2,1,0:T(8,128)(2,1)S(1)} %pad_maximum_fusion.1.mine), channel_id=1, source_target_pairs={{0,1},{1,0},{2,3},{3,2},{4,5},{5,4},{6,7},{7,6},{8,9},{9,8},{10,11... | collective-permute-start | bytes 393224 | tf_op jit(solution)/shard_map/ppermute | solution.py:40

commit v5 on v4

--- a/solution.py
+++ b/solution.py
@@ -28,16 +28,22 @@
     return chip, core, lax.rem(chip + core, CORES)
 
 
-def send(array, rows, cols, by_row, by_chip, other):
+def send(array, rows, cols, by_row, target):
     chips = cols // CORES
     pairs = []
     for row in range(rows):
         for col in range(cols):
-            chip, core = col // CORES, col % CORES
-            to_chip = (chip + by_chip) % chips
-            to_core = (chip + core + to_chip + other) % CORES
-            pairs.append((row * cols + col, ((row + by_row) % rows) * cols + to_chip * CORES + to_core))
+            chip, core = target(col // CORES, col % CORES)
+            pairs.append((row * cols + col, ((row + by_row) % rows) * cols + chip % chips * CORES + core))
     return lax.ppermute(array, ("row", "col"), pairs)
+
+
+def along(by, other=0):
+    return lambda chip, core: (chip + by, (core + by + other) % CORES)
+
+
+def fan(by):
+    return lambda chip, core: (chip + by + core, core)
 
 
 def columns(index, size):
@@ -97,31 +103,34 @@
 
 
 def parent_backward_kernel(upper, across, *rest):
-    halves, (full_ref, half_ref, forward) = rest[:-3], rest[-3:]
-    chips = len(halves)
+    mine, theirs, parent_ref, half_ref, forward = rest
+    chips = mine.shape[0]
     chip, core, parent = place()
     cut = upper.shape[2]
+    for by in range(chips):
+        at = columns(lax.rem(chip + chips - by, chips), mine.shape[2])
+        forward[parent, :, at] = mine[by]
+        forward[1 - parent, :, at] = theirs[by]
+    for this in range(CORES):
+        part = dot(forward[this], upper[this])
+        parent_ref[this] = part
+        half_ref[this, :, columns(core, cut)] = part.astype(BF16)
+        half_ref[this, :, columns(1 - core, cut)] = dot(forward[this], across[1 + this]).astype(BF16)
+
+
+def backward_kernel(targets, full, solved, mine, theirs, blocks, upper, *rest):
+    halves, (leaf_ref, parent_ref, window) = rest[:-3], rest[-3:]
+    parent_ref[...] = full[...]
+    leaves, k, wide, width = blocks.shape
+    chips = len(halves)
+    depth = wide // chips
+    chip, core, _ = place()
     for by, half in enumerate(halves):
-        forward[:, columns(lax.rem(chip + chips - by, chips), half.shape[1])] = half[...]
-    for at, block in ((core, upper[parent]), (1 - core, across[1])):
-        part = dot(forward[...], block)
-        full_ref[:, columns(at, cut)] = part
-        half_ref[:, columns(at, cut)] = part.astype(BF16)
-
-
-def backward_kernel(flows, targets, solved, own, mine, theirs, blocks, upper, leaf_ref, parent_ref, window):
-    leaves, k, wide, width = blocks.shape
-    depth = mine.shape[2]
-    chips = wide // depth
-    chip, core, parent = place()
-    for i, (level, by) in enumerate(flows):
-        at = columns(lax.rem(chip + chips - by, chips), depth)
-        of = lax.rem(parent + level * (by + 1), CORES)
-        window[CORES * level + of, :, at] = mine[i]
-        window[CORES * level + 1 - of, :, at] = theirs[i]
-    cut = parent_ref.shape[2]
-    parent_ref[parent] = own[:, columns(core, cut)]
-    parent_ref[1 - parent] = theirs[flows.index((0, 0)), :, columns(core, cut)].astype(F32)
+        window[pl.ds(0, 2), :, columns(lax.rem(chip + chips - by, chips), depth)] = half[...]
+    for by in range(0, chips, CORES):
+        for arrived, lag in ((mine, core), (theirs, 1 - core)):
+            at = columns(lax.rem(chip + chips - by - lag, chips), depth)
+            window[pl.ds(2, 2), :, at] = arrived[by // CORES]
     listed = targets[...]
     couplings = [
         functools.reduce(jnp.add, [dot(window[listed[i, a]], blocks[a, i]) for i in range(k)]) for a in range(leaves)
@@ -165,16 +174,18 @@
         name="forward",
     )(*in_hbm(listed, right_side, leaf_lower, lower_blocks))
 
-    give, lower_after, upper_after = lax.optimization_barrier((give, parent_lower, parent_upper))
-    came = go(give, by_row=0, by_chip=0, other=1)
+    give, lower, upper = lax.optimization_barrier((give, parent_lower, parent_upper))
+    came = go(give, by_row=0, target=along(0, 1))
     _, _, parent = place()
-    across = jnp.stack([lax.dynamic_index_in_dim(x, 1 - parent, 0, False) for x in (lower_after, upper_after)])
+    across = jnp.concatenate([lax.dynamic_index_in_dim(lower, 1 - parent, 0), upper])
     came, across = lax.optimization_barrier((came, across))
-    across = go(across, by_row=0, by_chip=0, other=1)
+    across = go(across, by_row=0, target=along(0, 1))
     own_sum = (keep[0] + came[2].astype(F32)).astype(BF16)
     next_sums = [(keep[1] + came[1].astype(F32)).astype(BF16), (keep[2] + came[0].astype(F32)).astype(BF16)]
-    sums = [go(next_sums[(by + 1) % CORES], by_row=1, by_chip=by, other=(by + 1) % CORES) for by in range(chips)]
-    sums += [go(own_sum, by_row=0, by_chip=by, other=0) for by in range(1, chips)]
+    sums = [
+        go(next_sums[(by + 1) % CORES], by_row=1, target=along(by, (by + 1) % CORES)) for by in reversed(range(chips))
+    ]
+    sums += [go(own_sum, by_row=0, target=along(by)) for by in range(1, chips)]
 
     half = pl.pallas_call(
         parent_forward_kernel,
@@ -184,42 +195,35 @@
         compiler_params=pltpu.CompilerParams(vmem_limit_bytes=16 << 20),
         cost_estimate=pl.CostEstimate(flops=1 << 25, bytes_accessed=2 << 20, transcendentals=0),
         name="parent_forward",
-    )(keep, came, parent_rhs, lower_after, across, *sums)
-    halves = [half] + [go(half, by_row=0, by_chip=by, other=0) for by in range(1, chips)]
+    )(keep, came, parent_rhs, lower, across, *sums)
+    halves = jnp.stack([half] + [go(half, by_row=0, target=along(by)) for by in range(1, chips)])
+    halves = (halves, go(halves, by_row=0, target=along(0, 1)))
 
     full, half = pl.pallas_call(
         parent_backward_kernel,
-        in_specs=[VMEM] * (2 + chips),
+        in_specs=[VMEM] * (2 + len(halves)),
         out_specs=[VMEM, VMEM],
-        out_shape=[jax.ShapeDtypeStruct((nrhs, depth), F32), jax.ShapeDtypeStruct((nrhs, depth), BF16)],
-        scratch_shapes=[pltpu.VMEM((nrhs, wide), BF16)],
+        out_shape=[jax.ShapeDtypeStruct((2, nrhs, cut), F32), jax.ShapeDtypeStruct((2, nrhs, depth), BF16)],
+        scratch_shapes=[pltpu.VMEM((2, nrhs, wide), BF16)],
         compiler_params=pltpu.CompilerParams(vmem_limit_bytes=16 << 20),
-        cost_estimate=pl.CostEstimate(flops=1 << 25, bytes_accessed=2 << 20, transcendentals=0),
+        cost_estimate=pl.CostEstimate(flops=1 << 26, bytes_accessed=4 << 20, transcendentals=0),
         name="parent_backward",
-    )(upper_after, across, *halves)
-
-    flows = [(0, 0)] + [(1, by) for by in reversed(range(chips))] + [(0, by) for by in range(1, chips)]
-    mine = jnp.stack(
-        [
-            half if flow == (0, 0) else go(half, by_row=-flow[0], by_chip=flow[1], other=flow[0] * (flow[1] + 1) % CORES)
-            for flow in flows
-        ]
-    )
-    theirs = go(mine, by_row=0, by_chip=0, other=1)
+    )(upper, across, *halves)
+
+    halves = [half] + [go(half, by_row=0, target=along(by, (by + 1) % CORES)) for by in range(1, chips)]
+    mine = jnp.stack([go(half, by_row=-1, target=fan(by)) for by in range(0, chips, CORES)])
+    theirs = go(mine, by_row=0, target=along(0, 1))
 
     return pl.pallas_call(
-        functools.partial(backward_kernel, flows),
-        in_specs=[VMEM] * 7,
+        backward_kernel,
+        in_specs=[VMEM] * (7 + chips),
         out_specs=[VMEM, VMEM],
-        out_shape=[
-            jax.ShapeDtypeStruct((leaves, nrhs, width), F32),
-            jax.ShapeDtypeStruct((2, nrhs, cut), F32),
-        ],
+        out_shape=[jax.ShapeDtypeStruct((leaves, nrhs, width), F32), jax.ShapeDtypeStruct(full.shape, F32)],
         scratch_shapes=[pltpu.VMEM((4, nrhs, wide), BF16)],
         compiler_params=pltpu.CompilerParams(vmem_limit_bytes=24 << 20),
         cost_estimate=pl.CostEstimate(flops=1 << 28, bytes_accessed=5 << 20, transcendentals=0),
         name="backward",
-    )(listed, solved, full, mine, theirs, upper_blocks, leaf_upper)
+    )(listed, full, solved, mine, theirs, upper_blocks, leaf_upper, *halves)
 
 
 def solution(mesh):

time: 30.3 us -> 29.3 us (0.967)
  starting transfers between devices: 12.3 us -> 10.7 us
  local copies, waits for them, and re-layouts: 0.1 us -> 0.72 us
    ppermute x10, starting transfers between devices: 12.3 us -> 10.7 us  [send(): return lax.ppermute(array, ('row', 'col'), pairs)]
    unnamed x12, local copies, waits for them, and re-layouts: 0.03 us -> 0.69 us
  transfers between devices with their start and end apart: 10 -> 10, of which waited for: 7 -> 8; matrix products, arithmetic and copies ran while one was open for 1% -> 1% of each run, Pallas kernels for 0% -> 0%
where the time goes in v5:
time: 29.3 us; the launch traced here: 29.1 us
  waiting for transfers between devices  11.8 us (40%)
  starting transfers between devices  10.7 us (37%)
  Pallas kernels  4.98 us (17%)
  local copies, waits for them, and re-layouts  0.72 us (2%)
  between operations  0.72 us (2%)
    ppermute x10, waiting for transfers between devices, send(): return lax.ppermute(array, ('row', 'col'), pairs)  11.8 us
    ppermute x10, starting transfers between devices, send(): return lax.ppermute(array, ('row', 'col'), pairs)  10.7 us
    pallas_call x1, Pallas kernels, local(): pl.pallas_call(forward_kernel, in_specs=[HBM] * 4, out_specs=[VMEM] * 3,...  2.68 us
    pallas_call x1, Pallas kernels, local(): pl.pallas_call(backward_kernel, in_specs=[VMEM] * (7 + chips), out_specs=...  1.58 us
    unnamed x12, local copies, waits for them, and re-layouts  0.69 us
  transfers between devices with their start and end apart: 10, of which 8 were waited for; matrix products, arithmetic and copies ran while one was open for 1% of the time, Pallas kernels for 0%

profile of v5, /device:TPU:0, one launch (start us, length us, event | category | flops | bytes accessed | tf_op | source)
XLA Modules:
  0.0 29.1 jit_solution(15415931335201996044)
XLA Ops:
  0.6 2.7 %forward.1 = (bf16[8,32,128]{2,1,0:T(8,128)(2,1)S(1)}, f32[3,32,1024]{2,1,0:T(8,128)S(1)}, bf16[3,32,1024]{2,1,0:T(8,128)(2,1)S(1)}) custom-call(s32[2,8]{1,0:T(2,128)} %bitcast.13, bf16[8,32,128]{2,1,0:T(8,128)(2,1)} %rhs_hbm.1, bf16[8,128,128]{2,1,0:T(8,128)(2,1)} %lower_hbm.1, bf16[8,2,128,1024]{3,2,1,0:T(8,128)(2,1)} %blocks_hbm.1), custom_call_target="tpu_custom_call" | custom-call | flops 536870912 | bytes 5242880 | tf_op jit(solution)/shard_map/forward/pallas_call | solution.py:155
  3.3 0.0 copy-start
  3.3 0.5 %collective-permute-start = (bf16[3,32,1024]{2,1,0:T(8,128)(2,1)S(1)}, bf16[3,32,1024]{2,1,0:T(8,128)(2,1)S(1)}, u32[]{:S(2)}, u32[]{:S(2)}) collective-permute-start(bf16[3,32,1024]{2,1,0:T(8,128)(2,1)S(1)} %get-tuple-element.14), channel_id=1, source_target_pairs={{0,1},{1,0},{2,3},{3,2},{4,5},{5,4},{6,7},{7,6},{8,9},{9,8},{10,11... | collective-permute-start | bytes 589832 | tf_op jit(solution)/shard_map/ppermute | solution.py:38
  3.9 0.7 %copy-done = bf16[2,1024,256]{2,1,0:T(8,128)(2,1)S(1)} copy-done((bf16[2,1024,256]{2,1,0:T(8,128)(2,1)S(1)}, bf16[2,1024,256]{2,1,0:T(8,128)(2,1)}, u32[]{:S(2)}) %copy-start) | copy-done | bytes 1048600
  4.6 0.1 pad_maximum_fusion
  4.7 0.2 collective-permute-done.came
  4.9 0.4 %collective-permute-start.1 = (bf16[3,1024,256]{2,1,0:T(8,128)(2,1)S(1)}, bf16[3,1024,256]{2,1,0:T(8,128)(2,1)S(1)}, u32[]{:S(2)}, u32[]{:S(2)}) collective-permute-start(bf16[3,1024,256]{2,1,0:T(8,128)(2,1)S(1)} %pad_maximum_fusion), channel_id=1, source_target_pairs={{0,1},{1,0},{2,3},{3,2},{4,5},{5,4},{6,7},{7,6},{8,9},{9,8},{10,11... | collective-permute-start | bytes 4718600 | tf_op jit(solution)/shard_map/ppermute | solution.py:38
  5.3 3.6 %collective-permute-start.2 = (bf16[32,1024]{1,0:T(8,128)(2,1)S(1)}, bf16[32,1024]{1,0:T(8,128)(2,1)S(1)}, u32[]{:S(2)}, u32[]{:S(2)}) collective-permute-start(bf16[32,1024]{1,0:T(8,128)(2,1)S(1)} %get-tuple-element.24), channel_id=1, source_target_pairs={{0,7},{1,6},{2,5},{3,4},{4,11},{5,10},{6,9},{7,8},{8,15},{9,14},{1... | collective-permute-start | bytes 196616 | tf_op jit(solution)/shard_map/ppermute | solution.py:38
  9.0 1.3 %collective-permute-start.3 = (bf16[32,1024]{1,0:T(8,128)(2,1)S(1)}, bf16[32,1024]{1,0:T(8,128)(2,1)S(1)}, u32[]{:S(2)}, u32[]{:S(2)}) collective-permute-start(bf16[32,1024]{1,0:T(8,128)(2,1)S(1)} %get-tuple-element.23), channel_id=1, source_target_pairs={{0,5},{1,4},{2,7},{3,6},{4,9},{5,8},{6,11},{7,10},{8,13},{9,12},{1... | collective-permute-start | bytes 196616 | tf_op jit(solution)/shard_map/ppermute | solution.py:38
  10.2 0.5 %collective-permute-start.4 = (bf16[32,1024]{1,0:T(8,128)(2,1)S(1)}, bf16[32,1024]{1,0:T(8,128)(2,1)S(1)}, u32[]{:S(2)}, u32[]{:S(2)}) collective-permute-start(bf16[32,1024]{1,0:T(8,128)(2,1)S(1)} %get-tuple-element.22), channel_id=1, source_target_pairs={{0,3},{1,2},{2,1},{3,0},{4,7},{5,6},{6,5},{7,4},{8,11},{9,10},{10,... | collective-permute-start | bytes 196616 | tf_op jit(solution)/shard_map/ppermute | solution.py:38
  10.7 3.6 %collective-permute-done.2.rest_0_ = bf16[32,1024]{1,0:T(8,128)(2,1)S(1)} collective-permute-done((bf16[32,1024]{1,0:T(8,128)(2,1)S(1)}, bf16[32,1024]{1,0:T(8,128)(2,1)S(1)}, u32[]{:S(2)}, u32[]{:S(2)}) %collective-permute-start.2) | collective-permute-done | bytes 65568 | tf_op jit(solution)/shard_map/ppermute | solution.py:38
  14.3 1.4 %collective-permute-done.3.rest_1_ = bf16[32,1024]{1,0:T(8,128)(2,1)S(1)} collective-permute-done((bf16[32,1024]{1,0:T(8,128)(2,1)S(1)}, bf16[32,1024]{1,0:T(8,128)(2,1)S(1)}, u32[]{:S(2)}, u32[]{:S(2)}) %collective-permute-start.3) | collective-permute-done | bytes 65568 | tf_op jit(solution)/shard_map/ppermute | solution.py:38
  15.8 0.3 parent_forward.1
  16.1 1.2 %collective-permute-start.5 = (bf16[32,512]{1,0:T(8,128)(2,1)S(1)}, bf16[32,512]{1,0:T(8,128)(2,1)S(1)}, u32[]{:S(2)}, u32[]{:S(2)}) collective-permute-start(bf16[32,512]{1,0:T(8,128)(2,1)S(1)} %parent_forward.1), channel_id=1, source_target_pairs={{0,3},{1,2},{2,1},{3,0},{4,7},{5,6},{6,5},{7,4},{8,11},{9,10},{10,... | collective-permute-start | bytes 98312 | tf_op jit(solution)/shard_map/ppermute | solution.py:38
  17.3 2.2 %collective-permute-done.5 = bf16[32,512]{1,0:T(8,128)(2,1)S(1)} collective-permute-done((bf16[32,512]{1,0:T(8,128)(2,1)S(1)}, bf16[32,512]{1,0:T(8,128)(2,1)S(1)}, u32[]{:S(2)}, u32[]{:S(2)}) %collective-permute-start.5) | collective-permute-done | bytes 32800 | tf_op jit(solution)/shard_map/ppermute | solution.py:38
  19.5 0.2 collective-permute-start.6
  19.7 1.1 %collective-permute-done.6.rest_1_ = bf16[2,32,512]{2,1,0:T(8,128)(2,1)S(1)} collective-permute-done((bf16[2,32,512]{2,1,0:T(8,128)(2,1)S(1)}, bf16[2,32,512]{2,1,0:T(8,128)(2,1)S(1)}, u32[]{:S(2)}, u32[]{:S(2)}) %collective-permute-start.6) | collective-permute-done | bytes 65568 | tf_op jit(solution)/shard_map/ppermute | solution.py:38
  20.8 0.5 %parent_backward.1 = (f32[2,32,256]{2,1,0:T(8,128)S(1)}, bf16[2,32,512]{2,1,0:T(8,128)(2,1)S(1)}) custom-call(bf16[2,1024,256]{2,1,0:T(8,128)(2,1)S(1)} %copy-done, bf16[3,1024,256]{2,1,0:T(8,128)(2,1)S(1)} %collective-permute-done.1.across, bf16[2,32,512]{2,1,0:T(8,128)(2,1)S(1)} %pad_maximum_fusion.1.rest_0_, ...), custom_call_target="tpu_custom_call" | custom-call | flops 67108864 | bytes 4194304 | tf_op jit(solution)/shard_map/parent_backward/pallas_call | solution.py:202
  21.3 2.1 %collective-permute-start.7 = (bf16[2,32,512]{2,1,0:T(8,128)(2,1)S(1)}, bf16[2,32,512]{2,1,0:T(8,128)(2,1)S(1)}, u32[]{:S(2)}, u32[]{:S(2)}) collective-permute-start(bf16[2,32,512]{2,1,0:T(8,128)(2,1)S(1)} %get-tuple-element.21.rest_0_), channel_id=1, source_target_pairs={{0,28},{1,31},{2,30},{3,29},{4,0},{5,3},{6,2},{7,1},{8,4},{9,7},{1... | collective-permute-start | bytes 196616 | tf_op jit(solution)/shard_map/ppermute | solution.py:38
  23.3 0.9 %collective-permute-start.9 = (bf16[2,32,512]{2,1,0:T(8,128)(2,1)S(1)}, bf16[2,32,512]{2,1,0:T(8,128)(2,1)S(1)}, u32[]{:S(2)}, u32[]{:S(2)}) collective-permute-start(bf16[2,32,512]{2,1,0:T(8,128)(2,1)S(1)} %get-tuple-element.21.rest_0_), channel_id=1, source_target_pairs={{0,3},{1,2},{2,1},{3,0},{4,7},{5,6},{6,5},{7,4},{8,11},{9,10},{10,... | collective-permute-start | bytes 196616 | tf_op jit(solution)/shard_map/ppermute | solution.py:38
  24.3 2.0 %collective-permute-done.7 = bf16[2,32,512]{2,1,0:T(8,128)(2,1)S(1)} collective-permute-done((bf16[2,32,512]{2,1,0:T(8,128)(2,1)S(1)}, bf16[2,32,512]{2,1,0:T(8,128)(2,1)S(1)}, u32[]{:S(2)}, u32[]{:S(2)}) %collective-permute-start.7) | collective-permute-done | bytes 65568 | tf_op jit(solution)/shard_map/ppermute | solution.py:38
  26.3 0.8 %collective-permute-done.9.rest_1_ = bf16[2,32,512]{2,1,0:T(8,128)(2,1)S(1)} collective-permute-done((bf16[2,32,512]{2,1,0:T(8,128)(2,1)S(1)}, bf16[2,32,512]{2,1,0:T(8,128)(2,1)S(1)}, u32[]{:S(2)}, u32[]{:S(2)}) %collective-permute-start.9) | collective-permute-done | bytes 65568 | tf_op jit(solution)/shard_map/ppermute | solution.py:38
  27.0 0.5 %collective-permute-done.8.theirs = bf16[1,2,32,512]{3,2,1,0:T(8,128)(2,1)S(1)} collective-permute-done((bf16[1,2,32,512]{3,2,1,0:T(8,128)(2,1)S(1)}, bf16[1,2,32,512]{3,2,1,0:T(8,128)(2,1)S(1)}, u32[]{:S(2)}, u32[]{:S(2)}) %collective-permute-start.8) | collective-permute-done | bytes 65568 | tf_op jit(solution)/shard_map/ppermute | solution.py:38
  27.5 1.6 %backward.1 = (f32[8,32,128]{2,1,0:T(8,128)}, f32[2,32,256]{2,1,0:T(8,128)}) custom-call(s32[2,8]{1,0:T(2,128)S(1)} %bitcast.14, f32[2,32,256]{2,1,0:T(8,128)S(1)} %get-tuple-element.19.full, bf16[8,32,128]{2,1,0:T(8,128)(2,1)S(1)} %get-tuple-element.20.solved, bf16[1,2,32,512]{3,2,1,0:T(8,128)(2,1)S(1)} %bitcast.12, ...), custom_call_target="tpu_custom_call" | custom-call | flops 268435456 | bytes 5242880 | tf_op jit(solution)/shard_map/backward/pallas_call | solution.py:217
  (16 shorter events, 0.1 us)
Async XLA Ops:
  0.6 3.2 %copy-start.2 = (bf16[2,1024,256]{2,1,0:T(8,128)(2,1)S(1)}, bf16[2,1024,256]{2,1,0:T(8,128)(2,1)}, u32[]{:S(2)}) copy-start(bf16[2,1024,256]{2,1,0:T(8,128)(2,1)} %lower) | copy-start | bytes 3145732
  3.3 1.2 %copy-start = (bf16[2,1024,256]{2,1,0:T(8,128)(2,1)S(1)}, bf16[2,1024,256]{2,1,0:T(8,128)(2,1)}, u32[]{:S(2)}) copy-start(bf16[2,1024,256]{2,1,0:T(8,128)(2,1)} %upper.1) | copy-start | bytes 3145732
  3.3 1.6 %collective-permute-start = (bf16[3,32,1024]{2,1,0:T(8,128)(2,1)S(1)}, bf16[3,32,1024]{2,1,0:T(8,128)(2,1)S(1)}, u32[]{:S(2)}, u32[]{:S(2)}) collective-permute-start(bf16[3,32,1024]{2,1,0:T(8,128)(2,1)S(1)} %get-tuple-element.14), channel_id=1, source_target_pairs={{0,1},{1,0},{2,3},{3,2},{4,5},{5,4},{6,7},{7,6},{8,9},{9,8},{10,11... | collective-permute-start | bytes 589832 | tf_op jit(solution)/shard_map/ppermute | solution.py:38
  4.6 11.2 %copy-start.4 = (bf16[2,32,1024]{2,1,0:T(8,128)(2,1)S(1)}, bf16[2,32,1024]{2,1,0:T(8,128)(2,1)}, u32[]{:S(2)}) copy-start(bf16[2,32,1024]{2,1,0:T(8,128)(2,1)} %rhs.1) | copy-start | bytes 393220
  4.9 10.8 %collective-permute-start.1 = (bf16[3,1024,256]{2,1,0:T(8,128)(2,1)S(1)}, bf16[3,1024,256]{2,1,0:T(8,128)(2,1)S(1)}, u32[]{:S(2)}, u32[]{:S(2)}) collective-permute-start(bf16[3,1024,256]{2,1,0:T(8,128)(2,1)S(1)} %pad_maximum_fusion), channel_id=1, source_target_pairs={{0,1},{1,0},{2,3},{3,2},{4,5},{5,4},{6,7},{7,6},{8,9},{9,8},{10,11... | collective-permute-start | bytes 4718600 | tf_op jit(solution)/shard_map/ppermute | solution.py:38
  5.3 9.0 %collective-permute-start.2 = (bf16[32,1024]{1,0:T(8,128)(2,1)S(1)}, bf16[32,1024]{1,0:T(8,128)(2,1)S(1)}, u32[]{:S(2)}, u32[]{:S(2)}) collective-permute-start(bf16[32,1024]{1,0:T(8,128)(2,1)S(1)} %get-tuple-element.24), channel_id=1, source_target_pairs={{0,7},{1,6},{2,5},{3,4},{4,11},{5,10},{6,9},{7,8},{8,15},{9,14},{1... | collective-permute-start | bytes 196616 | tf_op jit(solution)/shard_map/ppermute | solution.py:38
  9.0 6.8 %collective-permute-start.3 = (bf16[32,1024]{1,0:T(8,128)(2,1)S(1)}, bf16[32,1024]{1,0:T(8,128)(2,1)S(1)}, u32[]{:S(2)}, u32[]{:S(2)}) collective-permute-start(bf16[32,1024]{1,0:T(8,128)(2,1)S(1)} %get-tuple-element.23), channel_id=1, source_target_pairs={{0,5},{1,4},{2,7},{3,6},{4,9},{5,8},{6,11},{7,10},{8,13},{9,12},{1... | collective-permute-start | bytes 196616 | tf_op jit(solution)/shard_map/ppermute | solution.py:38
  10.2 5.5 %collective-permute-start.4 = (bf16[32,1024]{1,0:T(8,128)(2,1)S(1)}, bf16[32,1024]{1,0:T(8,128)(2,1)S(1)}, u32[]{:S(2)}, u32[]{:S(2)}) collective-permute-start(bf16[32,1024]{1,0:T(8,128)(2,1)S(1)} %get-tuple-element.22), channel_id=1, source_target_pairs={{0,3},{1,2},{2,1},{3,0},{4,7},{5,6},{6,5},{7,4},{8,11},{9,10},{10,... | collective-permute-start | bytes 196616 | tf_op jit(solution)/shard_map/ppermute | solution.py:38
  15.8 11.7 %copy-start.1 = (bf16[8,2,1024,128]{3,2,1,0:T(8,128)(2,1)S(1)}, bf16[8,2,1024,128]{3,2,1,0:T(8,128)(2,1)}, u32[]{:S(2)}) copy-start(bf16[8,2,1024,128]{3,2,1,0:T(8,128)(2,1)} %blocks.1) | copy-start | bytes 12582916
  16.1 11.5 %copy-start.3 = (bf16[8,128,128]{2,1,0:T(8,128)(2,1)S(1)}, bf16[8,128,128]{2,1,0:T(8,128)(2,1)}, u32[]{:S(2)}) copy-start(bf16[8,128,128]{2,1,0:T(8,128)(2,1)} %upper.2) | copy-start | bytes 786436
  16.1 11.5 %copy-start.5 = (s32[8,2]{0,1:T(2,128)S(1)}, s32[8,2]{0,1:T(2,128)}, u32[]{:S(2)}) copy-start(s32[8,2]{0,1:T(2,128)} %param.17) | copy-start | bytes 196
  16.1 3.4 %collective-permute-start.5 = (bf16[32,512]{1,0:T(8,128)(2,1)S(1)}, bf16[32,512]{1,0:T(8,128)(2,1)S(1)}, u32[]{:S(2)}, u32[]{:S(2)}) collective-permute-start(bf16[32,512]{1,0:T(8,128)(2,1)S(1)} %parent_forward.1), channel_id=1, source_target_pairs={{0,3},{1,2},{2,1},{3,0},{4,7},{5,6},{6,5},{7,4},{8,11},{9,10},{10,... | collective-permute-start | bytes 98312 | tf_op jit(solution)/shard_map/ppermute | solution.py:38
  19.5 1.3 %collective-permute-start.6 = (bf16[2,32,512]{2,1,0:T(8,128)(2,1)S(1)}, bf16[2,32,512]{2,1,0:T(8,128)(2,1)S(1)}, u32[]{:S(2)}, u32[]{:S(2)}) collective-permute-start(bf16[2,32,512]{2,1,0:T(8,128)(2,1)S(1)} %pad_maximum_fusion.1.rest_0_), channel_id=1, source_target_pairs={{0,1},{1,0},{2,3},{3,2},{4,5},{5,4},{6,7},{7,6},{8,9},{9,8},{10,11... | collective-permute-start | bytes 196616 | tf_op jit(solution)/shard_map/ppermute | solution.py:38
  21.3 5.0 %collective-permute-start.7 = (bf16[2,32,512]{2,1,0:T(8,128)(2,1)S(1)}, bf16[2,32,512]{2,1,0:T(8,128)(2,1)S(1)}, u32[]{:S(2)}, u32[]{:S(2)}) collective-permute-start(bf16[2,32,512]{2,1,0:T(8,128)(2,1)S(1)} %get-tuple-element.21.rest_0_), channel_id=1, source_target_pairs={{0,28},{1,31},{2,30},{3,29},{4,0},{5,3},{6,2},{7,1},{8,4},{9,7},{1... | collective-permute-start | bytes 196616 | tf_op jit(solution)/shard_map/ppermute | solution.py:38
  23.3 3.7 %collective-permute-start.9 = (bf16[2,32,512]{2,1,0:T(8,128)(2,1)S(1)}, bf16[2,32,512]{2,1,0:T(8,128)(2,1)S(1)}, u32[]{:S(2)}, u32[]{:S(2)}) collective-permute-start(bf16[2,32,512]{2,1,0:T(8,128)(2,1)S(1)} %get-tuple-element.21.rest_0_), channel_id=1, source_target_pairs={{0,3},{1,2},{2,1},{3,0},{4,7},{5,6},{6,5},{7,4},{8,11},{9,10},{10,... | collective-permute-start | bytes 196616 | tf_op jit(solution)/shard_map/ppermute | solution.py:38
  26.3 1.3 %collective-permute-start.8 = (bf16[1,2,32,512]{3,2,1,0:T(8,128)(2,1)S(1)}, bf16[1,2,32,512]{3,2,1,0:T(8,128)(2,1)S(1)}, u32[]{:S(2)}, u32[]{:S(2)}) collective-permute-start(bf16[1,2,32,512]{3,2,1,0:T(8,128)(2,1)S(1)} %bitcast.11), channel_id=1, source_target_pairs={{0,1},{1,0},{2,3},{3,2},{4,5},{5,4},{6,7},{7,6},{8,9},{9,8},{10,11... | collective-permute-start | bytes 196616 | tf_op jit(solution)/shard_map/ppermute | solution.py:38

commit v6 on v5

--- a/solution.py
+++ b/solution.py
@@ -62,7 +62,7 @@
     copies = [pltpu.make_async_copy(blocks_hbm.at[a], blocks.at[a], sems.at[3 + a]) for a in range(leaves)]
     for copy in first + copies:
         copy.start()
-    windows = (parent, 2 + parent, 3 - parent, 1 - parent)
+    windows = (parent, 3 - parent, 1 - parent, 2 + parent)
     for copy in first:
         copy.wait()
     solved = [dot(rhs[a], lower[a]).astype(BF16) for a in range(leaves)]
@@ -86,15 +86,15 @@
             acc[...] += part
         else:
             total = acc[...] + part
-            keep_ref[...] = total[: 3 * nrhs].reshape(3, nrhs, wide)
-            give_ref[...] = total[nrhs:].astype(BF16).reshape(3, nrhs, wide)
+            keep_ref[...] = total[: 2 * nrhs].reshape(2, nrhs, wide)
+            give_ref[...] = total[2 * nrhs :].astype(BF16).reshape(2, nrhs, wide)
 
 
 def parent_forward_kernel(keep, came, rhs, lower, across, *rest):
     sums, half_ref = rest[:-1], rest[-1]
     _, core, parent = place()
     cut = lower.shape[2]
-    update = keep[0] + came[2].astype(F32)
+    update = keep[0] + came[0].astype(F32)
     for term in sums:
         update = update + term[...].astype(F32)
     combined = (rhs[parent].astype(F32) - update).astype(BF16)
@@ -102,20 +102,33 @@
     half_ref[:, columns(1 - core, cut)] = dot(combined, across[0]).astype(BF16)
 
 
-def parent_backward_kernel(upper, across, *rest):
-    mine, theirs, parent_ref, half_ref, forward = rest
-    chips = mine.shape[0]
+def through_upper(forward, of, source, depth, upper, across):
+    rows = pl.ds(pl.multiple_of(source * depth, depth), depth)
+    return dot(forward, upper[of, rows, :]), dot(forward, across[1 + of, rows, :])
+
+
+def parent_early_kernel(mine, theirs, upper, across, part_ref):
     chip, core, parent = place()
     cut = upper.shape[2]
-    for by in range(chips):
-        at = columns(lax.rem(chip + chips - by, chips), mine.shape[2])
-        forward[parent, :, at] = mine[by]
-        forward[1 - parent, :, at] = theirs[by]
-    for this in range(CORES):
-        part = dot(forward[this], upper[this])
-        parent_ref[this] = part
-        half_ref[this, :, columns(core, cut)] = part.astype(BF16)
-        half_ref[this, :, columns(1 - core, cut)] = dot(forward[this], across[1 + this]).astype(BF16)
+    for of, forward in ((parent, mine), (1 - parent, theirs)):
+        here, there = through_upper(forward[...], of, chip, forward.shape[1], upper, across)
+        part_ref[of, :, columns(core, cut)] = here
+        part_ref[of, :, columns(1 - core, cut)] = there
+
+
+def parent_backward_kernel(part, mine, theirs, upper, across, parent_ref, half_ref):
+    chip, core, parent = place()
+    cut = upper.shape[2]
+    moved, _, depth = mine.shape
+    for of, arrived in ((parent, mine), (1 - parent, theirs)):
+        here, there = part[of, :, columns(core, cut)], part[of, :, columns(1 - core, cut)]
+        for by in range(1, moved + 1):
+            source = lax.rem(chip + moved + 1 - by, moved + 1)
+            more_here, more_there = through_upper(arrived[by - 1], of, source, depth, upper, across)
+            here, there = here + more_here, there + more_there
+        parent_ref[of] = here
+        half_ref[of, :, columns(core, cut)] = here.astype(BF16)
+        half_ref[of, :, columns(1 - core, cut)] = there.astype(BF16)
 
 
 def backward_kernel(targets, full, solved, mine, theirs, blocks, upper, *rest):
@@ -158,8 +171,8 @@
         out_specs=[VMEM] * 3,
         out_shape=[
             jax.ShapeDtypeStruct((leaves, nrhs, width), BF16),
-            jax.ShapeDtypeStruct((3, nrhs, wide), F32),
-            jax.ShapeDtypeStruct((3, nrhs, wide), BF16),
+            jax.ShapeDtypeStruct((2, nrhs, wide), F32),
+            jax.ShapeDtypeStruct((2, nrhs, wide), BF16),
         ],
         scratch_shapes=[
             pltpu.SMEM(listed.shape, jnp.int32),
@@ -180,11 +193,9 @@
     across = jnp.concatenate([lax.dynamic_index_in_dim(lower, 1 - parent, 0), upper])
     came, across = lax.optimization_barrier((came, across))
     across = go(across, by_row=0, target=along(0, 1))
-    own_sum = (keep[0] + came[2].astype(F32)).astype(BF16)
-    next_sums = [(keep[1] + came[1].astype(F32)).astype(BF16), (keep[2] + came[0].astype(F32)).astype(BF16)]
-    sums = [
-        go(next_sums[(by + 1) % CORES], by_row=1, target=along(by, (by + 1) % CORES)) for by in reversed(range(chips))
-    ]
+    own_sum = (keep[0] + came[0].astype(F32)).astype(BF16)
+    next_sum = (keep[1] + came[1].astype(F32)).astype(BF16)
+    sums = [go(next_sum, by_row=1, target=along(by, 1)) for by in reversed(range(chips))]
     sums += [go(own_sum, by_row=0, target=along(by)) for by in range(1, chips)]
 
     half = pl.pallas_call(
@@ -196,19 +207,28 @@
         cost_estimate=pl.CostEstimate(flops=1 << 25, bytes_accessed=2 << 20, transcendentals=0),
         name="parent_forward",
     )(keep, came, parent_rhs, lower, across, *sums)
-    halves = jnp.stack([half] + [go(half, by_row=0, target=along(by)) for by in range(1, chips)])
-    halves = (halves, go(halves, by_row=0, target=along(0, 1)))
+    mine = jnp.stack([go(half, by_row=0, target=along(by)) for by in range(1, chips)])
+    other_half = go(half, by_row=0, target=along(0, 1))
+    part = pl.pallas_call(
+        parent_early_kernel,
+        in_specs=[VMEM] * 4,
+        out_specs=VMEM,
+        out_shape=jax.ShapeDtypeStruct((2, nrhs, depth), F32),
+        compiler_params=pltpu.CompilerParams(vmem_limit_bytes=16 << 20),
+        cost_estimate=pl.CostEstimate(flops=1 << 26, bytes_accessed=2 << 20, transcendentals=0),
+        name="parent_early",
+    )(half, other_half, upper, across)
+    theirs = go(mine, by_row=0, target=along(0, 1))
 
     full, half = pl.pallas_call(
         parent_backward_kernel,
-        in_specs=[VMEM] * (2 + len(halves)),
+        in_specs=[VMEM] * 5,
         out_specs=[VMEM, VMEM],
         out_shape=[jax.ShapeDtypeStruct((2, nrhs, cut), F32), jax.ShapeDtypeStruct((2, nrhs, depth), BF16)],
-        scratch_shapes=[pltpu.VMEM((2, nrhs, wide), BF16)],
         compiler_params=pltpu.CompilerParams(vmem_limit_bytes=16 << 20),
-        cost_estimate=pl.CostEstimate(flops=1 << 26, bytes_accessed=4 << 20, transcendentals=0),
+        cost_estimate=pl.CostEstimate(flops=1 << 26, bytes_accessed=2 << 20, transcendentals=0),
         name="parent_backward",
-    )(upper, across, *halves)
+    )(part, mine, theirs, upper, across)
 
     halves = [half] + [go(half, by_row=0, target=along(by, (by + 1) % CORES)) for by in range(1, chips)]
     mine = jnp.stack([go(half, by_row=-1, target=fan(by)) for by in range(0, chips, CORES)])

time: 29.3 us -> 29 us (0.990)
  waiting for transfers between devices: 11.8 us -> 11.3 us
    ppermute x10 -> x11, waiting for transfers between devices: 11.8 us -> 11.3 us  [send(): return lax.ppermute(array, ('row', 'col'), pairs)]
    ppermute x10 -> x11, starting transfers between devices: 10.7 us -> 10.8 us  [send(): return lax.ppermute(array, ('row', 'col'), pairs)]
  transfers between devices with their start and end apart: 10 -> 11, of which waited for: 8 -> 8; matrix products, arithmetic and copies ran while one was open for 1% -> 1% of each run, Pallas kernels for 0% -> 1%
where the time goes in v6:
time: 29 us; the launch traced here: 28.9 us
  waiting for transfers between devices  11.3 us (39%)
  starting transfers between devices  10.8 us (37%)
  Pallas kernels  5.09 us (18%)
  local copies, waits for them, and re-layouts  0.72 us (2%)
  between operations  0.71 us (2%)
    ppermute x11, waiting for transfers between devices, send(): return lax.ppermute(array, ('row', 'col'), pairs)  11.3 us
    ppermute x11, starting transfers between devices, send(): return lax.ppermute(array, ('row', 'col'), pairs)  10.8 us
    pallas_call x1, Pallas kernels, local(): pl.pallas_call(forward_kernel, in_specs=[HBM] * 4, out_specs=[VMEM] * 3,...  2.68 us
    pallas_call x1, Pallas kernels, local(): pl.pallas_call(backward_kernel, in_specs=[VMEM] * (7 + chips), out_specs=...  1.58 us
    unnamed x12, local copies, waits for them, and re-layouts  0.68 us
  transfers between devices with their start and end apart: 11, of which 8 were waited for; matrix products, arithmetic and copies ran while one was open for 1% of the time, Pallas kernels for 1%

profile of v6, /device:TPU:0, one launch (start us, length us, event | category | flops | bytes accessed | tf_op | source)
XLA Modules:
  0.0 28.9 jit_solution(5906330631986216609)
XLA Ops:
  0.6 2.7 %forward.1 = (bf16[8,32,128]{2,1,0:T(8,128)(2,1)S(1)}, f32[2,32,1024]{2,1,0:T(8,128)S(1)}, bf16[2,32,1024]{2,1,0:T(8,128)(2,1)S(1)}) custom-call(s32[2,8]{1,0:T(2,128)} %bitcast.11, bf16[8,32,128]{2,1,0:T(8,128)(2,1)} %rhs_hbm.1, bf16[8,128,128]{2,1,0:T(8,128)(2,1)} %lower_hbm.1, bf16[8,2,128,1024]{3,2,1,0:T(8,128)(2,1)} %blocks_hbm.1), custom_call_target="tpu_custom_call" | custom-call | flops 536870912 | bytes 5242880 | tf_op jit(solution)/shard_map/forward/pallas_call | solution.py:168
  3.3 0.5 %collective-permute-start = (bf16[2,32,1024]{2,1,0:T(8,128)(2,1)S(1)}, bf16[2,32,1024]{2,1,0:T(8,128)(2,1)S(1)}, u32[]{:S(2)}, u32[]{:S(2)}) collective-permute-start(bf16[2,32,1024]{2,1,0:T(8,128)(2,1)S(1)} %get-tuple-element.14), channel_id=1, source_target_pairs={{0,1},{1,0},{2,3},{3,2},{4,5},{5,4},{6,7},{7,6},{8,9},{9,8},{10,11... | collective-permute-start | bytes 393224 | tf_op jit(solution)/shard_map/ppermute | solution.py:38
  3.9 0.7 %copy-done = bf16[2,1024,256]{2,1,0:T(8,128)(2,1)S(1)} copy-done((bf16[2,1024,256]{2,1,0:T(8,128)(2,1)S(1)}, bf16[2,1024,256]{2,1,0:T(8,128)(2,1)}, u32[]{:S(2)}) %copy-start) | copy-done | bytes 1048600
  4.6 0.1 pad_maximum_fusion
  4.7 0.1 collective-permute-done.came
  4.8 0.4 %collective-permute-start.1 = (bf16[3,1024,256]{2,1,0:T(8,128)(2,1)S(1)}, bf16[3,1024,256]{2,1,0:T(8,128)(2,1)S(1)}, u32[]{:S(2)}, u32[]{:S(2)}) collective-permute-start(bf16[3,1024,256]{2,1,0:T(8,128)(2,1)S(1)} %pad_maximum_fusion), channel_id=1, source_target_pairs={{0,1},{1,0},{2,3},{3,2},{4,5},{5,4},{6,7},{7,6},{8,9},{9,8},{10,11... | collective-permute-start | bytes 4718600 | tf_op jit(solution)/shard_map/ppermute | solution.py:38
  5.3 3.6 %collective-permute-start.2 = (bf16[32,1024]{1,0:T(8,128)(2,1)S(1)}, bf16[32,1024]{1,0:T(8,128)(2,1)S(1)}, u32[]{:S(2)}, u32[]{:S(2)}) collective-permute-start(bf16[32,1024]{1,0:T(8,128)(2,1)S(1)} %get-tuple-element.23), channel_id=1, source_target_pairs={{0,6},{1,7},{2,4},{3,5},{4,10},{5,11},{6,8},{7,9},{8,14},{9,15},{1... | collective-permute-start | bytes 196616 | tf_op jit(solution)/shard_map/ppermute | solution.py:38
  8.9 1.2 %collective-permute-start.3 = (bf16[32,1024]{1,0:T(8,128)(2,1)S(1)}, bf16[32,1024]{1,0:T(8,128)(2,1)S(1)}, u32[]{:S(2)}, u32[]{:S(2)}) collective-permute-start(bf16[32,1024]{1,0:T(8,128)(2,1)S(1)} %get-tuple-element.23), channel_id=1, source_target_pairs={{0,5},{1,4},{2,7},{3,6},{4,9},{5,8},{6,11},{7,10},{8,13},{9,12},{1... | collective-permute-start | bytes 196616 | tf_op jit(solution)/shard_map/ppermute | solution.py:38
  10.1 0.6 %collective-permute-start.4 = (bf16[32,1024]{1,0:T(8,128)(2,1)S(1)}, bf16[32,1024]{1,0:T(8,128)(2,1)S(1)}, u32[]{:S(2)}, u32[]{:S(2)}) collective-permute-start(bf16[32,1024]{1,0:T(8,128)(2,1)S(1)} %get-tuple-element.22), channel_id=1, source_target_pairs={{0,3},{1,2},{2,1},{3,0},{4,7},{5,6},{6,5},{7,4},{8,11},{9,10},{10,... | collective-permute-start | bytes 196616 | tf_op jit(solution)/shard_map/ppermute | solution.py:38
  10.7 3.9 %collective-permute-done.2.rest_0_ = bf16[32,1024]{1,0:T(8,128)(2,1)S(1)} collective-permute-done((bf16[32,1024]{1,0:T(8,128)(2,1)S(1)}, bf16[32,1024]{1,0:T(8,128)(2,1)S(1)}, u32[]{:S(2)}, u32[]{:S(2)}) %collective-permute-start.2) | collective-permute-done | bytes 65568 | tf_op jit(solution)/shard_map/ppermute | solution.py:38
  14.6 1.1 %collective-permute-done.3.rest_1_ = bf16[32,1024]{1,0:T(8,128)(2,1)S(1)} collective-permute-done((bf16[32,1024]{1,0:T(8,128)(2,1)S(1)}, bf16[32,1024]{1,0:T(8,128)(2,1)S(1)}, u32[]{:S(2)}, u32[]{:S(2)}) %collective-permute-start.3) | collective-permute-done | bytes 65568 | tf_op jit(solution)/shard_map/ppermute | solution.py:38
  15.8 0.3 parent_forward.1.mine
  16.0 1.1 %collective-permute-start.6 = (bf16[32,512]{1,0:T(8,128)(2,1)S(1)}, bf16[32,512]{1,0:T(8,128)(2,1)S(1)}, u32[]{:S(2)}, u32[]{:S(2)}) collective-permute-start(bf16[32,512]{1,0:T(8,128)(2,1)S(1)} %parent_forward.1.mine), channel_id=1, source_target_pairs={{0,3},{1,2},{2,1},{3,0},{4,7},{5,6},{6,5},{7,4},{8,11},{9,10},{10,... | collective-permute-start | bytes 98312 | tf_op jit(solution)/shard_map/ppermute | solution.py:38
  17.1 0.4 %collective-permute-start.5 = (bf16[32,512]{1,0:T(8,128)(2,1)S(1)}, bf16[32,512]{1,0:T(8,128)(2,1)S(1)}, u32[]{:S(2)}, u32[]{:S(2)}) collective-permute-start(bf16[32,512]{1,0:T(8,128)(2,1)S(1)} %parent_forward.1.mine), channel_id=1, source_target_pairs={{0,1},{1,0},{2,3},{3,2},{4,5},{5,4},{6,7},{7,6},{8,9},{9,8},{10,11... | collective-permute-start | bytes 98312 | tf_op jit(solution)/shard_map/ppermute | solution.py:38
  17.6 2.0 %collective-permute-done.6 = bf16[32,512]{1,0:T(8,128)(2,1)S(1)} collective-permute-done((bf16[32,512]{1,0:T(8,128)(2,1)S(1)}, bf16[32,512]{1,0:T(8,128)(2,1)S(1)}, u32[]{:S(2)}, u32[]{:S(2)}) %collective-permute-start.6) | collective-permute-done | bytes 32800 | tf_op jit(solution)/shard_map/ppermute | solution.py:38
  19.6 0.3 parent_early.1.part
  19.9 0.8 %collective-permute-done.7.theirs = bf16[1,32,512]{2,1,0:T(8,128)(2,1)S(1)} collective-permute-done((bf16[1,32,512]{2,1,0:T(8,128)(2,1)S(1)}, bf16[1,32,512]{2,1,0:T(8,128)(2,1)S(1)}, u32[]{:S(2)}, u32[]{:S(2)}) %collective-permute-start.7) | collective-permute-done | bytes 32800 | tf_op jit(solution)/shard_map/ppermute | solution.py:38
  20.7 0.3 parent_backward.1
  21.0 1.9 %collective-permute-start.8 = (bf16[2,32,512]{2,1,0:T(8,128)(2,1)S(1)}, bf16[2,32,512]{2,1,0:T(8,128)(2,1)S(1)}, u32[]{:S(2)}, u32[]{:S(2)}) collective-permute-start(bf16[2,32,512]{2,1,0:T(8,128)(2,1)S(1)} %get-tuple-element.21.rest_0_), channel_id=1, source_target_pairs={{0,28},{1,31},{2,30},{3,29},{4,0},{5,3},{6,2},{7,1},{8,4},{9,7},{1... | collective-permute-start | bytes 196616 | tf_op jit(solution)/shard_map/ppermute | solution.py:38
  22.9 0.9 %collective-permute-start.10 = (bf16[2,32,512]{2,1,0:T(8,128)(2,1)S(1)}, bf16[2,32,512]{2,1,0:T(8,128)(2,1)S(1)}, u32[]{:S(2)}, u32[]{:S(2)}) collective-permute-start(bf16[2,32,512]{2,1,0:T(8,128)(2,1)S(1)} %get-tuple-element.21.rest_0_), channel_id=1, source_target_pairs={{0,3},{1,2},{2,1},{3,0},{4,7},{5,6},{6,5},{7,4},{8,11},{9,10},{10,... | collective-permute-start | bytes 196616 | tf_op jit(solution)/shard_map/ppermute | solution.py:38
  23.9 2.1 %collective-permute-done.8 = bf16[2,32,512]{2,1,0:T(8,128)(2,1)S(1)} collective-permute-done((bf16[2,32,512]{2,1,0:T(8,128)(2,1)S(1)}, bf16[2,32,512]{2,1,0:T(8,128)(2,1)S(1)}, u32[]{:S(2)}, u32[]{:S(2)}) %collective-permute-start.8) | collective-permute-done | bytes 65568 | tf_op jit(solution)/shard_map/ppermute | solution.py:38
  26.0 0.6 %collective-permute-done.10.rest_1_ = bf16[2,32,512]{2,1,0:T(8,128)(2,1)S(1)} collective-permute-done((bf16[2,32,512]{2,1,0:T(8,128)(2,1)S(1)}, bf16[2,32,512]{2,1,0:T(8,128)(2,1)S(1)}, u32[]{:S(2)}, u32[]{:S(2)}) %collective-permute-start.10) | collective-permute-done | bytes 65568 | tf_op jit(solution)/shard_map/ppermute | solution.py:38
  26.6 0.7 %collective-permute-done.9.theirs = bf16[1,2,32,512]{3,2,1,0:T(8,128)(2,1)S(1)} collective-permute-done((bf16[1,2,32,512]{3,2,1,0:T(8,128)(2,1)S(1)}, bf16[1,2,32,512]{3,2,1,0:T(8,128)(2,1)S(1)}, u32[]{:S(2)}, u32[]{:S(2)}) %collective-permute-start.9) | collective-permute-done | bytes 65568 | tf_op jit(solution)/shard_map/ppermute | solution.py:38
  27.3 1.6 %backward.1 = (f32[8,32,128]{2,1,0:T(8,128)}, f32[2,32,256]{2,1,0:T(8,128)}) custom-call(s32[2,8]{1,0:T(2,128)S(1)} %bitcast.12, f32[2,32,256]{2,1,0:T(8,128)S(1)} %get-tuple-element.19.full, bf16[8,32,128]{2,1,0:T(8,128)(2,1)S(1)} %get-tuple-element.20.solved, bf16[1,2,32,512]{3,2,1,0:T(8,128)(2,1)S(1)} %bitcast.8, ...), custom_call_target="tpu_custom_call" | custom-call | flops 268435456 | bytes 5242880 | tf_op jit(solution)/shard_map/backward/pallas_call | solution.py:237
  (18 shorter events, 0.2 us)
Async XLA Ops:
  0.6 3.2 %copy-start.2 = (bf16[2,1024,256]{2,1,0:T(8,128)(2,1)S(1)}, bf16[2,1024,256]{2,1,0:T(8,128)(2,1)}, u32[]{:S(2)}) copy-start(bf16[2,1024,256]{2,1,0:T(8,128)(2,1)} %lower) | copy-start | bytes 3145732
  3.3 1.2 %copy-start = (bf16[2,1024,256]{2,1,0:T(8,128)(2,1)S(1)}, bf16[2,1024,256]{2,1,0:T(8,128)(2,1)}, u32[]{:S(2)}) copy-start(bf16[2,1024,256]{2,1,0:T(8,128)(2,1)} %upper.2) | copy-start | bytes 3145732
  3.3 1.5 %collective-permute-start = (bf16[2,32,1024]{2,1,0:T(8,128)(2,1)S(1)}, bf16[2,32,1024]{2,1,0:T(8,128)(2,1)S(1)}, u32[]{:S(2)}, u32[]{:S(2)}) collective-permute-start(bf16[2,32,1024]{2,1,0:T(8,128)(2,1)S(1)} %get-tuple-element.14), channel_id=1, source_target_pairs={{0,1},{1,0},{2,3},{3,2},{4,5},{5,4},{6,7},{7,6},{8,9},{9,8},{10,11... | collective-permute-start | bytes 393224 | tf_op jit(solution)/shard_map/ppermute | solution.py:38
  4.6 11.2 %copy-start.4 = (bf16[2,32,1024]{2,1,0:T(8,128)(2,1)S(1)}, bf16[2,32,1024]{2,1,0:T(8,128)(2,1)}, u32[]{:S(2)}) copy-start(bf16[2,32,1024]{2,1,0:T(8,128)(2,1)} %rhs.1) | copy-start | bytes 393220
  4.8 10.9 %collective-permute-start.1 = (bf16[3,1024,256]{2,1,0:T(8,128)(2,1)S(1)}, bf16[3,1024,256]{2,1,0:T(8,128)(2,1)S(1)}, u32[]{:S(2)}, u32[]{:S(2)}) collective-permute-start(bf16[3,1024,256]{2,1,0:T(8,128)(2,1)S(1)} %pad_maximum_fusion), channel_id=1, source_target_pairs={{0,1},{1,0},{2,3},{3,2},{4,5},{5,4},{6,7},{7,6},{8,9},{9,8},{10,11... | collective-permute-start | bytes 4718600 | tf_op jit(solution)/shard_map/ppermute | solution.py:38
  5.3 9.4 %collective-permute-start.2 = (bf16[32,1024]{1,0:T(8,128)(2,1)S(1)}, bf16[32,1024]{1,0:T(8,128)(2,1)S(1)}, u32[]{:S(2)}, u32[]{:S(2)}) collective-permute-start(bf16[32,1024]{1,0:T(8,128)(2,1)S(1)} %get-tuple-element.23), channel_id=1, source_target_pairs={{0,6},{1,7},{2,4},{3,5},{4,10},{5,11},{6,8},{7,9},{8,14},{9,15},{1... | collective-permute-start | bytes 196616 | tf_op jit(solution)/shard_map/ppermute | solution.py:38
  8.9 6.8 %collective-permute-start.3 = (bf16[32,1024]{1,0:T(8,128)(2,1)S(1)}, bf16[32,1024]{1,0:T(8,128)(2,1)S(1)}, u32[]{:S(2)}, u32[]{:S(2)}) collective-permute-start(bf16[32,1024]{1,0:T(8,128)(2,1)S(1)} %get-tuple-element.23), channel_id=1, source_target_pairs={{0,5},{1,4},{2,7},{3,6},{4,9},{5,8},{6,11},{7,10},{8,13},{9,12},{1... | collective-permute-start | bytes 196616 | tf_op jit(solution)/shard_map/ppermute | solution.py:38
  10.1 5.6 %collective-permute-start.4 = (bf16[32,1024]{1,0:T(8,128)(2,1)S(1)}, bf16[32,1024]{1,0:T(8,128)(2,1)S(1)}, u32[]{:S(2)}, u32[]{:S(2)}) collective-permute-start(bf16[32,1024]{1,0:T(8,128)(2,1)S(1)} %get-tuple-element.22), channel_id=1, source_target_pairs={{0,3},{1,2},{2,1},{3,0},{4,7},{5,6},{6,5},{7,4},{8,11},{9,10},{10,... | collective-permute-start | bytes 196616 | tf_op jit(solution)/shard_map/ppermute | solution.py:38
  16.0 3.5 %collective-permute-start.6 = (bf16[32,512]{1,0:T(8,128)(2,1)S(1)}, bf16[32,512]{1,0:T(8,128)(2,1)S(1)}, u32[]{:S(2)}, u32[]{:S(2)}) collective-permute-start(bf16[32,512]{1,0:T(8,128)(2,1)S(1)} %parent_forward.1.mine), channel_id=1, source_target_pairs={{0,3},{1,2},{2,1},{3,0},{4,7},{5,6},{6,5},{7,4},{8,11},{9,10},{10,... | collective-permute-start | bytes 98312 | tf_op jit(solution)/shard_map/ppermute | solution.py:38
  17.1 2.5 %collective-permute-start.5 = (bf16[32,512]{1,0:T(8,128)(2,1)S(1)}, bf16[32,512]{1,0:T(8,128)(2,1)S(1)}, u32[]{:S(2)}, u32[]{:S(2)}) collective-permute-start(bf16[32,512]{1,0:T(8,128)(2,1)S(1)} %parent_forward.1.mine), channel_id=1, source_target_pairs={{0,1},{1,0},{2,3},{3,2},{4,5},{5,4},{6,7},{7,6},{8,9},{9,8},{10,11... | collective-permute-start | bytes 98312 | tf_op jit(solution)/shard_map/ppermute | solution.py:38
  19.5 1.2 %collective-permute-start.7 = (bf16[1,32,512]{2,1,0:T(8,128)(2,1)S(1)}, bf16[1,32,512]{2,1,0:T(8,128)(2,1)S(1)}, u32[]{:S(2)}, u32[]{:S(2)}) collective-permute-start(bf16[1,32,512]{2,1,0:T(8,128)(2,1)S(1)} %bitcast.9), channel_id=1, source_target_pairs={{0,1},{1,0},{2,3},{3,2},{4,5},{5,4},{6,7},{7,6},{8,9},{9,8},{10,11... | collective-permute-start | bytes 98312 | tf_op jit(solution)/shard_map/ppermute | solution.py:38
  19.6 7.7 %copy-start.1 = (bf16[8,2,1024,128]{3,2,1,0:T(8,128)(2,1)S(1)}, bf16[8,2,1024,128]{3,2,1,0:T(8,128)(2,1)}, u32[]{:S(2)}) copy-start(bf16[8,2,1024,128]{3,2,1,0:T(8,128)(2,1)} %blocks.1) | copy-start | bytes 12582916
  19.9 7.4 %copy-start.3 = (bf16[8,128,128]{2,1,0:T(8,128)(2,1)S(1)}, bf16[8,128,128]{2,1,0:T(8,128)(2,1)}, u32[]{:S(2)}) copy-start(bf16[8,128,128]{2,1,0:T(8,128)(2,1)} %upper.3) | copy-start | bytes 786436
  19.9 7.4 %copy-start.5 = (s32[8,2]{0,1:T(2,128)S(1)}, s32[8,2]{0,1:T(2,128)}, u32[]{:S(2)}) copy-start(s32[8,2]{0,1:T(2,128)} %param.17) | copy-start | bytes 196
  21.0 5.0 %collective-permute-start.8 = (bf16[2,32,512]{2,1,0:T(8,128)(2,1)S(1)}, bf16[2,32,512]{2,1,0:T(8,128)(2,1)S(1)}, u32[]{:S(2)}, u32[]{:S(2)}) collective-permute-start(bf16[2,32,512]{2,1,0:T(8,128)(2,1)S(1)} %get-tuple-element.21.rest_0_), channel_id=1, source_target_pairs={{0,28},{1,31},{2,30},{3,29},{4,0},{5,3},{6,2},{7,1},{8,4},{9,7},{1... | collective-permute-start | bytes 196616 | tf_op jit(solution)/shard_map/ppermute | solution.py:38
  22.9 3.7 %collective-permute-start.10 = (bf16[2,32,512]{2,1,0:T(8,128)(2,1)S(1)}, bf16[2,32,512]{2,1,0:T(8,128)(2,1)S(1)}, u32[]{:S(2)}, u32[]{:S(2)}) collective-permute-start(bf16[2,32,512]{2,1,0:T(8,128)(2,1)S(1)} %get-tuple-element.21.rest_0_), channel_id=1, source_target_pairs={{0,3},{1,2},{2,1},{3,0},{4,7},{5,6},{6,5},{7,4},{8,11},{9,10},{10,... | collective-permute-start | bytes 196616 | tf_op jit(solution)/shard_map/ppermute | solution.py:38
  26.0 1.3 %collective-permute-start.9 = (bf16[1,2,32,512]{3,2,1,0:T(8,128)(2,1)S(1)}, bf16[1,2,32,512]{3,2,1,0:T(8,128)(2,1)S(1)}, u32[]{:S(2)}, u32[]{:S(2)}) collective-permute-start(bf16[1,2,32,512]{3,2,1,0:T(8,128)(2,1)S(1)} %bitcast.7), channel_id=1, source_target_pairs={{0,1},{1,0},{2,3},{3,2},{4,5},{5,4},{6,7},{7,6},{8,9},{9,8},{10,11... | collective-permute-start | bytes 196616 | tf_op jit(solution)/shard_map/ppermute | solution.py:38

commit v7 on v6

--- a/solution.py
+++ b/solution.py
@@ -43,7 +43,7 @@
 
 
 def fan(by):
-    return lambda chip, core: (chip + by + core, core)
+    return lambda chip, core: (chip + by + core, 1 - core)
 
 
 def columns(index, size):
@@ -141,7 +141,7 @@
     for by, half in enumerate(halves):
         window[pl.ds(0, 2), :, columns(lax.rem(chip + chips - by, chips), depth)] = half[...]
     for by in range(0, chips, CORES):
-        for arrived, lag in ((mine, core), (theirs, 1 - core)):
+        for arrived, lag in ((mine, 1 - core), (theirs, core)):
             at = columns(lax.rem(chip + chips - by - lag, chips), depth)
             window[pl.ds(2, 2), :, at] = arrived[by // CORES]
     listed = targets[...]

time: 29 us -> 28.9 us (level)
  waiting for transfers between devices: 11.3 us -> 10.7 us
  starting transfers between devices: 10.8 us -> 11.3 us
    ppermute x11, waiting for transfers between devices: 11.3 us -> 10.7 us  [send(): return lax.ppermute(array, ('row', 'col'), pairs)]
    ppermute x11, starting transfers between devices: 10.8 us -> 11.3 us  [send(): return lax.ppermute(array, ('row', 'col'), pairs)]
where the time goes in v7:
time: 28.9 us; the launch traced here: 28.6 us
  starting transfers between devices  11.3 us (39%)
  waiting for transfers between devices  10.7 us (37%)
  Pallas kernels  5.09 us (18%)
  local copies, waits for them, and re-layouts  0.72 us (2%)
  between operations  0.71 us (2%)
    ppermute x11, starting transfers between devices, send(): return lax.ppermute(array, ('row', 'col'), pairs)  11.3 us
    ppermute x11, waiting for transfers between devices, send(): return lax.ppermute(array, ('row', 'col'), pairs)  10.7 us
    pallas_call x1, Pallas kernels, local(): pl.pallas_call(forward_kernel, in_specs=[HBM] * 4, out_specs=[VMEM] * 3,...  2.68 us
    pallas_call x1, Pallas kernels, local(): pl.pallas_call(backward_kernel, in_specs=[VMEM] * (7 + chips), out_specs=...  1.58 us
    unnamed x12, local copies, waits for them, and re-layouts  0.68 us
  transfers between devices with their start and end apart: 11, of which 8 were waited for; matrix products, arithmetic and copies ran while one was open for 1% of the time, Pallas kernels for 1%

profile of v7, /device:TPU:0, one launch (start us, length us, event | category | flops | bytes accessed | tf_op | source)
XLA Modules:
  0.0 28.6 jit_solution(7134005743933184720)
XLA Ops:
  0.6 2.7 %forward.1 = (bf16[8,32,128]{2,1,0:T(8,128)(2,1)S(1)}, f32[2,32,1024]{2,1,0:T(8,128)S(1)}, bf16[2,32,1024]{2,1,0:T(8,128)(2,1)S(1)}) custom-call(s32[2,8]{1,0:T(2,128)} %bitcast.11, bf16[8,32,128]{2,1,0:T(8,128)(2,1)} %rhs_hbm.1, bf16[8,128,128]{2,1,0:T(8,128)(2,1)} %lower_hbm.1, bf16[8,2,128,1024]{3,2,1,0:T(8,128)(2,1)} %blocks_hbm.1), custom_call_target="tpu_custom_call" | custom-call | flops 536870912 | bytes 5242880 | tf_op jit(solution)/shard_map/forward/pallas_call | solution.py:168
  3.3 0.5 %collective-permute-start = (bf16[2,32,1024]{2,1,0:T(8,128)(2,1)S(1)}, bf16[2,32,1024]{2,1,0:T(8,128)(2,1)S(1)}, u32[]{:S(2)}, u32[]{:S(2)}) collective-permute-start(bf16[2,32,1024]{2,1,0:T(8,128)(2,1)S(1)} %get-tuple-element.14), channel_id=1, source_target_pairs={{0,1},{1,0},{2,3},{3,2},{4,5},{5,4},{6,7},{7,6},{8,9},{9,8},{10,11... | collective-permute-start | bytes 393224 | tf_op jit(solution)/shard_map/ppermute | solution.py:38
  3.9 0.7 %copy-done = bf16[2,1024,256]{2,1,0:T(8,128)(2,1)S(1)} copy-done((bf16[2,1024,256]{2,1,0:T(8,128)(2,1)S(1)}, bf16[2,1024,256]{2,1,0:T(8,128)(2,1)}, u32[]{:S(2)}) %copy-start) | copy-done | bytes 1048600
  4.7 0.1 collective-permute-done.came
  4.8 0.4 %collective-permute-start.1 = (bf16[3,1024,256]{2,1,0:T(8,128)(2,1)S(1)}, bf16[3,1024,256]{2,1,0:T(8,128)(2,1)S(1)}, u32[]{:S(2)}, u32[]{:S(2)}) collective-permute-start(bf16[3,1024,256]{2,1,0:T(8,128)(2,1)S(1)} %pad_maximum_fusion), channel_id=1, source_target_pairs={{0,1},{1,0},{2,3},{3,2},{4,5},{5,4},{6,7},{7,6},{8,9},{9,8},{10,11... | collective-permute-start | bytes 4718600 | tf_op jit(solution)/shard_map/ppermute | solution.py:38
  5.3 3.6 %collective-permute-start.2 = (bf16[32,1024]{1,0:T(8,128)(2,1)S(1)}, bf16[32,1024]{1,0:T(8,128)(2,1)S(1)}, u32[]{:S(2)}, u32[]{:S(2)}) collective-permute-start(bf16[32,1024]{1,0:T(8,128)(2,1)S(1)} %get-tuple-element.23), channel_id=1, source_target_pairs={{0,6},{1,7},{2,4},{3,5},{4,10},{5,11},{6,8},{7,9},{8,14},{9,15},{1... | collective-permute-start | bytes 196616 | tf_op jit(solution)/shard_map/ppermute | solution.py:38
  8.9 1.2 %collective-permute-start.3 = (bf16[32,1024]{1,0:T(8,128)(2,1)S(1)}, bf16[32,1024]{1,0:T(8,128)(2,1)S(1)}, u32[]{:S(2)}, u32[]{:S(2)}) collective-permute-start(bf16[32,1024]{1,0:T(8,128)(2,1)S(1)} %get-tuple-element.23), channel_id=1, source_target_pairs={{0,5},{1,4},{2,7},{3,6},{4,9},{5,8},{6,11},{7,10},{8,13},{9,12},{1... | collective-permute-start | bytes 196616 | tf_op jit(solution)/shard_map/ppermute | solution.py:38
  10.1 0.6 %collective-permute-start.4 = (bf16[32,1024]{1,0:T(8,128)(2,1)S(1)}, bf16[32,1024]{1,0:T(8,128)(2,1)S(1)}, u32[]{:S(2)}, u32[]{:S(2)}) collective-permute-start(bf16[32,1024]{1,0:T(8,128)(2,1)S(1)} %get-tuple-element.22), channel_id=1, source_target_pairs={{0,3},{1,2},{2,1},{3,0},{4,7},{5,6},{6,5},{7,4},{8,11},{9,10},{10,... | collective-permute-start | bytes 196616 | tf_op jit(solution)/shard_map/ppermute | solution.py:38
  10.7 3.9 %collective-permute-done.2.rest_0_ = bf16[32,1024]{1,0:T(8,128)(2,1)S(1)} collective-permute-done((bf16[32,1024]{1,0:T(8,128)(2,1)S(1)}, bf16[32,1024]{1,0:T(8,128)(2,1)S(1)}, u32[]{:S(2)}, u32[]{:S(2)}) %collective-permute-start.2) | collective-permute-done | bytes 65568 | tf_op jit(solution)/shard_map/ppermute | solution.py:38
  14.6 1.1 %collective-permute-done.3.rest_1_ = bf16[32,1024]{1,0:T(8,128)(2,1)S(1)} collective-permute-done((bf16[32,1024]{1,0:T(8,128)(2,1)S(1)}, bf16[32,1024]{1,0:T(8,128)(2,1)S(1)}, u32[]{:S(2)}, u32[]{:S(2)}) %collective-permute-start.3) | collective-permute-done | bytes 65568 | tf_op jit(solution)/shard_map/ppermute | solution.py:38
  15.8 0.3 parent_forward.1.mine
  16.0 1.1 %collective-permute-start.6 = (bf16[32,512]{1,0:T(8,128)(2,1)S(1)}, bf16[32,512]{1,0:T(8,128)(2,1)S(1)}, u32[]{:S(2)}, u32[]{:S(2)}) collective-permute-start(bf16[32,512]{1,0:T(8,128)(2,1)S(1)} %parent_forward.1.mine), channel_id=1, source_target_pairs={{0,3},{1,2},{2,1},{3,0},{4,7},{5,6},{6,5},{7,4},{8,11},{9,10},{10,... | collective-permute-start | bytes 98312 | tf_op jit(solution)/shard_map/ppermute | solution.py:38
  17.1 0.4 %collective-permute-start.5 = (bf16[32,512]{1,0:T(8,128)(2,1)S(1)}, bf16[32,512]{1,0:T(8,128)(2,1)S(1)}, u32[]{:S(2)}, u32[]{:S(2)}) collective-permute-start(bf16[32,512]{1,0:T(8,128)(2,1)S(1)} %parent_forward.1.mine), channel_id=1, source_target_pairs={{0,1},{1,0},{2,3},{3,2},{4,5},{5,4},{6,7},{7,6},{8,9},{9,8},{10,11... | collective-permute-start | bytes 98312 | tf_op jit(solution)/shard_map/ppermute | solution.py:38
  17.6 2.0 %collective-permute-done.6 = bf16[32,512]{1,0:T(8,128)(2,1)S(1)} collective-permute-done((bf16[32,512]{1,0:T(8,128)(2,1)S(1)}, bf16[32,512]{1,0:T(8,128)(2,1)S(1)}, u32[]{:S(2)}, u32[]{:S(2)}) %collective-permute-start.6) | collective-permute-done | bytes 32800 | tf_op jit(solution)/shard_map/ppermute | solution.py:38
  19.6 0.3 parent_early.1.part
  19.9 0.8 %collective-permute-done.7.theirs = bf16[1,32,512]{2,1,0:T(8,128)(2,1)S(1)} collective-permute-done((bf16[1,32,512]{2,1,0:T(8,128)(2,1)S(1)}, bf16[1,32,512]{2,1,0:T(8,128)(2,1)S(1)}, u32[]{:S(2)}, u32[]{:S(2)}) %collective-permute-start.7) | collective-permute-done | bytes 32800 | tf_op jit(solution)/shard_map/ppermute | solution.py:38
  20.7 0.3 %parent_backward.1 = (f32[2,32,256]{2,1,0:T(8,128)S(1)}, bf16[2,32,512]{2,1,0:T(8,128)(2,1)S(1)}) custom-call(f32[2,32,512]{2,1,0:T(8,128)S(1)} %parent_early.1.part, bf16[1,32,512]{2,1,0:T(8,128)(2,1)S(1)} %bitcast.10, bf16[1,32,512]{2,1,0:T(8,128)(2,1)S(1)} %collective-permute-done.7.theirs, bf16[2,1024,256]{2,1,0:T(8,128)(2,1)S(1)} %copy-done, ...), custom_call_target="tpu_custom_call" | custom-call | flops 67108864 | bytes 2097152 | tf_op jit(solution)/shard_map/parent_backward/pallas_call | solution.py:223
  21.0 1.7 %collective-permute-start.8 = (bf16[2,32,512]{2,1,0:T(8,128)(2,1)S(1)}, bf16[2,32,512]{2,1,0:T(8,128)(2,1)S(1)}, u32[]{:S(2)}, u32[]{:S(2)}) collective-permute-start(bf16[2,32,512]{2,1,0:T(8,128)(2,1)S(1)} %get-tuple-element.21.rest_0_), channel_id=1, source_target_pairs={{0,29},{1,30},{2,31},{3,28},{4,1},{5,2},{6,3},{7,0},{8,5},{9,6},{1... | collective-permute-start | bytes 196616 | tf_op jit(solution)/shard_map/ppermute | solution.py:38
  22.7 1.4 %collective-permute-start.10 = (bf16[2,32,512]{2,1,0:T(8,128)(2,1)S(1)}, bf16[2,32,512]{2,1,0:T(8,128)(2,1)S(1)}, u32[]{:S(2)}, u32[]{:S(2)}) collective-permute-start(bf16[2,32,512]{2,1,0:T(8,128)(2,1)S(1)} %get-tuple-element.21.rest_0_), channel_id=1, source_target_pairs={{0,3},{1,2},{2,1},{3,0},{4,7},{5,6},{6,5},{7,4},{8,11},{9,10},{10,... | collective-permute-start | bytes 196616 | tf_op jit(solution)/shard_map/ppermute | solution.py:38
  24.1 1.6 %collective-permute-done.8 = bf16[2,32,512]{2,1,0:T(8,128)(2,1)S(1)} collective-permute-done((bf16[2,32,512]{2,1,0:T(8,128)(2,1)S(1)}, bf16[2,32,512]{2,1,0:T(8,128)(2,1)S(1)}, u32[]{:S(2)}, u32[]{:S(2)}) %collective-permute-start.8) | collective-permute-done | bytes 65568 | tf_op jit(solution)/shard_map/ppermute | solution.py:38
  25.8 0.2 collective-permute-start.9
  25.9 0.7 %collective-permute-done.10.rest_1_ = bf16[2,32,512]{2,1,0:T(8,128)(2,1)S(1)} collective-permute-done((bf16[2,32,512]{2,1,0:T(8,128)(2,1)S(1)}, bf16[2,32,512]{2,1,0:T(8,128)(2,1)S(1)}, u32[]{:S(2)}, u32[]{:S(2)}) %collective-permute-start.10) | collective-permute-done | bytes 65568 | tf_op jit(solution)/shard_map/ppermute | solution.py:38
  26.6 0.4 %collective-permute-done.9.theirs = bf16[1,2,32,512]{3,2,1,0:T(8,128)(2,1)S(1)} collective-permute-done((bf16[1,2,32,512]{3,2,1,0:T(8,128)(2,1)S(1)}, bf16[1,2,32,512]{3,2,1,0:T(8,128)(2,1)S(1)}, u32[]{:S(2)}, u32[]{:S(2)}) %collective-permute-start.9) | collective-permute-done | bytes 65568 | tf_op jit(solution)/shard_map/ppermute | solution.py:38
  27.0 1.6 %backward.1 = (f32[8,32,128]{2,1,0:T(8,128)}, f32[2,32,256]{2,1,0:T(8,128)}) custom-call(s32[2,8]{1,0:T(2,128)S(1)} %bitcast.12, f32[2,32,256]{2,1,0:T(8,128)S(1)} %get-tuple-element.19.full, bf16[8,32,128]{2,1,0:T(8,128)(2,1)S(1)} %get-tuple-element.20.solved, bf16[1,2,32,512]{3,2,1,0:T(8,128)(2,1)S(1)} %bitcast.8, ...), custom_call_target="tpu_custom_call" | custom-call | flops 268435456 | bytes 5242880 | tf_op jit(solution)/shard_map/backward/pallas_call | solution.py:237
  (18 shorter events, 0.3 us)
Async XLA Ops:
  0.6 3.2 %copy-start.2 = (bf16[2,1024,256]{2,1,0:T(8,128)(2,1)S(1)}, bf16[2,1024,256]{2,1,0:T(8,128)(2,1)}, u32[]{:S(2)}) copy-start(bf16[2,1024,256]{2,1,0:T(8,128)(2,1)} %lower) | copy-start | bytes 3145732
  3.3 1.2 %copy-start = (bf16[2,1024,256]{2,1,0:T(8,128)(2,1)S(1)}, bf16[2,1024,256]{2,1,0:T(8,128)(2,1)}, u32[]{:S(2)}) copy-start(bf16[2,1024,256]{2,1,0:T(8,128)(2,1)} %upper.2) | copy-start | bytes 3145732
  3.3 1.5 %collective-permute-start = (bf16[2,32,1024]{2,1,0:T(8,128)(2,1)S(1)}, bf16[2,32,1024]{2,1,0:T(8,128)(2,1)S(1)}, u32[]{:S(2)}, u32[]{:S(2)}) collective-permute-start(bf16[2,32,1024]{2,1,0:T(8,128)(2,1)S(1)} %get-tuple-element.14), channel_id=1, source_target_pairs={{0,1},{1,0},{2,3},{3,2},{4,5},{5,4},{6,7},{7,6},{8,9},{9,8},{10,11... | collective-permute-start | bytes 393224 | tf_op jit(solution)/shard_map/ppermute | solution.py:38
  4.6 11.2 %copy-start.4 = (bf16[2,32,1024]{2,1,0:T(8,128)(2,1)S(1)}, bf16[2,32,1024]{2,1,0:T(8,128)(2,1)}, u32[]{:S(2)}) copy-start(bf16[2,32,1024]{2,1,0:T(8,128)(2,1)} %rhs.1) | copy-start | bytes 393220
  4.8 10.9 %collective-permute-start.1 = (bf16[3,1024,256]{2,1,0:T(8,128)(2,1)S(1)}, bf16[3,1024,256]{2,1,0:T(8,128)(2,1)S(1)}, u32[]{:S(2)}, u32[]{:S(2)}) collective-permute-start(bf16[3,1024,256]{2,1,0:T(8,128)(2,1)S(1)} %pad_maximum_fusion), channel_id=1, source_target_pairs={{0,1},{1,0},{2,3},{3,2},{4,5},{5,4},{6,7},{7,6},{8,9},{9,8},{10,11... | collective-permute-start | bytes 4718600 | tf_op jit(solution)/shard_map/ppermute | solution.py:38
  5.3 9.4 %collective-permute-start.2 = (bf16[32,1024]{1,0:T(8,128)(2,1)S(1)}, bf16[32,1024]{1,0:T(8,128)(2,1)S(1)}, u32[]{:S(2)}, u32[]{:S(2)}) collective-permute-start(bf16[32,1024]{1,0:T(8,128)(2,1)S(1)} %get-tuple-element.23), channel_id=1, source_target_pairs={{0,6},{1,7},{2,4},{3,5},{4,10},{5,11},{6,8},{7,9},{8,14},{9,15},{1... | collective-permute-start | bytes 196616 | tf_op jit(solution)/shard_map/ppermute | solution.py:38
  8.9 6.8 %collective-permute-start.3 = (bf16[32,1024]{1,0:T(8,128)(2,1)S(1)}, bf16[32,1024]{1,0:T(8,128)(2,1)S(1)}, u32[]{:S(2)}, u32[]{:S(2)}) collective-permute-start(bf16[32,1024]{1,0:T(8,128)(2,1)S(1)} %get-tuple-element.23), channel_id=1, source_target_pairs={{0,5},{1,4},{2,7},{3,6},{4,9},{5,8},{6,11},{7,10},{8,13},{9,12},{1... | collective-permute-start | bytes 196616 | tf_op jit(solution)/shard_map/ppermute | solution.py:38
  10.1 5.6 %collective-permute-start.4 = (bf16[32,1024]{1,0:T(8,128)(2,1)S(1)}, bf16[32,1024]{1,0:T(8,128)(2,1)S(1)}, u32[]{:S(2)}, u32[]{:S(2)}) collective-permute-start(bf16[32,1024]{1,0:T(8,128)(2,1)S(1)} %get-tuple-element.22), channel_id=1, source_target_pairs={{0,3},{1,2},{2,1},{3,0},{4,7},{5,6},{6,5},{7,4},{8,11},{9,10},{10,... | collective-permute-start | bytes 196616 | tf_op jit(solution)/shard_map/ppermute | solution.py:38
  16.0 3.5 %collective-permute-start.6 = (bf16[32,512]{1,0:T(8,128)(2,1)S(1)}, bf16[32,512]{1,0:T(8,128)(2,1)S(1)}, u32[]{:S(2)}, u32[]{:S(2)}) collective-permute-start(bf16[32,512]{1,0:T(8,128)(2,1)S(1)} %parent_forward.1.mine), channel_id=1, source_target_pairs={{0,3},{1,2},{2,1},{3,0},{4,7},{5,6},{6,5},{7,4},{8,11},{9,10},{10,... | collective-permute-start | bytes 98312 | tf_op jit(solution)/shard_map/ppermute | solution.py:38
  17.1 2.5 %collective-permute-start.5 = (bf16[32,512]{1,0:T(8,128)(2,1)S(1)}, bf16[32,512]{1,0:T(8,128)(2,1)S(1)}, u32[]{:S(2)}, u32[]{:S(2)}) collective-permute-start(bf16[32,512]{1,0:T(8,128)(2,1)S(1)} %parent_forward.1.mine), channel_id=1, source_target_pairs={{0,1},{1,0},{2,3},{3,2},{4,5},{5,4},{6,7},{7,6},{8,9},{9,8},{10,11... | collective-permute-start | bytes 98312 | tf_op jit(solution)/shard_map/ppermute | solution.py:38
  19.5 1.2 %collective-permute-start.7 = (bf16[1,32,512]{2,1,0:T(8,128)(2,1)S(1)}, bf16[1,32,512]{2,1,0:T(8,128)(2,1)S(1)}, u32[]{:S(2)}, u32[]{:S(2)}) collective-permute-start(bf16[1,32,512]{2,1,0:T(8,128)(2,1)S(1)} %bitcast.9), channel_id=1, source_target_pairs={{0,1},{1,0},{2,3},{3,2},{4,5},{5,4},{6,7},{7,6},{8,9},{9,8},{10,11... | collective-permute-start | bytes 98312 | tf_op jit(solution)/shard_map/ppermute | solution.py:38
  19.6 7.4 %copy-start.1 = (bf16[8,2,1024,128]{3,2,1,0:T(8,128)(2,1)S(1)}, bf16[8,2,1024,128]{3,2,1,0:T(8,128)(2,1)}, u32[]{:S(2)}) copy-start(bf16[8,2,1024,128]{3,2,1,0:T(8,128)(2,1)} %blocks.1) | copy-start | bytes 12582916
  19.9 7.1 %copy-start.3 = (bf16[8,128,128]{2,1,0:T(8,128)(2,1)S(1)}, bf16[8,128,128]{2,1,0:T(8,128)(2,1)}, u32[]{:S(2)}) copy-start(bf16[8,128,128]{2,1,0:T(8,128)(2,1)} %upper.3) | copy-start | bytes 786436
  19.9 7.1 %copy-start.5 = (s32[8,2]{0,1:T(2,128)S(1)}, s32[8,2]{0,1:T(2,128)}, u32[]{:S(2)}) copy-start(s32[8,2]{0,1:T(2,128)} %param.17) | copy-start | bytes 196
  21.0 4.7 %collective-permute-start.8 = (bf16[2,32,512]{2,1,0:T(8,128)(2,1)S(1)}, bf16[2,32,512]{2,1,0:T(8,128)(2,1)S(1)}, u32[]{:S(2)}, u32[]{:S(2)}) collective-permute-start(bf16[2,32,512]{2,1,0:T(8,128)(2,1)S(1)} %get-tuple-element.21.rest_0_), channel_id=1, source_target_pairs={{0,29},{1,30},{2,31},{3,28},{4,1},{5,2},{6,3},{7,0},{8,5},{9,6},{1... | collective-permute-start | bytes 196616 | tf_op jit(solution)/shard_map/ppermute | solution.py:38
  22.7 3.9 %collective-permute-start.10 = (bf16[2,32,512]{2,1,0:T(8,128)(2,1)S(1)}, bf16[2,32,512]{2,1,0:T(8,128)(2,1)S(1)}, u32[]{:S(2)}, u32[]{:S(2)}) collective-permute-start(bf16[2,32,512]{2,1,0:T(8,128)(2,1)S(1)} %get-tuple-element.21.rest_0_), channel_id=1, source_target_pairs={{0,3},{1,2},{2,1},{3,0},{4,7},{5,6},{6,5},{7,4},{8,11},{9,10},{10,... | collective-permute-start | bytes 196616 | tf_op jit(solution)/shard_map/ppermute | solution.py:38
  25.8 1.3 %collective-permute-start.9 = (bf16[1,2,32,512]{3,2,1,0:T(8,128)(2,1)S(1)}, bf16[1,2,32,512]{3,2,1,0:T(8,128)(2,1)S(1)}, u32[]{:S(2)}, u32[]{:S(2)}) collective-permute-start(bf16[1,2,32,512]{3,2,1,0:T(8,128)(2,1)S(1)} %bitcast.7), channel_id=1, source_target_pairs={{0,1},{1,0},{2,3},{3,2},{4,5},{5,4},{6,7},{7,6},{8,9},{9,8},{10,11... | collective-permute-start | bytes 196616 | tf_op jit(solution)/shard_map/ppermute | solution.py:38

commit v8 on v7

--- a/solution.py
+++ b/solution.py
@@ -131,23 +131,70 @@
         half_ref[of, :, columns(1 - core, cut)] = there.astype(BF16)
 
 
-def backward_kernel(targets, full, solved, mine, theirs, blocks, upper, *rest):
-    halves, (leaf_ref, parent_ref, window) = rest[:-3], rest[-3:]
-    parent_ref[...] = full[...]
-    leaves, k, wide, width = blocks.shape
-    chips = len(halves)
-    depth = wide // chips
-    chip, core, _ = place()
+def fill_window(window, halves, nexts, lag):
+    chip, _, _ = place()
+    chips, depth = len(halves), halves[0].shape[2]
     for by, half in enumerate(halves):
         window[pl.ds(0, 2), :, columns(lax.rem(chip + chips - by, chips), depth)] = half[...]
-    for by in range(0, chips, CORES):
-        for arrived, lag in ((mine, 1 - core), (theirs, core)):
-            at = columns(lax.rem(chip + chips - by - lag, chips), depth)
-            window[pl.ds(2, 2), :, at] = arrived[by // CORES]
+    parts = [columns(lax.rem(chip + chips - by - lag, chips), depth) for by in range(0, chips, CORES)]
+    for i, at in enumerate(parts):
+        window[pl.ds(2, 2), :, at] = nexts[i]
+    return parts
+
+
+def coupled(window, listed, blocks, a, parts):
+    return functools.reduce(
+        jnp.add, [dot(window[listed[i, a], :, at], blocks[a, i, at, :]) for i in range(blocks.shape[1]) for at in parts]
+    )
+
+
+def backward_first_kernel(targets, nexts, half, blocks, upper, part_ref, window):
+    chip, core, _ = place()
+    depth = half.shape[2]
+    rows = columns(chip, depth)
+
+    @pl.when(core == 1)
+    def _():
+        window[pl.ds(0, 2)] = half[...]
+        window[pl.ds(2, 2)] = nexts[0]
+        listed = targets[...]
+        for a in range(blocks.shape[0]):
+            part_ref[a] = functools.reduce(
+                jnp.add, [dot(window[listed[i, a]], blocks[a, i, rows, :]) for i in range(blocks.shape[1])]
+            )
+
+    @pl.when(core == 0)
+    def _():
+        part_ref[...] = jnp.zeros_like(part_ref)
+
+
+def backward_second_kernel(targets, nexts, blocks, first, *rest):
+    halves, (part_ref, window) = rest[:-2], rest[-2:]
+    _, core, _ = place()
+    part_ref[...] = first[...]
+
+    def add(parts):
+        listed = targets[...]
+        for a in range(blocks.shape[0]):
+            part_ref[a] += coupled(window, listed, blocks, a, parts)
+
+    chips = len(halves)
+    if chips > CORES:
+        add(fill_window(window, halves, nexts, 1 - core)[1:])
+
+    @pl.when(core == 0)
+    def _():
+        add(fill_window(window, halves, nexts, 1 - core)[:1])
+
+
+def backward_kernel(targets, full, solved, part, nexts, blocks, upper, *rest):
+    halves, (leaf_ref, parent_ref, window) = rest[:-3], rest[-3:]
+    _, core, _ = place()
+    parent_ref[...] = full[...]
+    parts = fill_window(window, halves, nexts, core)
     listed = targets[...]
-    couplings = [
-        functools.reduce(jnp.add, [dot(window[listed[i, a]], blocks[a, i]) for i in range(k)]) for a in range(leaves)
-    ]
+    leaves = blocks.shape[0]
+    couplings = [part[a] + coupled(window, listed, blocks, a, parts) for a in range(leaves)]
     for a in range(leaves):
         reduced = (solved[a].astype(F32) - couplings[a]).astype(BF16)
         leaf_ref[a] = dot(reduced, upper[a])
@@ -234,16 +281,40 @@
     mine = jnp.stack([go(half, by_row=-1, target=fan(by)) for by in range(0, chips, CORES)])
     theirs = go(mine, by_row=0, target=along(0, 1))
 
+    first = pl.pallas_call(
+        backward_first_kernel,
+        in_specs=[VMEM] * 5,
+        out_specs=VMEM,
+        out_shape=jax.ShapeDtypeStruct((leaves, nrhs, width), F32),
+        scratch_shapes=[pltpu.VMEM((4, nrhs, depth), BF16)],
+        compiler_params=pltpu.CompilerParams(vmem_limit_bytes=16 << 20),
+        cost_estimate=pl.CostEstimate(flops=1 << 26, bytes_accessed=2 << 20, transcendentals=0),
+        name="backward_first",
+    )(listed, mine, half, upper_blocks, leaf_upper)
+    part = pl.pallas_call(
+        backward_second_kernel,
+        in_specs=[VMEM] * (4 + chips),
+        out_specs=VMEM,
+        out_shape=jax.ShapeDtypeStruct((leaves, nrhs, width), F32),
+        scratch_shapes=[pltpu.VMEM((4, nrhs, wide), BF16)],
+        compiler_params=pltpu.CompilerParams(vmem_limit_bytes=16 << 20),
+        cost_estimate=pl.CostEstimate(flops=1 << 26, bytes_accessed=2 << 20, transcendentals=0),
+        name="backward_second",
+    )(listed, mine, upper_blocks, first, *halves)
+
     return pl.pallas_call(
         backward_kernel,
         in_specs=[VMEM] * (7 + chips),
         out_specs=[VMEM, VMEM],
-        out_shape=[jax.ShapeDtypeStruct((leaves, nrhs, width), F32), jax.ShapeDtypeStruct(full.shape, F32)],
+        out_shape=[
+            jax.ShapeDtypeStruct((leaves, nrhs, width), F32),
+            jax.ShapeDtypeStruct(full.shape, F32),
+        ],
         scratch_shapes=[pltpu.VMEM((4, nrhs, wide), BF16)],
-        compiler_params=pltpu.CompilerParams(vmem_limit_bytes=24 << 20),
-        cost_estimate=pl.CostEstimate(flops=1 << 28, bytes_accessed=5 << 20, transcendentals=0),
+        compiler_params=pltpu.CompilerParams(vmem_limit_bytes=16 << 20),
+        cost_estimate=pl.CostEstimate(flops=1 << 27, bytes_accessed=3 << 20, transcendentals=0),
         name="backward",
-    )(listed, full, solved, mine, theirs, upper_blocks, leaf_upper, *halves)
+    )(listed, full, solved, part, theirs, upper_blocks, leaf_upper, *halves)
 
 
 def solution(mesh):

time: 28.9 us -> 28.6 us (0.990)
  waiting for transfers between devices: 10.7 us -> 10.2 us
    pallas_call x0 -> x2, Pallas kernels: none -> 0.53 us  [the longest x1 0.51 us: local(): pl.pallas_call(backward_second_kernel, in_specs=[VMEM] * (4 + chips), out...]
    ppermute x11, waiting for transfers between devices: 10.7 us -> 10.2 us  [send(): return lax.ppermute(array, ('row', 'col'), pairs)]
  transfers between devices with their start and end apart: 11 -> 11, of which waited for: 8 -> 7; matrix products, arithmetic and copies ran while one was open for 1% -> 1% of each run, Pallas kernels for 1% -> 3%
where the time goes in v8:
time: 28.6 us; the launch traced here: 28.5 us
  starting transfers between devices  11.3 us (40%)
  waiting for transfers between devices  10.2 us (36%)
  Pallas kernels  5.36 us (19%)
  between operations  0.73 us (3%)
  local copies, waits for them, and re-layouts  0.72 us (3%)
    ppermute x11, starting transfers between devices, send(): return lax.ppermute(array, ('row', 'col'), pairs)  11.3 us
    ppermute x11, waiting for transfers between devices, send(): return lax.ppermute(array, ('row', 'col'), pairs)  10.2 us
    pallas_call x1, Pallas kernels, local(): pl.pallas_call(forward_kernel, in_specs=[HBM] * 4, out_specs=[VMEM] * 3,...  2.68 us
    pallas_call x1, Pallas kernels, local(): pl.pallas_call(backward_kernel, in_specs=[VMEM] * (7 + chips), out_specs=...  1.29 us
    unnamed x12, local copies, waits for them, and re-layouts  0.68 us
  transfers between devices with their start and end apart: 11, of which 7 were waited for; matrix products, arithmetic and copies ran while one was open for 1% of the time, Pallas kernels for 3%

profile of v8, /device:TPU:0, one launch (start us, length us, event | category | flops | bytes accessed | tf_op | source)
XLA Modules:
  0.0 28.5 jit_solution(1036885833293508429)
XLA Ops:
  0.6 2.7 %forward.1 = (bf16[8,32,128]{2,1,0:T(8,128)(2,1)S(1)}, f32[2,32,1024]{2,1,0:T(8,128)S(1)}, bf16[2,32,1024]{2,1,0:T(8,128)(2,1)S(1)}) custom-call(s32[2,8]{1,0:T(2,128)} %bitcast.12, bf16[8,32,128]{2,1,0:T(8,128)(2,1)} %rhs_hbm.1, bf16[8,128,128]{2,1,0:T(8,128)(2,1)} %lower_hbm.1, bf16[8,2,128,1024]{3,2,1,0:T(8,128)(2,1)} %blocks_hbm.1), custom_call_target="tpu_custom_call" | custom-call | flops 536870912 | bytes 5242880 | tf_op jit(solution)/shard_map/forward/pallas_call | solution.py:215
  3.3 0.5 %collective-permute-start = (bf16[2,32,1024]{2,1,0:T(8,128)(2,1)S(1)}, bf16[2,32,1024]{2,1,0:T(8,128)(2,1)S(1)}, u32[]{:S(2)}, u32[]{:S(2)}) collective-permute-start(bf16[2,32,1024]{2,1,0:T(8,128)(2,1)S(1)} %get-tuple-element.14), channel_id=1, source_target_pairs={{0,1},{1,0},{2,3},{3,2},{4,5},{5,4},{6,7},{7,6},{8,9},{9,8},{10,11... | collective-permute-start | bytes 393224 | tf_op jit(solution)/shard_map/ppermute | solution.py:38
  3.9 0.7 %copy-done.1 = bf16[2,1024,256]{2,1,0:T(8,128)(2,1)S(1)} copy-done((bf16[2,1024,256]{2,1,0:T(8,128)(2,1)S(1)}, bf16[2,1024,256]{2,1,0:T(8,128)(2,1)}, u32[]{:S(2)}) %copy-start.1) | copy-done | bytes 1048600
  4.7 0.1 collective-permute-done.came
  4.8 0.4 %collective-permute-start.1 = (bf16[3,1024,256]{2,1,0:T(8,128)(2,1)S(1)}, bf16[3,1024,256]{2,1,0:T(8,128)(2,1)S(1)}, u32[]{:S(2)}, u32[]{:S(2)}) collective-permute-start(bf16[3,1024,256]{2,1,0:T(8,128)(2,1)S(1)} %pad_maximum_fusion), channel_id=1, source_target_pairs={{0,1},{1,0},{2,3},{3,2},{4,5},{5,4},{6,7},{7,6},{8,9},{9,8},{10,11... | collective-permute-start | bytes 4718600 | tf_op jit(solution)/shard_map/ppermute | solution.py:38
  5.3 3.6 %collective-permute-start.2 = (bf16[32,1024]{1,0:T(8,128)(2,1)S(1)}, bf16[32,1024]{1,0:T(8,128)(2,1)S(1)}, u32[]{:S(2)}, u32[]{:S(2)}) collective-permute-start(bf16[32,1024]{1,0:T(8,128)(2,1)S(1)} %get-tuple-element.23), channel_id=1, source_target_pairs={{0,6},{1,7},{2,4},{3,5},{4,10},{5,11},{6,8},{7,9},{8,14},{9,15},{1... | collective-permute-start | bytes 196616 | tf_op jit(solution)/shard_map/ppermute | solution.py:38
  8.9 1.2 %collective-permute-start.3 = (bf16[32,1024]{1,0:T(8,128)(2,1)S(1)}, bf16[32,1024]{1,0:T(8,128)(2,1)S(1)}, u32[]{:S(2)}, u32[]{:S(2)}) collective-permute-start(bf16[32,1024]{1,0:T(8,128)(2,1)S(1)} %get-tuple-element.23), channel_id=1, source_target_pairs={{0,5},{1,4},{2,7},{3,6},{4,9},{5,8},{6,11},{7,10},{8,13},{9,12},{1... | collective-permute-start | bytes 196616 | tf_op jit(solution)/shard_map/ppermute | solution.py:38
  10.1 0.6 %collective-permute-start.4 = (bf16[32,1024]{1,0:T(8,128)(2,1)S(1)}, bf16[32,1024]{1,0:T(8,128)(2,1)S(1)}, u32[]{:S(2)}, u32[]{:S(2)}) collective-permute-start(bf16[32,1024]{1,0:T(8,128)(2,1)S(1)} %get-tuple-element.22), channel_id=1, source_target_pairs={{0,3},{1,2},{2,1},{3,0},{4,7},{5,6},{6,5},{7,4},{8,11},{9,10},{10,... | collective-permute-start | bytes 196616 | tf_op jit(solution)/shard_map/ppermute | solution.py:38
  10.7 3.9 %collective-permute-done.2.rest_0_ = bf16[32,1024]{1,0:T(8,128)(2,1)S(1)} collective-permute-done((bf16[32,1024]{1,0:T(8,128)(2,1)S(1)}, bf16[32,1024]{1,0:T(8,128)(2,1)S(1)}, u32[]{:S(2)}, u32[]{:S(2)}) %collective-permute-start.2) | collective-permute-done | bytes 65568 | tf_op jit(solution)/shard_map/ppermute | solution.py:38
  14.6 1.1 %collective-permute-done.3.rest_1_ = bf16[32,1024]{1,0:T(8,128)(2,1)S(1)} collective-permute-done((bf16[32,1024]{1,0:T(8,128)(2,1)S(1)}, bf16[32,1024]{1,0:T(8,128)(2,1)S(1)}, u32[]{:S(2)}, u32[]{:S(2)}) %collective-permute-start.3) | collective-permute-done | bytes 65568 | tf_op jit(solution)/shard_map/ppermute | solution.py:38
  15.8 0.3 parent_forward.1.mine
  16.0 1.1 %collective-permute-start.6 = (bf16[32,512]{1,0:T(8,128)(2,1)S(1)}, bf16[32,512]{1,0:T(8,128)(2,1)S(1)}, u32[]{:S(2)}, u32[]{:S(2)}) collective-permute-start(bf16[32,512]{1,0:T(8,128)(2,1)S(1)} %parent_forward.1.mine), channel_id=1, source_target_pairs={{0,3},{1,2},{2,1},{3,0},{4,7},{5,6},{6,5},{7,4},{8,11},{9,10},{10,... | collective-permute-start | bytes 98312 | tf_op jit(solution)/shard_map/ppermute | solution.py:38
  17.1 0.4 %collective-permute-start.5 = (bf16[32,512]{1,0:T(8,128)(2,1)S(1)}, bf16[32,512]{1,0:T(8,128)(2,1)S(1)}, u32[]{:S(2)}, u32[]{:S(2)}) collective-permute-start(bf16[32,512]{1,0:T(8,128)(2,1)S(1)} %parent_forward.1.mine), channel_id=1, source_target_pairs={{0,1},{1,0},{2,3},{3,2},{4,5},{5,4},{6,7},{7,6},{8,9},{9,8},{10,11... | collective-permute-start | bytes 98312 | tf_op jit(solution)/shard_map/ppermute | solution.py:38
  17.6 2.0 %collective-permute-done.6 = bf16[32,512]{1,0:T(8,128)(2,1)S(1)} collective-permute-done((bf16[32,512]{1,0:T(8,128)(2,1)S(1)}, bf16[32,512]{1,0:T(8,128)(2,1)S(1)}, u32[]{:S(2)}, u32[]{:S(2)}) %collective-permute-start.6) | collective-permute-done | bytes 32800 | tf_op jit(solution)/shard_map/ppermute | solution.py:38
  19.6 0.3 parent_early.1.part
  19.9 0.8 %collective-permute-done.7.theirs = bf16[1,32,512]{2,1,0:T(8,128)(2,1)S(1)} collective-permute-done((bf16[1,32,512]{2,1,0:T(8,128)(2,1)S(1)}, bf16[1,32,512]{2,1,0:T(8,128)(2,1)S(1)}, u32[]{:S(2)}, u32[]{:S(2)}) %collective-permute-start.7) | collective-permute-done | bytes 32800 | tf_op jit(solution)/shard_map/ppermute | solution.py:38
  20.7 0.3 %parent_backward.1 = (f32[2,32,256]{2,1,0:T(8,128)S(1)}, bf16[2,32,512]{2,1,0:T(8,128)(2,1)S(1)}) custom-call(f32[2,32,512]{2,1,0:T(8,128)S(1)} %parent_early.1.part, bf16[1,32,512]{2,1,0:T(8,128)(2,1)S(1)} %bitcast.11, bf16[1,32,512]{2,1,0:T(8,128)(2,1)S(1)} %collective-permute-done.7.theirs, bf16[2,1024,256]{2,1,0:T(8,128)(2,1)S(1)} %copy-done.1, ...), custom_call_target="tpu_custom_call" | custom-call | flops 67108864 | bytes 2097152 | tf_op jit(solution)/shard_map/parent_backward/pallas_call | solution.py:270
  21.0 1.7 %collective-permute-start.8 = (bf16[2,32,512]{2,1,0:T(8,128)(2,1)S(1)}, bf16[2,32,512]{2,1,0:T(8,128)(2,1)S(1)}, u32[]{:S(2)}, u32[]{:S(2)}) collective-permute-start(bf16[2,32,512]{2,1,0:T(8,128)(2,1)S(1)} %get-tuple-element.21.half.rest_0_), channel_id=1, source_target_pairs={{0,29},{1,30},{2,31},{3,28},{4,1},{5,2},{6,3},{7,0},{8,5},{9,6},{1... | collective-permute-start | bytes 196616 | tf_op jit(solution)/shard_map/ppermute | solution.py:38
  22.7 1.4 %collective-permute-start.9 = (bf16[2,32,512]{2,1,0:T(8,128)(2,1)S(1)}, bf16[2,32,512]{2,1,0:T(8,128)(2,1)S(1)}, u32[]{:S(2)}, u32[]{:S(2)}) collective-permute-start(bf16[2,32,512]{2,1,0:T(8,128)(2,1)S(1)} %get-tuple-element.21.half.rest_0_), channel_id=1, source_target_pairs={{0,3},{1,2},{2,1},{3,0},{4,7},{5,6},{6,5},{7,4},{8,11},{9,10},{10,... | collective-permute-start | bytes 196616 | tf_op jit(solution)/shard_map/ppermute | solution.py:38
  24.2 1.6 %collective-permute-done.8 = bf16[2,32,512]{2,1,0:T(8,128)(2,1)S(1)} collective-permute-done((bf16[2,32,512]{2,1,0:T(8,128)(2,1)S(1)}, bf16[2,32,512]{2,1,0:T(8,128)(2,1)S(1)}, u32[]{:S(2)}, u32[]{:S(2)}) %collective-permute-start.8) | collective-permute-done | bytes 65568 | tf_op jit(solution)/shard_map/ppermute | solution.py:38
  25.8 0.2 collective-permute-start.10
  26.0 0.7 %collective-permute-done.9.rest_1_ = bf16[2,32,512]{2,1,0:T(8,128)(2,1)S(1)} collective-permute-done((bf16[2,32,512]{2,1,0:T(8,128)(2,1)S(1)}, bf16[2,32,512]{2,1,0:T(8,128)(2,1)S(1)}, u32[]{:S(2)}, u32[]{:S(2)}) %collective-permute-start.9) | collective-permute-done | bytes 65568 | tf_op jit(solution)/shard_map/ppermute | solution.py:38
  26.6 0.5 %backward_second.1.part = f32[8,32,128]{2,1,0:T(8,128)S(1)} custom-call(s32[2,8]{1,0:T(2,128)S(1)} %bitcast.14, bf16[1,2,32,512]{3,2,1,0:T(8,128)(2,1)S(1)} %bitcast.9, bf16[8,2,1024,128]{3,2,1,0:T(8,128)(2,1)S(1)} %copy-done, f32[8,32,128]{2,1,0:T(8,128)S(1)} %backward_first.1.first, bf16[2,32,512]{2,1,0:T(8,128)(2,1)S(1)} %get-tuple-element.21.half.rest_0_, ...), custom_call_target="tpu_custom_call" | custom-call | flops 67108864 | bytes 2097152 | tf_op jit(solution)/shard_map/backward_second/pallas_call | solution.py:294
  27.2 1.3 %backward.1 = (f32[8,32,128]{2,1,0:T(8,128)}, f32[2,32,256]{2,1,0:T(8,128)}) custom-call(s32[2,8]{1,0:T(2,128)S(1)} %bitcast.15, f32[2,32,256]{2,1,0:T(8,128)S(1)} %get-tuple-element.19.full, bf16[8,32,128]{2,1,0:T(8,128)(2,1)S(1)} %get-tuple-element.20.solved, f32[8,32,128]{2,1,0:T(8,128)S(1)} %backward_second.1.part, ...), custom_call_target="tpu_custom_call" | custom-call | flops 134217728 | bytes 3145728 | tf_op jit(solution)/shard_map/backward/pallas_call | solution.py:305
  (20 shorter events, 0.4 us)
Async XLA Ops:
  0.6 3.2 %copy-start.2 = (bf16[2,1024,256]{2,1,0:T(8,128)(2,1)S(1)}, bf16[2,1024,256]{2,1,0:T(8,128)(2,1)}, u32[]{:S(2)}) copy-start(bf16[2,1024,256]{2,1,0:T(8,128)(2,1)} %lower) | copy-start | bytes 3145732
  3.3 1.2 %copy-start.1 = (bf16[2,1024,256]{2,1,0:T(8,128)(2,1)S(1)}, bf16[2,1024,256]{2,1,0:T(8,128)(2,1)}, u32[]{:S(2)}) copy-start(bf16[2,1024,256]{2,1,0:T(8,128)(2,1)} %upper.3) | copy-start | bytes 3145732
  3.3 1.5 %collective-permute-start = (bf16[2,32,1024]{2,1,0:T(8,128)(2,1)S(1)}, bf16[2,32,1024]{2,1,0:T(8,128)(2,1)S(1)}, u32[]{:S(2)}, u32[]{:S(2)}) collective-permute-start(bf16[2,32,1024]{2,1,0:T(8,128)(2,1)S(1)} %get-tuple-element.14), channel_id=1, source_target_pairs={{0,1},{1,0},{2,3},{3,2},{4,5},{5,4},{6,7},{7,6},{8,9},{9,8},{10,11... | collective-permute-start | bytes 393224 | tf_op jit(solution)/shard_map/ppermute | solution.py:38
  4.6 11.2 %copy-start.4 = (bf16[2,32,1024]{2,1,0:T(8,128)(2,1)S(1)}, bf16[2,32,1024]{2,1,0:T(8,128)(2,1)}, u32[]{:S(2)}) copy-start(bf16[2,32,1024]{2,1,0:T(8,128)(2,1)} %rhs.1) | copy-start | bytes 393220
  4.8 10.9 %collective-permute-start.1 = (bf16[3,1024,256]{2,1,0:T(8,128)(2,1)S(1)}, bf16[3,1024,256]{2,1,0:T(8,128)(2,1)S(1)}, u32[]{:S(2)}, u32[]{:S(2)}) collective-permute-start(bf16[3,1024,256]{2,1,0:T(8,128)(2,1)S(1)} %pad_maximum_fusion), channel_id=1, source_target_pairs={{0,1},{1,0},{2,3},{3,2},{4,5},{5,4},{6,7},{7,6},{8,9},{9,8},{10,11... | collective-permute-start | bytes 4718600 | tf_op jit(solution)/shard_map/ppermute | solution.py:38
  5.3 9.4 %collective-permute-start.2 = (bf16[32,1024]{1,0:T(8,128)(2,1)S(1)}, bf16[32,1024]{1,0:T(8,128)(2,1)S(1)}, u32[]{:S(2)}, u32[]{:S(2)}) collective-permute-start(bf16[32,1024]{1,0:T(8,128)(2,1)S(1)} %get-tuple-element.23), channel_id=1, source_target_pairs={{0,6},{1,7},{2,4},{3,5},{4,10},{5,11},{6,8},{7,9},{8,14},{9,15},{1... | collective-permute-start | bytes 196616 | tf_op jit(solution)/shard_map/ppermute | solution.py:38
  8.9 6.8 %collective-permute-start.3 = (bf16[32,1024]{1,0:T(8,128)(2,1)S(1)}, bf16[32,1024]{1,0:T(8,128)(2,1)S(1)}, u32[]{:S(2)}, u32[]{:S(2)}) collective-permute-start(bf16[32,1024]{1,0:T(8,128)(2,1)S(1)} %get-tuple-element.23), channel_id=1, source_target_pairs={{0,5},{1,4},{2,7},{3,6},{4,9},{5,8},{6,11},{7,10},{8,13},{9,12},{1... | collective-permute-start | bytes 196616 | tf_op jit(solution)/shard_map/ppermute | solution.py:38
  10.1 5.6 %collective-permute-start.4 = (bf16[32,1024]{1,0:T(8,128)(2,1)S(1)}, bf16[32,1024]{1,0:T(8,128)(2,1)S(1)}, u32[]{:S(2)}, u32[]{:S(2)}) collective-permute-start(bf16[32,1024]{1,0:T(8,128)(2,1)S(1)} %get-tuple-element.22), channel_id=1, source_target_pairs={{0,3},{1,2},{2,1},{3,0},{4,7},{5,6},{6,5},{7,4},{8,11},{9,10},{10,... | collective-permute-start | bytes 196616 | tf_op jit(solution)/shard_map/ppermute | solution.py:38
  16.0 3.5 %collective-permute-start.6 = (bf16[32,512]{1,0:T(8,128)(2,1)S(1)}, bf16[32,512]{1,0:T(8,128)(2,1)S(1)}, u32[]{:S(2)}, u32[]{:S(2)}) collective-permute-start(bf16[32,512]{1,0:T(8,128)(2,1)S(1)} %parent_forward.1.mine), channel_id=1, source_target_pairs={{0,3},{1,2},{2,1},{3,0},{4,7},{5,6},{6,5},{7,4},{8,11},{9,10},{10,... | collective-permute-start | bytes 98312 | tf_op jit(solution)/shard_map/ppermute | solution.py:38
  17.1 2.5 %collective-permute-start.5 = (bf16[32,512]{1,0:T(8,128)(2,1)S(1)}, bf16[32,512]{1,0:T(8,128)(2,1)S(1)}, u32[]{:S(2)}, u32[]{:S(2)}) collective-permute-start(bf16[32,512]{1,0:T(8,128)(2,1)S(1)} %parent_forward.1.mine), channel_id=1, source_target_pairs={{0,1},{1,0},{2,3},{3,2},{4,5},{5,4},{6,7},{7,6},{8,9},{9,8},{10,11... | collective-permute-start | bytes 98312 | tf_op jit(solution)/shard_map/ppermute | solution.py:38
  19.5 1.2 %collective-permute-start.7 = (bf16[1,32,512]{2,1,0:T(8,128)(2,1)S(1)}, bf16[1,32,512]{2,1,0:T(8,128)(2,1)S(1)}, u32[]{:S(2)}, u32[]{:S(2)}) collective-permute-start(bf16[1,32,512]{2,1,0:T(8,128)(2,1)S(1)} %bitcast.10), channel_id=1, source_target_pairs={{0,1},{1,0},{2,3},{3,2},{4,5},{5,4},{6,7},{7,6},{8,9},{9,8},{10,11... | collective-permute-start | bytes 98312 | tf_op jit(solution)/shard_map/ppermute | solution.py:38
  19.6 6.3 %copy-start = (bf16[8,2,1024,128]{3,2,1,0:T(8,128)(2,1)S(1)}, bf16[8,2,1024,128]{3,2,1,0:T(8,128)(2,1)}, u32[]{:S(2)}) copy-start(bf16[8,2,1024,128]{3,2,1,0:T(8,128)(2,1)} %blocks.5) | copy-start | bytes 12582916
  19.9 6.0 %copy-start.3 = (bf16[8,128,128]{2,1,0:T(8,128)(2,1)S(1)}, bf16[8,128,128]{2,1,0:T(8,128)(2,1)}, u32[]{:S(2)}) copy-start(bf16[8,128,128]{2,1,0:T(8,128)(2,1)} %upper.5) | copy-start | bytes 786436
  19.9 6.0 %copy-start.5 = (s32[8,2]{0,1:T(2,128)S(1)}, s32[8,2]{0,1:T(2,128)}, u32[]{:S(2)}) copy-start(s32[8,2]{0,1:T(2,128)} %param.17) | copy-start | bytes 196
  21.0 4.7 %collective-permute-start.8 = (bf16[2,32,512]{2,1,0:T(8,128)(2,1)S(1)}, bf16[2,32,512]{2,1,0:T(8,128)(2,1)S(1)}, u32[]{:S(2)}, u32[]{:S(2)}) collective-permute-start(bf16[2,32,512]{2,1,0:T(8,128)(2,1)S(1)} %get-tuple-element.21.half.rest_0_), channel_id=1, source_target_pairs={{0,29},{1,30},{2,31},{3,28},{4,1},{5,2},{6,3},{7,0},{8,5},{9,6},{1... | collective-permute-start | bytes 196616 | tf_op jit(solution)/shard_map/ppermute | solution.py:38
  22.7 3.9 %collective-permute-start.9 = (bf16[2,32,512]{2,1,0:T(8,128)(2,1)S(1)}, bf16[2,32,512]{2,1,0:T(8,128)(2,1)S(1)}, u32[]{:S(2)}, u32[]{:S(2)}) collective-permute-start(bf16[2,32,512]{2,1,0:T(8,128)(2,1)S(1)} %get-tuple-element.21.half.rest_0_), channel_id=1, source_target_pairs={{0,3},{1,2},{2,1},{3,0},{4,7},{5,6},{6,5},{7,4},{8,11},{9,10},{10,... | collective-permute-start | bytes 196616 | tf_op jit(solution)/shard_map/ppermute | solution.py:38
  25.8 1.4 %collective-permute-start.10 = (bf16[1,2,32,512]{3,2,1,0:T(8,128)(2,1)S(1)}, bf16[1,2,32,512]{3,2,1,0:T(8,128)(2,1)S(1)}, u32[]{:S(2)}, u32[]{:S(2)}) collective-permute-start(bf16[1,2,32,512]{3,2,1,0:T(8,128)(2,1)S(1)} %bitcast.7), channel_id=1, source_target_pairs={{0,1},{1,0},{2,3},{3,2},{4,5},{5,4},{6,7},{7,6},{8,9},{9,8},{10,11... | collective-permute-start | bytes 196616 | tf_op jit(solution)/shard_map/ppermute | solution.py:38

commit v9 on v8

--- a/solution.py
+++ b/solution.py
@@ -242,8 +242,9 @@
     across = go(across, by_row=0, target=along(0, 1))
     own_sum = (keep[0] + came[0].astype(F32)).astype(BF16)
     next_sum = (keep[1] + came[1].astype(F32)).astype(BF16)
-    sums = [go(next_sum, by_row=1, target=along(by, 1)) for by in reversed(range(chips))]
+    sums = [go(next_sum, by_row=1, target=along(by, 1)) for by in reversed(range(1, chips))]
     sums += [go(own_sum, by_row=0, target=along(by)) for by in range(1, chips)]
+    sums += [go(next_sum, by_row=1, target=along(0, 1))]
 
     half = pl.pallas_call(
         parent_forward_kernel,

time: 28.6 us -> 28.6 us (level)
  waiting for transfers between devices: 10.2 us -> 9.26 us
  starting transfers between devices: 11.3 us -> 12 us
    ppermute x11, waiting for transfers between devices: 10.2 us -> 9.26 us  [send(): return lax.ppermute(array, ('row', 'col'), pairs)]
    ppermute x11, starting transfers between devices: 11.3 us -> 12 us  [send(): return lax.ppermute(array, ('row', 'col'), pairs)]
where the time goes in v9:
time: 28.6 us; the launch traced here: 28.2 us
  starting transfers between devices  12 us (42%)
  waiting for transfers between devices  9.26 us (32%)
  Pallas kernels  5.36 us (19%)
  between operations  0.73 us (3%)
  local copies, waits for them, and re-layouts  0.72 us (3%)
    ppermute x11, starting transfers between devices, send(): return lax.ppermute(array, ('row', 'col'), pairs)  12 us
    ppermute x11, waiting for transfers between devices, send(): return lax.ppermute(array, ('row', 'col'), pairs)  9.26 us
    pallas_call x1, Pallas kernels, local(): pl.pallas_call(forward_kernel, in_specs=[HBM] * 4, out_specs=[VMEM] * 3,...  2.68 us
    pallas_call x1, Pallas kernels, local(): pl.pallas_call(backward_kernel, in_specs=[VMEM] * (7 + chips), out_specs=...  1.29 us
    unnamed x12, local copies, waits for them, and re-layouts  0.68 us
  transfers between devices with their start and end apart: 11, of which 7 were waited for; matrix products, arithmetic and copies ran while one was open for 1% of the time, Pallas kernels for 3%

profile of v9, /device:TPU:0, one launch (start us, length us, event | category | flops | bytes accessed | tf_op | source)
XLA Modules:
  0.0 28.2 jit_solution(4267426631848669342)
XLA Ops:
  0.6 2.7 %forward.1 = (bf16[8,32,128]{2,1,0:T(8,128)(2,1)S(1)}, f32[2,32,1024]{2,1,0:T(8,128)S(1)}, bf16[2,32,1024]{2,1,0:T(8,128)(2,1)S(1)}) custom-call(s32[2,8]{1,0:T(2,128)} %bitcast.12, bf16[8,32,128]{2,1,0:T(8,128)(2,1)} %rhs_hbm.1, bf16[8,128,128]{2,1,0:T(8,128)(2,1)} %lower_hbm.1, bf16[8,2,128,1024]{3,2,1,0:T(8,128)(2,1)} %blocks_hbm.1), custom_call_target="tpu_custom_call" | custom-call | flops 536870912 | bytes 5242880 | tf_op jit(solution)/shard_map/forward/pallas_call | solution.py:215
  3.3 0.5 %collective-permute-start = (bf16[2,32,1024]{2,1,0:T(8,128)(2,1)S(1)}, bf16[2,32,1024]{2,1,0:T(8,128)(2,1)S(1)}, u32[]{:S(2)}, u32[]{:S(2)}) collective-permute-start(bf16[2,32,1024]{2,1,0:T(8,128)(2,1)S(1)} %get-tuple-element.14), channel_id=1, source_target_pairs={{0,1},{1,0},{2,3},{3,2},{4,5},{5,4},{6,7},{7,6},{8,9},{9,8},{10,11... | collective-permute-start | bytes 393224 | tf_op jit(solution)/shard_map/ppermute | solution.py:38
  3.9 0.7 %copy-done.1 = bf16[2,1024,256]{2,1,0:T(8,128)(2,1)S(1)} copy-done((bf16[2,1024,256]{2,1,0:T(8,128)(2,1)S(1)}, bf16[2,1024,256]{2,1,0:T(8,128)(2,1)}, u32[]{:S(2)}) %copy-start.1) | copy-done | bytes 1048600
  4.8 0.4 %collective-permute-start.1 = (bf16[3,1024,256]{2,1,0:T(8,128)(2,1)S(1)}, bf16[3,1024,256]{2,1,0:T(8,128)(2,1)S(1)}, u32[]{:S(2)}, u32[]{:S(2)}) collective-permute-start(bf16[3,1024,256]{2,1,0:T(8,128)(2,1)S(1)} %pad_maximum_fusion), channel_id=1, source_target_pairs={{0,1},{1,0},{2,3},{3,2},{4,5},{5,4},{6,7},{7,6},{8,9},{9,8},{10,11... | collective-permute-start | bytes 4718600 | tf_op jit(solution)/shard_map/ppermute | solution.py:38
  5.3 3.6 %collective-permute-start.2 = (bf16[32,1024]{1,0:T(8,128)(2,1)S(1)}, bf16[32,1024]{1,0:T(8,128)(2,1)S(1)}, u32[]{:S(2)}, u32[]{:S(2)}) collective-permute-start(bf16[32,1024]{1,0:T(8,128)(2,1)S(1)} %get-tuple-element.23), channel_id=1, source_target_pairs={{0,6},{1,7},{2,4},{3,5},{4,10},{5,11},{6,8},{7,9},{8,14},{9,15},{1... | collective-permute-start | bytes 196616 | tf_op jit(solution)/shard_map/ppermute | solution.py:38
  8.9 0.2 collective-permute-start.3
  9.1 1.6 %collective-permute-start.4 = (bf16[32,1024]{1,0:T(8,128)(2,1)S(1)}, bf16[32,1024]{1,0:T(8,128)(2,1)S(1)}, u32[]{:S(2)}, u32[]{:S(2)}) collective-permute-start(bf16[32,1024]{1,0:T(8,128)(2,1)S(1)} %get-tuple-element.23), channel_id=1, source_target_pairs={{0,5},{1,4},{2,7},{3,6},{4,9},{5,8},{6,11},{7,10},{8,13},{9,12},{1... | collective-permute-start | bytes 196616 | tf_op jit(solution)/shard_map/ppermute | solution.py:38
  10.7 4.0 %collective-permute-done.2.rest_0_ = bf16[32,1024]{1,0:T(8,128)(2,1)S(1)} collective-permute-done((bf16[32,1024]{1,0:T(8,128)(2,1)S(1)}, bf16[32,1024]{1,0:T(8,128)(2,1)S(1)}, u32[]{:S(2)}, u32[]{:S(2)}) %collective-permute-start.2) | collective-permute-done | bytes 65568 | tf_op jit(solution)/shard_map/ppermute | solution.py:38
  14.7 1.0 %collective-permute-done.4.rest_2_ = bf16[32,1024]{1,0:T(8,128)(2,1)S(1)} collective-permute-done((bf16[32,1024]{1,0:T(8,128)(2,1)S(1)}, bf16[32,1024]{1,0:T(8,128)(2,1)S(1)}, u32[]{:S(2)}, u32[]{:S(2)}) %collective-permute-start.4) | collective-permute-done | bytes 65568 | tf_op jit(solution)/shard_map/ppermute | solution.py:38
  15.6 0.3 parent_forward.1.mine
  15.9 1.6 %collective-permute-start.6 = (bf16[32,512]{1,0:T(8,128)(2,1)S(1)}, bf16[32,512]{1,0:T(8,128)(2,1)S(1)}, u32[]{:S(2)}, u32[]{:S(2)}) collective-permute-start(bf16[32,512]{1,0:T(8,128)(2,1)S(1)} %parent_forward.1.mine), channel_id=1, source_target_pairs={{0,3},{1,2},{2,1},{3,0},{4,7},{5,6},{6,5},{7,4},{8,11},{9,10},{10,... | collective-permute-start | bytes 98312 | tf_op jit(solution)/shard_map/ppermute | solution.py:38
  17.5 0.1 collective-permute-start.5
  17.6 1.7 %collective-permute-done.6 = bf16[32,512]{1,0:T(8,128)(2,1)S(1)} collective-permute-done((bf16[32,512]{1,0:T(8,128)(2,1)S(1)}, bf16[32,512]{1,0:T(8,128)(2,1)S(1)}, u32[]{:S(2)}, u32[]{:S(2)}) %collective-permute-start.6) | collective-permute-done | bytes 32800 | tf_op jit(solution)/shard_map/ppermute | solution.py:38
  19.4 0.4 %collective-permute-start.7 = (bf16[1,32,512]{2,1,0:T(8,128)(2,1)S(1)}, bf16[1,32,512]{2,1,0:T(8,128)(2,1)S(1)}, u32[]{:S(2)}, u32[]{:S(2)}) collective-permute-start(bf16[1,32,512]{2,1,0:T(8,128)(2,1)S(1)} %bitcast.10), channel_id=1, source_target_pairs={{0,1},{1,0},{2,3},{3,2},{4,5},{5,4},{6,7},{7,6},{8,9},{9,8},{10,11... | collective-permute-start | bytes 98312 | tf_op jit(solution)/shard_map/ppermute | solution.py:38
  19.7 0.3 %parent_early.1.part = f32[2,32,512]{2,1,0:T(8,128)S(1)} custom-call(bf16[32,512]{1,0:T(8,128)(2,1)S(1)} %parent_forward.1.mine, bf16[32,512]{1,0:T(8,128)(2,1)S(1)} %collective-permute-done.5.theirs, bf16[2,1024,256]{2,1,0:T(8,128)(2,1)S(1)} %copy-done.1, bf16[3,1024,256]{2,1,0:T(8,128)(2,1)S(1)} %collective-permute-done.1.across), custom_call_target="tpu_custom_call" | custom-call | flops 67108864 | bytes 2097152 | tf_op jit(solution)/shard_map/parent_early/pallas_call | solution.py:260
  20.0 0.6 %collective-permute-done.7.theirs = bf16[1,32,512]{2,1,0:T(8,128)(2,1)S(1)} collective-permute-done((bf16[1,32,512]{2,1,0:T(8,128)(2,1)S(1)}, bf16[1,32,512]{2,1,0:T(8,128)(2,1)S(1)}, u32[]{:S(2)}, u32[]{:S(2)}) %collective-permute-start.7) | collective-permute-done | bytes 32800 | tf_op jit(solution)/shard_map/ppermute | solution.py:38
  20.6 0.3 %parent_backward.1 = (f32[2,32,256]{2,1,0:T(8,128)S(1)}, bf16[2,32,512]{2,1,0:T(8,128)(2,1)S(1)}) custom-call(f32[2,32,512]{2,1,0:T(8,128)S(1)} %parent_early.1.part, bf16[1,32,512]{2,1,0:T(8,128)(2,1)S(1)} %bitcast.11, bf16[1,32,512]{2,1,0:T(8,128)(2,1)S(1)} %collective-permute-done.7.theirs, bf16[2,1024,256]{2,1,0:T(8,128)(2,1)S(1)} %copy-done.1, ...), custom_call_target="tpu_custom_call" | custom-call | flops 67108864 | bytes 2097152 | tf_op jit(solution)/shard_map/parent_backward/pallas_call | solution.py:271
  20.9 1.8 %collective-permute-start.8 = (bf16[2,32,512]{2,1,0:T(8,128)(2,1)S(1)}, bf16[2,32,512]{2,1,0:T(8,128)(2,1)S(1)}, u32[]{:S(2)}, u32[]{:S(2)}) collective-permute-start(bf16[2,32,512]{2,1,0:T(8,128)(2,1)S(1)} %get-tuple-element.21.half.rest_0_), channel_id=1, source_target_pairs={{0,29},{1,30},{2,31},{3,28},{4,1},{5,2},{6,3},{7,0},{8,5},{9,6},{1... | collective-permute-start | bytes 196616 | tf_op jit(solution)/shard_map/ppermute | solution.py:38
  22.7 1.4 %collective-permute-start.9 = (bf16[2,32,512]{2,1,0:T(8,128)(2,1)S(1)}, bf16[2,32,512]{2,1,0:T(8,128)(2,1)S(1)}, u32[]{:S(2)}, u32[]{:S(2)}) collective-permute-start(bf16[2,32,512]{2,1,0:T(8,128)(2,1)S(1)} %get-tuple-element.21.half.rest_0_), channel_id=1, source_target_pairs={{0,3},{1,2},{2,1},{3,0},{4,7},{5,6},{6,5},{7,4},{8,11},{9,10},{10,... | collective-permute-start | bytes 196616 | tf_op jit(solution)/shard_map/ppermute | solution.py:38
  24.2 1.5 %collective-permute-done.8 = bf16[2,32,512]{2,1,0:T(8,128)(2,1)S(1)} collective-permute-done((bf16[2,32,512]{2,1,0:T(8,128)(2,1)S(1)}, bf16[2,32,512]{2,1,0:T(8,128)(2,1)S(1)}, u32[]{:S(2)}, u32[]{:S(2)}) %collective-permute-start.8) | collective-permute-done | bytes 65568 | tf_op jit(solution)/shard_map/ppermute | solution.py:38
  25.6 0.3 %collective-permute-start.10 = (bf16[1,2,32,512]{3,2,1,0:T(8,128)(2,1)S(1)}, bf16[1,2,32,512]{3,2,1,0:T(8,128)(2,1)S(1)}, u32[]{:S(2)}, u32[]{:S(2)}) collective-permute-start(bf16[1,2,32,512]{3,2,1,0:T(8,128)(2,1)S(1)} %bitcast.7), channel_id=1, source_target_pairs={{0,1},{1,0},{2,3},{3,2},{4,5},{5,4},{6,7},{7,6},{8,9},{9,8},{10,11... | collective-permute-start | bytes 196616 | tf_op jit(solution)/shard_map/ppermute | solution.py:38
  26.0 0.4 %collective-permute-done.9.rest_1_ = bf16[2,32,512]{2,1,0:T(8,128)(2,1)S(1)} collective-permute-done((bf16[2,32,512]{2,1,0:T(8,128)(2,1)S(1)}, bf16[2,32,512]{2,1,0:T(8,128)(2,1)S(1)}, u32[]{:S(2)}, u32[]{:S(2)}) %collective-permute-start.9) | collective-permute-done | bytes 65568 | tf_op jit(solution)/shard_map/ppermute | solution.py:38
  26.4 0.5 %backward_second.1.part = f32[8,32,128]{2,1,0:T(8,128)S(1)} custom-call(s32[2,8]{1,0:T(2,128)S(1)} %bitcast.14, bf16[1,2,32,512]{3,2,1,0:T(8,128)(2,1)S(1)} %bitcast.9, bf16[8,2,1024,128]{3,2,1,0:T(8,128)(2,1)S(1)} %copy-done, f32[8,32,128]{2,1,0:T(8,128)S(1)} %backward_first.1.first, bf16[2,32,512]{2,1,0:T(8,128)(2,1)S(1)} %get-tuple-element.21.half.rest_0_, ...), custom_call_target="tpu_custom_call" | custom-call | flops 67108864 | bytes 2097152 | tf_op jit(solution)/shard_map/backward_second/pallas_call | solution.py:295
  27.0 1.3 %backward.1 = (f32[8,32,128]{2,1,0:T(8,128)}, f32[2,32,256]{2,1,0:T(8,128)}) custom-call(s32[2,8]{1,0:T(2,128)S(1)} %bitcast.15, f32[2,32,256]{2,1,0:T(8,128)S(1)} %get-tuple-element.19.full, bf16[8,32,128]{2,1,0:T(8,128)(2,1)S(1)} %get-tuple-element.20.solved, f32[8,32,128]{2,1,0:T(8,128)S(1)} %backward_second.1.part, ...), custom_call_target="tpu_custom_call" | custom-call | flops 134217728 | bytes 3145728 | tf_op jit(solution)/shard_map/backward/pallas_call | solution.py:306
  (20 shorter events, 0.4 us)
Async XLA Ops:
  0.6 3.2 %copy-start.2 = (bf16[2,1024,256]{2,1,0:T(8,128)(2,1)S(1)}, bf16[2,1024,256]{2,1,0:T(8,128)(2,1)}, u32[]{:S(2)}) copy-start(bf16[2,1024,256]{2,1,0:T(8,128)(2,1)} %lower) | copy-start | bytes 3145732
  3.3 1.2 %copy-start.1 = (bf16[2,1024,256]{2,1,0:T(8,128)(2,1)S(1)}, bf16[2,1024,256]{2,1,0:T(8,128)(2,1)}, u32[]{:S(2)}) copy-start(bf16[2,1024,256]{2,1,0:T(8,128)(2,1)} %upper.3) | copy-start | bytes 3145732
  3.3 1.5 %collective-permute-start = (bf16[2,32,1024]{2,1,0:T(8,128)(2,1)S(1)}, bf16[2,32,1024]{2,1,0:T(8,128)(2,1)S(1)}, u32[]{:S(2)}, u32[]{:S(2)}) collective-permute-start(bf16[2,32,1024]{2,1,0:T(8,128)(2,1)S(1)} %get-tuple-element.14), channel_id=1, source_target_pairs={{0,1},{1,0},{2,3},{3,2},{4,5},{5,4},{6,7},{7,6},{8,9},{9,8},{10,11... | collective-permute-start | bytes 393224 | tf_op jit(solution)/shard_map/ppermute | solution.py:38
  4.6 11.1 %copy-start.4 = (bf16[2,32,1024]{2,1,0:T(8,128)(2,1)S(1)}, bf16[2,32,1024]{2,1,0:T(8,128)(2,1)}, u32[]{:S(2)}) copy-start(bf16[2,32,1024]{2,1,0:T(8,128)(2,1)} %rhs.1) | copy-start | bytes 393220
  4.8 10.8 %collective-permute-start.1 = (bf16[3,1024,256]{2,1,0:T(8,128)(2,1)S(1)}, bf16[3,1024,256]{2,1,0:T(8,128)(2,1)S(1)}, u32[]{:S(2)}, u32[]{:S(2)}) collective-permute-start(bf16[3,1024,256]{2,1,0:T(8,128)(2,1)S(1)} %pad_maximum_fusion), channel_id=1, source_target_pairs={{0,1},{1,0},{2,3},{3,2},{4,5},{5,4},{6,7},{7,6},{8,9},{9,8},{10,11... | collective-permute-start | bytes 4718600 | tf_op jit(solution)/shard_map/ppermute | solution.py:38
  5.3 9.4 %collective-permute-start.2 = (bf16[32,1024]{1,0:T(8,128)(2,1)S(1)}, bf16[32,1024]{1,0:T(8,128)(2,1)S(1)}, u32[]{:S(2)}, u32[]{:S(2)}) collective-permute-start(bf16[32,1024]{1,0:T(8,128)(2,1)S(1)} %get-tuple-element.23), channel_id=1, source_target_pairs={{0,6},{1,7},{2,4},{3,5},{4,10},{5,11},{6,8},{7,9},{8,14},{9,15},{1... | collective-permute-start | bytes 196616 | tf_op jit(solution)/shard_map/ppermute | solution.py:38
  8.9 5.8 %collective-permute-start.3 = (bf16[32,1024]{1,0:T(8,128)(2,1)S(1)}, bf16[32,1024]{1,0:T(8,128)(2,1)S(1)}, u32[]{:S(2)}, u32[]{:S(2)}) collective-permute-start(bf16[32,1024]{1,0:T(8,128)(2,1)S(1)} %get-tuple-element.22), channel_id=1, source_target_pairs={{0,3},{1,2},{2,1},{3,0},{4,7},{5,6},{6,5},{7,4},{8,11},{9,10},{10,... | collective-permute-start | bytes 196616 | tf_op jit(solution)/shard_map/ppermute | solution.py:38
  9.1 6.5 %collective-permute-start.4 = (bf16[32,1024]{1,0:T(8,128)(2,1)S(1)}, bf16[32,1024]{1,0:T(8,128)(2,1)S(1)}, u32[]{:S(2)}, u32[]{:S(2)}) collective-permute-start(bf16[32,1024]{1,0:T(8,128)(2,1)S(1)} %get-tuple-element.23), channel_id=1, source_target_pairs={{0,5},{1,4},{2,7},{3,6},{4,9},{5,8},{6,11},{7,10},{8,13},{9,12},{1... | collective-permute-start | bytes 196616 | tf_op jit(solution)/shard_map/ppermute | solution.py:38
  15.9 3.4 %collective-permute-start.6 = (bf16[32,512]{1,0:T(8,128)(2,1)S(1)}, bf16[32,512]{1,0:T(8,128)(2,1)S(1)}, u32[]{:S(2)}, u32[]{:S(2)}) collective-permute-start(bf16[32,512]{1,0:T(8,128)(2,1)S(1)} %parent_forward.1.mine), channel_id=1, source_target_pairs={{0,3},{1,2},{2,1},{3,0},{4,7},{5,6},{6,5},{7,4},{8,11},{9,10},{10,... | collective-permute-start | bytes 98312 | tf_op jit(solution)/shard_map/ppermute | solution.py:38
  17.5 2.2 %collective-permute-start.5 = (bf16[32,512]{1,0:T(8,128)(2,1)S(1)}, bf16[32,512]{1,0:T(8,128)(2,1)S(1)}, u32[]{:S(2)}, u32[]{:S(2)}) collective-permute-start(bf16[32,512]{1,0:T(8,128)(2,1)S(1)} %parent_forward.1.mine), channel_id=1, source_target_pairs={{0,1},{1,0},{2,3},{3,2},{4,5},{5,4},{6,7},{7,6},{8,9},{9,8},{10,11... | collective-permute-start | bytes 98312 | tf_op jit(solution)/shard_map/ppermute | solution.py:38
  19.4 1.2 %collective-permute-start.7 = (bf16[1,32,512]{2,1,0:T(8,128)(2,1)S(1)}, bf16[1,32,512]{2,1,0:T(8,128)(2,1)S(1)}, u32[]{:S(2)}, u32[]{:S(2)}) collective-permute-start(bf16[1,32,512]{2,1,0:T(8,128)(2,1)S(1)} %bitcast.10), channel_id=1, source_target_pairs={{0,1},{1,0},{2,3},{3,2},{4,5},{5,4},{6,7},{7,6},{8,9},{9,8},{10,11... | collective-permute-start | bytes 98312 | tf_op jit(solution)/shard_map/ppermute | solution.py:38
  19.7 6.3 %copy-start = (bf16[8,2,1024,128]{3,2,1,0:T(8,128)(2,1)S(1)}, bf16[8,2,1024,128]{3,2,1,0:T(8,128)(2,1)}, u32[]{:S(2)}) copy-start(bf16[8,2,1024,128]{3,2,1,0:T(8,128)(2,1)} %blocks.5) | copy-start | bytes 12582916
  20.0 6.0 %copy-start.3 = (bf16[8,128,128]{2,1,0:T(8,128)(2,1)S(1)}, bf16[8,128,128]{2,1,0:T(8,128)(2,1)}, u32[]{:S(2)}) copy-start(bf16[8,128,128]{2,1,0:T(8,128)(2,1)} %upper.5) | copy-start | bytes 786436
  20.0 6.0 %copy-start.5 = (s32[8,2]{0,1:T(2,128)S(1)}, s32[8,2]{0,1:T(2,128)}, u32[]{:S(2)}) copy-start(s32[8,2]{0,1:T(2,128)} %param.17) | copy-start | bytes 196
  20.9 4.7 %collective-permute-start.8 = (bf16[2,32,512]{2,1,0:T(8,128)(2,1)S(1)}, bf16[2,32,512]{2,1,0:T(8,128)(2,1)S(1)}, u32[]{:S(2)}, u32[]{:S(2)}) collective-permute-start(bf16[2,32,512]{2,1,0:T(8,128)(2,1)S(1)} %get-tuple-element.21.half.rest_0_), channel_id=1, source_target_pairs={{0,29},{1,30},{2,31},{3,28},{4,1},{5,2},{6,3},{7,0},{8,5},{9,6},{1... | collective-permute-start | bytes 196616 | tf_op jit(solution)/shard_map/ppermute | solution.py:38
  22.7 3.7 %collective-permute-start.9 = (bf16[2,32,512]{2,1,0:T(8,128)(2,1)S(1)}, bf16[2,32,512]{2,1,0:T(8,128)(2,1)S(1)}, u32[]{:S(2)}, u32[]{:S(2)}) collective-permute-start(bf16[2,32,512]{2,1,0:T(8,128)(2,1)S(1)} %get-tuple-element.21.half.rest_0_), channel_id=1, source_target_pairs={{0,3},{1,2},{2,1},{3,0},{4,7},{5,6},{6,5},{7,4},{8,11},{9,10},{10,... | collective-permute-start | bytes 196616 | tf_op jit(solution)/shard_map/ppermute | solution.py:38
  25.6 1.3 %collective-permute-start.10 = (bf16[1,2,32,512]{3,2,1,0:T(8,128)(2,1)S(1)}, bf16[1,2,32,512]{3,2,1,0:T(8,128)(2,1)S(1)}, u32[]{:S(2)}, u32[]{:S(2)}) collective-permute-start(bf16[1,2,32,512]{3,2,1,0:T(8,128)(2,1)S(1)} %bitcast.7), channel_id=1, source_target_pairs={{0,1},{1,0},{2,3},{3,2},{4,5},{5,4},{6,7},{7,6},{8,9},{9,8},{10,11... | collective-permute-start | bytes 196616 | tf_op jit(solution)/shard_map/ppermute | solution.py:38

commit v10 on v9

--- a/solution.py
+++ b/solution.py
@@ -134,10 +134,9 @@
 def fill_window(window, halves, nexts, lag):
     chip, _, _ = place()
     chips, depth = len(halves), halves[0].shape[2]
-    for by, half in enumerate(halves):
-        window[pl.ds(0, 2), :, columns(lax.rem(chip + chips - by, chips), depth)] = half[...]
     parts = [columns(lax.rem(chip + chips - by - lag, chips), depth) for by in range(0, chips, CORES)]
     for i, at in enumerate(parts):
+        window[pl.ds(0, 2), :, at] = jnp.where(lag == 0, halves[CORES * i][...], halves[CORES * i + 1][...])
         window[pl.ds(2, 2), :, at] = nexts[i]
     return parts
 

time: 28.6 us -> 28.6 us (level)
  no operation moved by 1% of the time
where the time goes in v10:
time: 28.6 us; the launch traced here: 28.2 us
  starting transfers between devices  12 us (42%)
  waiting for transfers between devices  9.26 us (32%)
  Pallas kernels  5.36 us (19%)
  between operations  0.73 us (3%)
  local copies, waits for them, and re-layouts  0.72 us (3%)
    ppermute x11, starting transfers between devices, send(): return lax.ppermute(array, ('row', 'col'), pairs)  12 us
    ppermute x11, waiting for transfers between devices, send(): return lax.ppermute(array, ('row', 'col'), pairs)  9.26 us
    pallas_call x1, Pallas kernels, local(): pl.pallas_call(forward_kernel, in_specs=[HBM] * 4, out_specs=[VMEM] * 3,...  2.68 us
    pallas_call x1, Pallas kernels, local(): pl.pallas_call(backward_kernel, in_specs=[VMEM] * (7 + chips), out_specs=...  1.29 us
    unnamed x12, local copies, waits for them, and re-layouts  0.68 us
  transfers between devices with their start and end apart: 11, of which 7 were waited for; matrix products, arithmetic and copies ran while one was open for 1% of the time, Pallas kernels for 3%

profile of v10, /device:TPU:0, one launch (start us, length us, event | category | flops | bytes accessed | tf_op | source)
XLA Modules:
  0.0 28.2 jit_solution(4183435777171649482)
XLA Ops:
  0.6 2.7 %forward.1 = (bf16[8,32,128]{2,1,0:T(8,128)(2,1)S(1)}, f32[2,32,1024]{2,1,0:T(8,128)S(1)}, bf16[2,32,1024]{2,1,0:T(8,128)(2,1)S(1)}) custom-call(s32[2,8]{1,0:T(2,128)} %bitcast.12, bf16[8,32,128]{2,1,0:T(8,128)(2,1)} %rhs_hbm.1, bf16[8,128,128]{2,1,0:T(8,128)(2,1)} %lower_hbm.1, bf16[8,2,128,1024]{3,2,1,0:T(8,128)(2,1)} %blocks_hbm.1), custom_call_target="tpu_custom_call" | custom-call | flops 536870912 | bytes 5242880 | tf_op jit(solution)/shard_map/forward/pallas_call | solution.py:214
  3.3 0.5 %collective-permute-start = (bf16[2,32,1024]{2,1,0:T(8,128)(2,1)S(1)}, bf16[2,32,1024]{2,1,0:T(8,128)(2,1)S(1)}, u32[]{:S(2)}, u32[]{:S(2)}) collective-permute-start(bf16[2,32,1024]{2,1,0:T(8,128)(2,1)S(1)} %get-tuple-element.14), channel_id=1, source_target_pairs={{0,1},{1,0},{2,3},{3,2},{4,5},{5,4},{6,7},{7,6},{8,9},{9,8},{10,11... | collective-permute-start | bytes 393224 | tf_op jit(solution)/shard_map/ppermute | solution.py:38
  3.9 0.7 %copy-done.1 = bf16[2,1024,256]{2,1,0:T(8,128)(2,1)S(1)} copy-done((bf16[2,1024,256]{2,1,0:T(8,128)(2,1)S(1)}, bf16[2,1024,256]{2,1,0:T(8,128)(2,1)}, u32[]{:S(2)}) %copy-start.1) | copy-done | bytes 1048600
  4.8 0.4 %collective-permute-start.1 = (bf16[3,1024,256]{2,1,0:T(8,128)(2,1)S(1)}, bf16[3,1024,256]{2,1,0:T(8,128)(2,1)S(1)}, u32[]{:S(2)}, u32[]{:S(2)}) collective-permute-start(bf16[3,1024,256]{2,1,0:T(8,128)(2,1)S(1)} %pad_maximum_fusion), channel_id=1, source_target_pairs={{0,1},{1,0},{2,3},{3,2},{4,5},{5,4},{6,7},{7,6},{8,9},{9,8},{10,11... | collective-permute-start | bytes 4718600 | tf_op jit(solution)/shard_map/ppermute | solution.py:38
  5.3 3.6 %collective-permute-start.2 = (bf16[32,1024]{1,0:T(8,128)(2,1)S(1)}, bf16[32,1024]{1,0:T(8,128)(2,1)S(1)}, u32[]{:S(2)}, u32[]{:S(2)}) collective-permute-start(bf16[32,1024]{1,0:T(8,128)(2,1)S(1)} %get-tuple-element.23), channel_id=1, source_target_pairs={{0,6},{1,7},{2,4},{3,5},{4,10},{5,11},{6,8},{7,9},{8,14},{9,15},{1... | collective-permute-start | bytes 196616 | tf_op jit(solution)/shard_map/ppermute | solution.py:38
  8.9 0.2 collective-permute-start.3
  9.1 1.6 %collective-permute-start.4 = (bf16[32,1024]{1,0:T(8,128)(2,1)S(1)}, bf16[32,1024]{1,0:T(8,128)(2,1)S(1)}, u32[]{:S(2)}, u32[]{:S(2)}) collective-permute-start(bf16[32,1024]{1,0:T(8,128)(2,1)S(1)} %get-tuple-element.23), channel_id=1, source_target_pairs={{0,5},{1,4},{2,7},{3,6},{4,9},{5,8},{6,11},{7,10},{8,13},{9,12},{1... | collective-permute-start | bytes 196616 | tf_op jit(solution)/shard_map/ppermute | solution.py:38
  10.7 4.0 %collective-permute-done.2.rest_0_ = bf16[32,1024]{1,0:T(8,128)(2,1)S(1)} collective-permute-done((bf16[32,1024]{1,0:T(8,128)(2,1)S(1)}, bf16[32,1024]{1,0:T(8,128)(2,1)S(1)}, u32[]{:S(2)}, u32[]{:S(2)}) %collective-permute-start.2) | collective-permute-done | bytes 65568 | tf_op jit(solution)/shard_map/ppermute | solution.py:38
  14.7 1.0 %collective-permute-done.4.rest_2_ = bf16[32,1024]{1,0:T(8,128)(2,1)S(1)} collective-permute-done((bf16[32,1024]{1,0:T(8,128)(2,1)S(1)}, bf16[32,1024]{1,0:T(8,128)(2,1)S(1)}, u32[]{:S(2)}, u32[]{:S(2)}) %collective-permute-start.4) | collective-permute-done | bytes 65568 | tf_op jit(solution)/shard_map/ppermute | solution.py:38
  15.6 0.3 parent_forward.1.mine
  15.9 1.6 %collective-permute-start.6 = (bf16[32,512]{1,0:T(8,128)(2,1)S(1)}, bf16[32,512]{1,0:T(8,128)(2,1)S(1)}, u32[]{:S(2)}, u32[]{:S(2)}) collective-permute-start(bf16[32,512]{1,0:T(8,128)(2,1)S(1)} %parent_forward.1.mine), channel_id=1, source_target_pairs={{0,3},{1,2},{2,1},{3,0},{4,7},{5,6},{6,5},{7,4},{8,11},{9,10},{10,... | collective-permute-start | bytes 98312 | tf_op jit(solution)/shard_map/ppermute | solution.py:38
  17.5 0.1 collective-permute-start.5
  17.6 1.7 %collective-permute-done.6 = bf16[32,512]{1,0:T(8,128)(2,1)S(1)} collective-permute-done((bf16[32,512]{1,0:T(8,128)(2,1)S(1)}, bf16[32,512]{1,0:T(8,128)(2,1)S(1)}, u32[]{:S(2)}, u32[]{:S(2)}) %collective-permute-start.6) | collective-permute-done | bytes 32800 | tf_op jit(solution)/shard_map/ppermute | solution.py:38
  19.4 0.4 %collective-permute-start.7 = (bf16[1,32,512]{2,1,0:T(8,128)(2,1)S(1)}, bf16[1,32,512]{2,1,0:T(8,128)(2,1)S(1)}, u32[]{:S(2)}, u32[]{:S(2)}) collective-permute-start(bf16[1,32,512]{2,1,0:T(8,128)(2,1)S(1)} %bitcast.10), channel_id=1, source_target_pairs={{0,1},{1,0},{2,3},{3,2},{4,5},{5,4},{6,7},{7,6},{8,9},{9,8},{10,11... | collective-permute-start | bytes 98312 | tf_op jit(solution)/shard_map/ppermute | solution.py:38
  19.7 0.3 %parent_early.1.part = f32[2,32,512]{2,1,0:T(8,128)S(1)} custom-call(bf16[32,512]{1,0:T(8,128)(2,1)S(1)} %parent_forward.1.mine, bf16[32,512]{1,0:T(8,128)(2,1)S(1)} %collective-permute-done.5.theirs, bf16[2,1024,256]{2,1,0:T(8,128)(2,1)S(1)} %copy-done.1, bf16[3,1024,256]{2,1,0:T(8,128)(2,1)S(1)} %collective-permute-done.1.across), custom_call_target="tpu_custom_call" | custom-call | flops 67108864 | bytes 2097152 | tf_op jit(solution)/shard_map/parent_early/pallas_call | solution.py:259
  20.0 0.6 %collective-permute-done.7.theirs = bf16[1,32,512]{2,1,0:T(8,128)(2,1)S(1)} collective-permute-done((bf16[1,32,512]{2,1,0:T(8,128)(2,1)S(1)}, bf16[1,32,512]{2,1,0:T(8,128)(2,1)S(1)}, u32[]{:S(2)}, u32[]{:S(2)}) %collective-permute-start.7) | collective-permute-done | bytes 32800 | tf_op jit(solution)/shard_map/ppermute | solution.py:38
  20.6 0.3 %parent_backward.1 = (f32[2,32,256]{2,1,0:T(8,128)S(1)}, bf16[2,32,512]{2,1,0:T(8,128)(2,1)S(1)}) custom-call(f32[2,32,512]{2,1,0:T(8,128)S(1)} %parent_early.1.part, bf16[1,32,512]{2,1,0:T(8,128)(2,1)S(1)} %bitcast.11, bf16[1,32,512]{2,1,0:T(8,128)(2,1)S(1)} %collective-permute-done.7.theirs, bf16[2,1024,256]{2,1,0:T(8,128)(2,1)S(1)} %copy-done.1, ...), custom_call_target="tpu_custom_call" | custom-call | flops 67108864 | bytes 2097152 | tf_op jit(solution)/shard_map/parent_backward/pallas_call | solution.py:270
  20.9 1.8 %collective-permute-start.8 = (bf16[2,32,512]{2,1,0:T(8,128)(2,1)S(1)}, bf16[2,32,512]{2,1,0:T(8,128)(2,1)S(1)}, u32[]{:S(2)}, u32[]{:S(2)}) collective-permute-start(bf16[2,32,512]{2,1,0:T(8,128)(2,1)S(1)} %get-tuple-element.21.half.rest_0_), channel_id=1, source_target_pairs={{0,29},{1,30},{2,31},{3,28},{4,1},{5,2},{6,3},{7,0},{8,5},{9,6},{1... | collective-permute-start | bytes 196616 | tf_op jit(solution)/shard_map/ppermute | solution.py:38
  22.7 1.4 %collective-permute-start.9 = (bf16[2,32,512]{2,1,0:T(8,128)(2,1)S(1)}, bf16[2,32,512]{2,1,0:T(8,128)(2,1)S(1)}, u32[]{:S(2)}, u32[]{:S(2)}) collective-permute-start(bf16[2,32,512]{2,1,0:T(8,128)(2,1)S(1)} %get-tuple-element.21.half.rest_0_), channel_id=1, source_target_pairs={{0,3},{1,2},{2,1},{3,0},{4,7},{5,6},{6,5},{7,4},{8,11},{9,10},{10,... | collective-permute-start | bytes 196616 | tf_op jit(solution)/shard_map/ppermute | solution.py:38
  24.2 1.5 %collective-permute-done.8 = bf16[2,32,512]{2,1,0:T(8,128)(2,1)S(1)} collective-permute-done((bf16[2,32,512]{2,1,0:T(8,128)(2,1)S(1)}, bf16[2,32,512]{2,1,0:T(8,128)(2,1)S(1)}, u32[]{:S(2)}, u32[]{:S(2)}) %collective-permute-start.8) | collective-permute-done | bytes 65568 | tf_op jit(solution)/shard_map/ppermute | solution.py:38
  25.6 0.3 %collective-permute-start.10 = (bf16[1,2,32,512]{3,2,1,0:T(8,128)(2,1)S(1)}, bf16[1,2,32,512]{3,2,1,0:T(8,128)(2,1)S(1)}, u32[]{:S(2)}, u32[]{:S(2)}) collective-permute-start(bf16[1,2,32,512]{3,2,1,0:T(8,128)(2,1)S(1)} %bitcast.7), channel_id=1, source_target_pairs={{0,1},{1,0},{2,3},{3,2},{4,5},{5,4},{6,7},{7,6},{8,9},{9,8},{10,11... | collective-permute-start | bytes 196616 | tf_op jit(solution)/shard_map/ppermute | solution.py:38
  26.0 0.4 %collective-permute-done.9.rest_1_ = bf16[2,32,512]{2,1,0:T(8,128)(2,1)S(1)} collective-permute-done((bf16[2,32,512]{2,1,0:T(8,128)(2,1)S(1)}, bf16[2,32,512]{2,1,0:T(8,128)(2,1)S(1)}, u32[]{:S(2)}, u32[]{:S(2)}) %collective-permute-start.9) | collective-permute-done | bytes 65568 | tf_op jit(solution)/shard_map/ppermute | solution.py:38
  26.4 0.5 %backward_second.1.part = f32[8,32,128]{2,1,0:T(8,128)S(1)} custom-call(s32[2,8]{1,0:T(2,128)S(1)} %bitcast.14, bf16[1,2,32,512]{3,2,1,0:T(8,128)(2,1)S(1)} %bitcast.9, bf16[8,2,1024,128]{3,2,1,0:T(8,128)(2,1)S(1)} %copy-done, f32[8,32,128]{2,1,0:T(8,128)S(1)} %backward_first.1.first, bf16[2,32,512]{2,1,0:T(8,128)(2,1)S(1)} %get-tuple-element.21.half.rest_0_, ...), custom_call_target="tpu_custom_call" | custom-call | flops 67108864 | bytes 2097152 | tf_op jit(solution)/shard_map/backward_second/pallas_call | solution.py:294
  27.0 1.3 %backward.1 = (f32[8,32,128]{2,1,0:T(8,128)}, f32[2,32,256]{2,1,0:T(8,128)}) custom-call(s32[2,8]{1,0:T(2,128)S(1)} %bitcast.15, f32[2,32,256]{2,1,0:T(8,128)S(1)} %get-tuple-element.19.full, bf16[8,32,128]{2,1,0:T(8,128)(2,1)S(1)} %get-tuple-element.20.solved, f32[8,32,128]{2,1,0:T(8,128)S(1)} %backward_second.1.part, ...), custom_call_target="tpu_custom_call" | custom-call | flops 134217728 | bytes 3145728 | tf_op jit(solution)/shard_map/backward/pallas_call | solution.py:305
  (20 shorter events, 0.4 us)
Async XLA Ops:
  0.6 3.2 %copy-start.2 = (bf16[2,1024,256]{2,1,0:T(8,128)(2,1)S(1)}, bf16[2,1024,256]{2,1,0:T(8,128)(2,1)}, u32[]{:S(2)}) copy-start(bf16[2,1024,256]{2,1,0:T(8,128)(2,1)} %lower) | copy-start | bytes 3145732
  3.3 1.2 %copy-start.1 = (bf16[2,1024,256]{2,1,0:T(8,128)(2,1)S(1)}, bf16[2,1024,256]{2,1,0:T(8,128)(2,1)}, u32[]{:S(2)}) copy-start(bf16[2,1024,256]{2,1,0:T(8,128)(2,1)} %upper.3) | copy-start | bytes 3145732
  3.3 1.5 %collective-permute-start = (bf16[2,32,1024]{2,1,0:T(8,128)(2,1)S(1)}, bf16[2,32,1024]{2,1,0:T(8,128)(2,1)S(1)}, u32[]{:S(2)}, u32[]{:S(2)}) collective-permute-start(bf16[2,32,1024]{2,1,0:T(8,128)(2,1)S(1)} %get-tuple-element.14), channel_id=1, source_target_pairs={{0,1},{1,0},{2,3},{3,2},{4,5},{5,4},{6,7},{7,6},{8,9},{9,8},{10,11... | collective-permute-start | bytes 393224 | tf_op jit(solution)/shard_map/ppermute | solution.py:38
  4.6 11.1 %copy-start.4 = (bf16[2,32,1024]{2,1,0:T(8,128)(2,1)S(1)}, bf16[2,32,1024]{2,1,0:T(8,128)(2,1)}, u32[]{:S(2)}) copy-start(bf16[2,32,1024]{2,1,0:T(8,128)(2,1)} %rhs.1) | copy-start | bytes 393220
  4.8 10.8 %collective-permute-start.1 = (bf16[3,1024,256]{2,1,0:T(8,128)(2,1)S(1)}, bf16[3,1024,256]{2,1,0:T(8,128)(2,1)S(1)}, u32[]{:S(2)}, u32[]{:S(2)}) collective-permute-start(bf16[3,1024,256]{2,1,0:T(8,128)(2,1)S(1)} %pad_maximum_fusion), channel_id=1, source_target_pairs={{0,1},{1,0},{2,3},{3,2},{4,5},{5,4},{6,7},{7,6},{8,9},{9,8},{10,11... | collective-permute-start | bytes 4718600 | tf_op jit(solution)/shard_map/ppermute | solution.py:38
  5.3 9.4 %collective-permute-start.2 = (bf16[32,1024]{1,0:T(8,128)(2,1)S(1)}, bf16[32,1024]{1,0:T(8,128)(2,1)S(1)}, u32[]{:S(2)}, u32[]{:S(2)}) collective-permute-start(bf16[32,1024]{1,0:T(8,128)(2,1)S(1)} %get-tuple-element.23), channel_id=1, source_target_pairs={{0,6},{1,7},{2,4},{3,5},{4,10},{5,11},{6,8},{7,9},{8,14},{9,15},{1... | collective-permute-start | bytes 196616 | tf_op jit(solution)/shard_map/ppermute | solution.py:38
  8.9 5.8 %collective-permute-start.3 = (bf16[32,1024]{1,0:T(8,128)(2,1)S(1)}, bf16[32,1024]{1,0:T(8,128)(2,1)S(1)}, u32[]{:S(2)}, u32[]{:S(2)}) collective-permute-start(bf16[32,1024]{1,0:T(8,128)(2,1)S(1)} %get-tuple-element.22), channel_id=1, source_target_pairs={{0,3},{1,2},{2,1},{3,0},{4,7},{5,6},{6,5},{7,4},{8,11},{9,10},{10,... | collective-permute-start | bytes 196616 | tf_op jit(solution)/shard_map/ppermute | solution.py:38
  9.1 6.5 %collective-permute-start.4 = (bf16[32,1024]{1,0:T(8,128)(2,1)S(1)}, bf16[32,1024]{1,0:T(8,128)(2,1)S(1)}, u32[]{:S(2)}, u32[]{:S(2)}) collective-permute-start(bf16[32,1024]{1,0:T(8,128)(2,1)S(1)} %get-tuple-element.23), channel_id=1, source_target_pairs={{0,5},{1,4},{2,7},{3,6},{4,9},{5,8},{6,11},{7,10},{8,13},{9,12},{1... | collective-permute-start | bytes 196616 | tf_op jit(solution)/shard_map/ppermute | solution.py:38
  15.9 3.4 %collective-permute-start.6 = (bf16[32,512]{1,0:T(8,128)(2,1)S(1)}, bf16[32,512]{1,0:T(8,128)(2,1)S(1)}, u32[]{:S(2)}, u32[]{:S(2)}) collective-permute-start(bf16[32,512]{1,0:T(8,128)(2,1)S(1)} %parent_forward.1.mine), channel_id=1, source_target_pairs={{0,3},{1,2},{2,1},{3,0},{4,7},{5,6},{6,5},{7,4},{8,11},{9,10},{10,... | collective-permute-start | bytes 98312 | tf_op jit(solution)/shard_map/ppermute | solution.py:38
  17.5 2.2 %collective-permute-start.5 = (bf16[32,512]{1,0:T(8,128)(2,1)S(1)}, bf16[32,512]{1,0:T(8,128)(2,1)S(1)}, u32[]{:S(2)}, u32[]{:S(2)}) collective-permute-start(bf16[32,512]{1,0:T(8,128)(2,1)S(1)} %parent_forward.1.mine), channel_id=1, source_target_pairs={{0,1},{1,0},{2,3},{3,2},{4,5},{5,4},{6,7},{7,6},{8,9},{9,8},{10,11... | collective-permute-start | bytes 98312 | tf_op jit(solution)/shard_map/ppermute | solution.py:38
  19.4 1.2 %collective-permute-start.7 = (bf16[1,32,512]{2,1,0:T(8,128)(2,1)S(1)}, bf16[1,32,512]{2,1,0:T(8,128)(2,1)S(1)}, u32[]{:S(2)}, u32[]{:S(2)}) collective-permute-start(bf16[1,32,512]{2,1,0:T(8,128)(2,1)S(1)} %bitcast.10), channel_id=1, source_target_pairs={{0,1},{1,0},{2,3},{3,2},{4,5},{5,4},{6,7},{7,6},{8,9},{9,8},{10,11... | collective-permute-start | bytes 98312 | tf_op jit(solution)/shard_map/ppermute | solution.py:38
  19.7 6.3 %copy-start = (bf16[8,2,1024,128]{3,2,1,0:T(8,128)(2,1)S(1)}, bf16[8,2,1024,128]{3,2,1,0:T(8,128)(2,1)}, u32[]{:S(2)}) copy-start(bf16[8,2,1024,128]{3,2,1,0:T(8,128)(2,1)} %blocks.5) | copy-start | bytes 12582916
  20.0 6.0 %copy-start.3 = (bf16[8,128,128]{2,1,0:T(8,128)(2,1)S(1)}, bf16[8,128,128]{2,1,0:T(8,128)(2,1)}, u32[]{:S(2)}) copy-start(bf16[8,128,128]{2,1,0:T(8,128)(2,1)} %upper.5) | copy-start | bytes 786436
  20.0 6.0 %copy-start.5 = (s32[8,2]{0,1:T(2,128)S(1)}, s32[8,2]{0,1:T(2,128)}, u32[]{:S(2)}) copy-start(s32[8,2]{0,1:T(2,128)} %param.17) | copy-start | bytes 196
  20.9 4.7 %collective-permute-start.8 = (bf16[2,32,512]{2,1,0:T(8,128)(2,1)S(1)}, bf16[2,32,512]{2,1,0:T(8,128)(2,1)S(1)}, u32[]{:S(2)}, u32[]{:S(2)}) collective-permute-start(bf16[2,32,512]{2,1,0:T(8,128)(2,1)S(1)} %get-tuple-element.21.half.rest_0_), channel_id=1, source_target_pairs={{0,29},{1,30},{2,31},{3,28},{4,1},{5,2},{6,3},{7,0},{8,5},{9,6},{1... | collective-permute-start | bytes 196616 | tf_op jit(solution)/shard_map/ppermute | solution.py:38
  22.7 3.7 %collective-permute-start.9 = (bf16[2,32,512]{2,1,0:T(8,128)(2,1)S(1)}, bf16[2,32,512]{2,1,0:T(8,128)(2,1)S(1)}, u32[]{:S(2)}, u32[]{:S(2)}) collective-permute-start(bf16[2,32,512]{2,1,0:T(8,128)(2,1)S(1)} %get-tuple-element.21.half.rest_0_), channel_id=1, source_target_pairs={{0,3},{1,2},{2,1},{3,0},{4,7},{5,6},{6,5},{7,4},{8,11},{9,10},{10,... | collective-permute-start | bytes 196616 | tf_op jit(solution)/shard_map/ppermute | solution.py:38
  25.6 1.3 %collective-permute-start.10 = (bf16[1,2,32,512]{3,2,1,0:T(8,128)(2,1)S(1)}, bf16[1,2,32,512]{3,2,1,0:T(8,128)(2,1)S(1)}, u32[]{:S(2)}, u32[]{:S(2)}) collective-permute-start(bf16[1,2,32,512]{3,2,1,0:T(8,128)(2,1)S(1)} %bitcast.7), channel_id=1, source_target_pairs={{0,1},{1,0},{2,3},{3,2},{4,5},{5,4},{6,7},{7,6},{8,9},{9,8},{10,11... | collective-permute-start | bytes 196616 | tf_op jit(solution)/shard_map/ppermute | solution.py:38

commit v11 on v9

--- a/solution.py
+++ b/solution.py
@@ -107,7 +107,7 @@
     return dot(forward, upper[of, rows, :]), dot(forward, across[1 + of, rows, :])
 
 
-def parent_early_kernel(mine, theirs, upper, across, part_ref):
+def parent_early_kernel(mine, theirs, upper, across, leaf_upper, part_ref):
     chip, core, parent = place()
     cut = upper.shape[2]
     for of, forward in ((parent, mine), (1 - parent, theirs)):
@@ -148,7 +148,7 @@
     )
 
 
-def backward_first_kernel(targets, nexts, half, blocks, upper, part_ref, window):
+def backward_first_kernel(targets, nexts, half, blocks, part_ref, window):
     chip, core, _ = place()
     depth = half.shape[2]
     rows = columns(chip, depth)
@@ -259,13 +259,13 @@
     other_half = go(half, by_row=0, target=along(0, 1))
     part = pl.pallas_call(
         parent_early_kernel,
-        in_specs=[VMEM] * 4,
+        in_specs=[VMEM] * 5,
         out_specs=VMEM,
         out_shape=jax.ShapeDtypeStruct((2, nrhs, depth), F32),
         compiler_params=pltpu.CompilerParams(vmem_limit_bytes=16 << 20),
         cost_estimate=pl.CostEstimate(flops=1 << 26, bytes_accessed=2 << 20, transcendentals=0),
         name="parent_early",
-    )(half, other_half, upper, across)
+    )(half, other_half, upper, across, leaf_upper)
     theirs = go(mine, by_row=0, target=along(0, 1))
 
     full, half = pl.pallas_call(
@@ -284,14 +284,14 @@
 
     first = pl.pallas_call(
         backward_first_kernel,
-        in_specs=[VMEM] * 5,
+        in_specs=[VMEM] * 4,
         out_specs=VMEM,
         out_shape=jax.ShapeDtypeStruct((leaves, nrhs, width), F32),
         scratch_shapes=[pltpu.VMEM((4, nrhs, depth), BF16)],
         compiler_params=pltpu.CompilerParams(vmem_limit_bytes=16 << 20),
         cost_estimate=pl.CostEstimate(flops=1 << 26, bytes_accessed=2 << 20, transcendentals=0),
         name="backward_first",
-    )(listed, mine, half, upper_blocks, leaf_upper)
+    )(listed, mine, half, upper_blocks)
     part = pl.pallas_call(
         backward_second_kernel,
         in_specs=[VMEM] * (4 + chips),

time: 28.6 us -> 28.6 us (level)
  no operation moved by 1% of the time
where the time goes in v11:
time: 28.6 us; the launch traced here: 28.2 us
  starting transfers between devices  12 us (42%)
  waiting for transfers between devices  9.28 us (32%)
  Pallas kernels  5.36 us (19%)
  between operations  0.72 us (3%)
  local copies, waits for them, and re-layouts  0.71 us (2%)
    ppermute x11, starting transfers between devices, send(): return lax.ppermute(array, ('row', 'col'), pairs)  12 us
    ppermute x11, waiting for transfers between devices, send(): return lax.ppermute(array, ('row', 'col'), pairs)  9.28 us
    pallas_call x1, Pallas kernels, local(): pl.pallas_call(forward_kernel, in_specs=[HBM] * 4, out_specs=[VMEM] * 3,...  2.68 us
    pallas_call x1, Pallas kernels, local(): pl.pallas_call(backward_kernel, in_specs=[VMEM] * (7 + chips), out_specs=...  1.29 us
    unnamed x12, local copies, waits for them, and re-layouts  0.68 us
  transfers between devices with their start and end apart: 11, of which 7 were waited for; matrix products, arithmetic and copies ran while one was open for 1% of the time, Pallas kernels for 3%

profile of v11, /device:TPU:0, one launch (start us, length us, event | category | flops | bytes accessed | tf_op | source)
XLA Modules:
  0.0 28.2 jit_solution(11273590382130215777)
XLA Ops:
  0.6 2.7 %forward.1 = (bf16[8,32,128]{2,1,0:T(8,128)(2,1)S(1)}, f32[2,32,1024]{2,1,0:T(8,128)S(1)}, bf16[2,32,1024]{2,1,0:T(8,128)(2,1)S(1)}) custom-call(s32[2,8]{1,0:T(2,128)} %bitcast.12, bf16[8,32,128]{2,1,0:T(8,128)(2,1)} %rhs_hbm.1, bf16[8,128,128]{2,1,0:T(8,128)(2,1)} %lower_hbm.1, bf16[8,2,128,1024]{3,2,1,0:T(8,128)(2,1)} %blocks_hbm.1), custom_call_target="tpu_custom_call" | custom-call | flops 536870912 | bytes 5242880 | tf_op jit(solution)/shard_map/forward/pallas_call | solution.py:215
  3.3 0.5 %collective-permute-start = (bf16[2,32,1024]{2,1,0:T(8,128)(2,1)S(1)}, bf16[2,32,1024]{2,1,0:T(8,128)(2,1)S(1)}, u32[]{:S(2)}, u32[]{:S(2)}) collective-permute-start(bf16[2,32,1024]{2,1,0:T(8,128)(2,1)S(1)} %get-tuple-element.14), channel_id=1, source_target_pairs={{0,1},{1,0},{2,3},{3,2},{4,5},{5,4},{6,7},{7,6},{8,9},{9,8},{10,11... | collective-permute-start | bytes 393224 | tf_op jit(solution)/shard_map/ppermute | solution.py:38
  3.9 0.7 %copy-done.1 = bf16[2,1024,256]{2,1,0:T(8,128)(2,1)S(1)} copy-done((bf16[2,1024,256]{2,1,0:T(8,128)(2,1)S(1)}, bf16[2,1024,256]{2,1,0:T(8,128)(2,1)}, u32[]{:S(2)}) %copy-start.1) | copy-done | bytes 1048600
  4.8 0.4 %collective-permute-start.1 = (bf16[3,1024,256]{2,1,0:T(8,128)(2,1)S(1)}, bf16[3,1024,256]{2,1,0:T(8,128)(2,1)S(1)}, u32[]{:S(2)}, u32[]{:S(2)}) collective-permute-start(bf16[3,1024,256]{2,1,0:T(8,128)(2,1)S(1)} %pad_maximum_fusion), channel_id=1, source_target_pairs={{0,1},{1,0},{2,3},{3,2},{4,5},{5,4},{6,7},{7,6},{8,9},{9,8},{10,11... | collective-permute-start | bytes 4718600 | tf_op jit(solution)/shard_map/ppermute | solution.py:38
  5.3 3.6 %collective-permute-start.2 = (bf16[32,1024]{1,0:T(8,128)(2,1)S(1)}, bf16[32,1024]{1,0:T(8,128)(2,1)S(1)}, u32[]{:S(2)}, u32[]{:S(2)}) collective-permute-start(bf16[32,1024]{1,0:T(8,128)(2,1)S(1)} %get-tuple-element.23), channel_id=1, source_target_pairs={{0,6},{1,7},{2,4},{3,5},{4,10},{5,11},{6,8},{7,9},{8,14},{9,15},{1... | collective-permute-start | bytes 196616 | tf_op jit(solution)/shard_map/ppermute | solution.py:38
  8.9 0.2 collective-permute-start.3
  9.1 1.6 %collective-permute-start.4 = (bf16[32,1024]{1,0:T(8,128)(2,1)S(1)}, bf16[32,1024]{1,0:T(8,128)(2,1)S(1)}, u32[]{:S(2)}, u32[]{:S(2)}) collective-permute-start(bf16[32,1024]{1,0:T(8,128)(2,1)S(1)} %get-tuple-element.23), channel_id=1, source_target_pairs={{0,5},{1,4},{2,7},{3,6},{4,9},{5,8},{6,11},{7,10},{8,13},{9,12},{1... | collective-permute-start | bytes 196616 | tf_op jit(solution)/shard_map/ppermute | solution.py:38
  10.7 4.0 %collective-permute-done.2.rest_0_ = bf16[32,1024]{1,0:T(8,128)(2,1)S(1)} collective-permute-done((bf16[32,1024]{1,0:T(8,128)(2,1)S(1)}, bf16[32,1024]{1,0:T(8,128)(2,1)S(1)}, u32[]{:S(2)}, u32[]{:S(2)}) %collective-permute-start.2) | collective-permute-done | bytes 65568 | tf_op jit(solution)/shard_map/ppermute | solution.py:38
  14.7 1.0 %collective-permute-done.4.rest_2_ = bf16[32,1024]{1,0:T(8,128)(2,1)S(1)} collective-permute-done((bf16[32,1024]{1,0:T(8,128)(2,1)S(1)}, bf16[32,1024]{1,0:T(8,128)(2,1)S(1)}, u32[]{:S(2)}, u32[]{:S(2)}) %collective-permute-start.4) | collective-permute-done | bytes 65568 | tf_op jit(solution)/shard_map/ppermute | solution.py:38
  15.7 0.3 parent_forward.1.mine
  15.9 1.6 %collective-permute-start.6 = (bf16[32,512]{1,0:T(8,128)(2,1)S(1)}, bf16[32,512]{1,0:T(8,128)(2,1)S(1)}, u32[]{:S(2)}, u32[]{:S(2)}) collective-permute-start(bf16[32,512]{1,0:T(8,128)(2,1)S(1)} %parent_forward.1.mine), channel_id=1, source_target_pairs={{0,3},{1,2},{2,1},{3,0},{4,7},{5,6},{6,5},{7,4},{8,11},{9,10},{10,... | collective-permute-start | bytes 98312 | tf_op jit(solution)/shard_map/ppermute | solution.py:38
  17.5 0.1 collective-permute-start.5
  17.6 1.7 %collective-permute-done.6 = bf16[32,512]{1,0:T(8,128)(2,1)S(1)} collective-permute-done((bf16[32,512]{1,0:T(8,128)(2,1)S(1)}, bf16[32,512]{1,0:T(8,128)(2,1)S(1)}, u32[]{:S(2)}, u32[]{:S(2)}) %collective-permute-start.6) | collective-permute-done | bytes 32800 | tf_op jit(solution)/shard_map/ppermute | solution.py:38
  19.4 0.4 %collective-permute-start.7 = (bf16[1,32,512]{2,1,0:T(8,128)(2,1)S(1)}, bf16[1,32,512]{2,1,0:T(8,128)(2,1)S(1)}, u32[]{:S(2)}, u32[]{:S(2)}) collective-permute-start(bf16[1,32,512]{2,1,0:T(8,128)(2,1)S(1)} %bitcast.10), channel_id=1, source_target_pairs={{0,1},{1,0},{2,3},{3,2},{4,5},{5,4},{6,7},{7,6},{8,9},{9,8},{10,11... | collective-permute-start | bytes 98312 | tf_op jit(solution)/shard_map/ppermute | solution.py:38
  19.7 0.3 %parent_early.1.part = f32[2,32,512]{2,1,0:T(8,128)S(1)} custom-call(bf16[32,512]{1,0:T(8,128)(2,1)S(1)} %parent_forward.1.mine, bf16[32,512]{1,0:T(8,128)(2,1)S(1)} %collective-permute-done.5.theirs, bf16[2,1024,256]{2,1,0:T(8,128)(2,1)S(1)} %copy-done.1, bf16[3,1024,256]{2,1,0:T(8,128)(2,1)S(1)} %collective-permute-done.1.across, ...), custom_call_target="tpu_custom_call" | custom-call | flops 67108864 | bytes 2097152 | tf_op jit(solution)/shard_map/parent_early/pallas_call | solution.py:260
  20.0 0.6 %collective-permute-done.7.theirs = bf16[1,32,512]{2,1,0:T(8,128)(2,1)S(1)} collective-permute-done((bf16[1,32,512]{2,1,0:T(8,128)(2,1)S(1)}, bf16[1,32,512]{2,1,0:T(8,128)(2,1)S(1)}, u32[]{:S(2)}, u32[]{:S(2)}) %collective-permute-start.7) | collective-permute-done | bytes 32800 | tf_op jit(solution)/shard_map/ppermute | solution.py:38
  20.6 0.3 %parent_backward.1 = (f32[2,32,256]{2,1,0:T(8,128)S(1)}, bf16[2,32,512]{2,1,0:T(8,128)(2,1)S(1)}) custom-call(f32[2,32,512]{2,1,0:T(8,128)S(1)} %parent_early.1.part, bf16[1,32,512]{2,1,0:T(8,128)(2,1)S(1)} %bitcast.11, bf16[1,32,512]{2,1,0:T(8,128)(2,1)S(1)} %collective-permute-done.7.theirs, bf16[2,1024,256]{2,1,0:T(8,128)(2,1)S(1)} %copy-done.1, ...), custom_call_target="tpu_custom_call" | custom-call | flops 67108864 | bytes 2097152 | tf_op jit(solution)/shard_map/parent_backward/pallas_call | solution.py:271
  20.9 1.8 %collective-permute-start.8 = (bf16[2,32,512]{2,1,0:T(8,128)(2,1)S(1)}, bf16[2,32,512]{2,1,0:T(8,128)(2,1)S(1)}, u32[]{:S(2)}, u32[]{:S(2)}) collective-permute-start(bf16[2,32,512]{2,1,0:T(8,128)(2,1)S(1)} %get-tuple-element.21.half.rest_0_), channel_id=1, source_target_pairs={{0,29},{1,30},{2,31},{3,28},{4,1},{5,2},{6,3},{7,0},{8,5},{9,6},{1... | collective-permute-start | bytes 196616 | tf_op jit(solution)/shard_map/ppermute | solution.py:38
  22.7 1.4 %collective-permute-start.9 = (bf16[2,32,512]{2,1,0:T(8,128)(2,1)S(1)}, bf16[2,32,512]{2,1,0:T(8,128)(2,1)S(1)}, u32[]{:S(2)}, u32[]{:S(2)}) collective-permute-start(bf16[2,32,512]{2,1,0:T(8,128)(2,1)S(1)} %get-tuple-element.21.half.rest_0_), channel_id=1, source_target_pairs={{0,3},{1,2},{2,1},{3,0},{4,7},{5,6},{6,5},{7,4},{8,11},{9,10},{10,... | collective-permute-start | bytes 196616 | tf_op jit(solution)/shard_map/ppermute | solution.py:38
  24.2 1.5 %collective-permute-done.8 = bf16[2,32,512]{2,1,0:T(8,128)(2,1)S(1)} collective-permute-done((bf16[2,32,512]{2,1,0:T(8,128)(2,1)S(1)}, bf16[2,32,512]{2,1,0:T(8,128)(2,1)S(1)}, u32[]{:S(2)}, u32[]{:S(2)}) %collective-permute-start.8) | collective-permute-done | bytes 65568 | tf_op jit(solution)/shard_map/ppermute | solution.py:38
  25.6 0.3 %collective-permute-start.10 = (bf16[1,2,32,512]{3,2,1,0:T(8,128)(2,1)S(1)}, bf16[1,2,32,512]{3,2,1,0:T(8,128)(2,1)S(1)}, u32[]{:S(2)}, u32[]{:S(2)}) collective-permute-start(bf16[1,2,32,512]{3,2,1,0:T(8,128)(2,1)S(1)} %bitcast.7), channel_id=1, source_target_pairs={{0,1},{1,0},{2,3},{3,2},{4,5},{5,4},{6,7},{7,6},{8,9},{9,8},{10,11... | collective-permute-start | bytes 196616 | tf_op jit(solution)/shard_map/ppermute | solution.py:38
  26.0 0.4 %collective-permute-done.9.rest_1_ = bf16[2,32,512]{2,1,0:T(8,128)(2,1)S(1)} collective-permute-done((bf16[2,32,512]{2,1,0:T(8,128)(2,1)S(1)}, bf16[2,32,512]{2,1,0:T(8,128)(2,1)S(1)}, u32[]{:S(2)}, u32[]{:S(2)}) %collective-permute-start.9) | collective-permute-done | bytes 65568 | tf_op jit(solution)/shard_map/ppermute | solution.py:38
  26.4 0.5 %backward_second.1.part = f32[8,32,128]{2,1,0:T(8,128)S(1)} custom-call(s32[2,8]{1,0:T(2,128)S(1)} %bitcast.14, bf16[1,2,32,512]{3,2,1,0:T(8,128)(2,1)S(1)} %bitcast.9, bf16[8,2,1024,128]{3,2,1,0:T(8,128)(2,1)S(1)} %copy-done, f32[8,32,128]{2,1,0:T(8,128)S(1)} %backward_first.1.first, bf16[2,32,512]{2,1,0:T(8,128)(2,1)S(1)} %get-tuple-element.21.half.rest_0_, ...), custom_call_target="tpu_custom_call" | custom-call | flops 67108864 | bytes 2097152 | tf_op jit(solution)/shard_map/backward_second/pallas_call | solution.py:295
  27.0 1.3 %backward.1 = (f32[8,32,128]{2,1,0:T(8,128)}, f32[2,32,256]{2,1,0:T(8,128)}) custom-call(s32[2,8]{1,0:T(2,128)S(1)} %bitcast.15, f32[2,32,256]{2,1,0:T(8,128)S(1)} %get-tuple-element.19.full, bf16[8,32,128]{2,1,0:T(8,128)(2,1)S(1)} %get-tuple-element.20.solved, f32[8,32,128]{2,1,0:T(8,128)S(1)} %backward_second.1.part, ...), custom_call_target="tpu_custom_call" | custom-call | flops 134217728 | bytes 3145728 | tf_op jit(solution)/shard_map/backward/pallas_call | solution.py:306
  (20 shorter events, 0.4 us)
Async XLA Ops:
  0.6 3.2 %copy-start.2 = (bf16[2,1024,256]{2,1,0:T(8,128)(2,1)S(1)}, bf16[2,1024,256]{2,1,0:T(8,128)(2,1)}, u32[]{:S(2)}) copy-start(bf16[2,1024,256]{2,1,0:T(8,128)(2,1)} %lower) | copy-start | bytes 3145732
  3.3 1.2 %copy-start.1 = (bf16[2,1024,256]{2,1,0:T(8,128)(2,1)S(1)}, bf16[2,1024,256]{2,1,0:T(8,128)(2,1)}, u32[]{:S(2)}) copy-start(bf16[2,1024,256]{2,1,0:T(8,128)(2,1)} %upper.2) | copy-start | bytes 3145732
  3.3 1.5 %collective-permute-start = (bf16[2,32,1024]{2,1,0:T(8,128)(2,1)S(1)}, bf16[2,32,1024]{2,1,0:T(8,128)(2,1)S(1)}, u32[]{:S(2)}, u32[]{:S(2)}) collective-permute-start(bf16[2,32,1024]{2,1,0:T(8,128)(2,1)S(1)} %get-tuple-element.14), channel_id=1, source_target_pairs={{0,1},{1,0},{2,3},{3,2},{4,5},{5,4},{6,7},{7,6},{8,9},{9,8},{10,11... | collective-permute-start | bytes 393224 | tf_op jit(solution)/shard_map/ppermute | solution.py:38
  4.6 11.1 %copy-start.4 = (bf16[2,32,1024]{2,1,0:T(8,128)(2,1)S(1)}, bf16[2,32,1024]{2,1,0:T(8,128)(2,1)}, u32[]{:S(2)}) copy-start(bf16[2,32,1024]{2,1,0:T(8,128)(2,1)} %rhs.1) | copy-start | bytes 393220
  4.8 10.8 %collective-permute-start.1 = (bf16[3,1024,256]{2,1,0:T(8,128)(2,1)S(1)}, bf16[3,1024,256]{2,1,0:T(8,128)(2,1)S(1)}, u32[]{:S(2)}, u32[]{:S(2)}) collective-permute-start(bf16[3,1024,256]{2,1,0:T(8,128)(2,1)S(1)} %pad_maximum_fusion), channel_id=1, source_target_pairs={{0,1},{1,0},{2,3},{3,2},{4,5},{5,4},{6,7},{7,6},{8,9},{9,8},{10,11... | collective-permute-start | bytes 4718600 | tf_op jit(solution)/shard_map/ppermute | solution.py:38
  5.3 9.4 %collective-permute-start.2 = (bf16[32,1024]{1,0:T(8,128)(2,1)S(1)}, bf16[32,1024]{1,0:T(8,128)(2,1)S(1)}, u32[]{:S(2)}, u32[]{:S(2)}) collective-permute-start(bf16[32,1024]{1,0:T(8,128)(2,1)S(1)} %get-tuple-element.23), channel_id=1, source_target_pairs={{0,6},{1,7},{2,4},{3,5},{4,10},{5,11},{6,8},{7,9},{8,14},{9,15},{1... | collective-permute-start | bytes 196616 | tf_op jit(solution)/shard_map/ppermute | solution.py:38
  8.9 10.8 %copy-start.3 = (bf16[8,128,128]{2,1,0:T(8,128)(2,1)S(1)}, bf16[8,128,128]{2,1,0:T(8,128)(2,1)}, u32[]{:S(2)}) copy-start(bf16[8,128,128]{2,1,0:T(8,128)(2,1)} %upper.3) | copy-start | bytes 786436
  8.9 5.8 %collective-permute-start.3 = (bf16[32,1024]{1,0:T(8,128)(2,1)S(1)}, bf16[32,1024]{1,0:T(8,128)(2,1)S(1)}, u32[]{:S(2)}, u32[]{:S(2)}) collective-permute-start(bf16[32,1024]{1,0:T(8,128)(2,1)S(1)} %get-tuple-element.22), channel_id=1, source_target_pairs={{0,3},{1,2},{2,1},{3,0},{4,7},{5,6},{6,5},{7,4},{8,11},{9,10},{10,... | collective-permute-start | bytes 196616 | tf_op jit(solution)/shard_map/ppermute | solution.py:38
  9.1 6.5 %collective-permute-start.4 = (bf16[32,1024]{1,0:T(8,128)(2,1)S(1)}, bf16[32,1024]{1,0:T(8,128)(2,1)S(1)}, u32[]{:S(2)}, u32[]{:S(2)}) collective-permute-start(bf16[32,1024]{1,0:T(8,128)(2,1)S(1)} %get-tuple-element.23), channel_id=1, source_target_pairs={{0,5},{1,4},{2,7},{3,6},{4,9},{5,8},{6,11},{7,10},{8,13},{9,12},{1... | collective-permute-start | bytes 196616 | tf_op jit(solution)/shard_map/ppermute | solution.py:38
  15.9 3.4 %collective-permute-start.6 = (bf16[32,512]{1,0:T(8,128)(2,1)S(1)}, bf16[32,512]{1,0:T(8,128)(2,1)S(1)}, u32[]{:S(2)}, u32[]{:S(2)}) collective-permute-start(bf16[32,512]{1,0:T(8,128)(2,1)S(1)} %parent_forward.1.mine), channel_id=1, source_target_pairs={{0,3},{1,2},{2,1},{3,0},{4,7},{5,6},{6,5},{7,4},{8,11},{9,10},{10,... | collective-permute-start | bytes 98312 | tf_op jit(solution)/shard_map/ppermute | solution.py:38
  17.5 2.2 %collective-permute-start.5 = (bf16[32,512]{1,0:T(8,128)(2,1)S(1)}, bf16[32,512]{1,0:T(8,128)(2,1)S(1)}, u32[]{:S(2)}, u32[]{:S(2)}) collective-permute-start(bf16[32,512]{1,0:T(8,128)(2,1)S(1)} %parent_forward.1.mine), channel_id=1, source_target_pairs={{0,1},{1,0},{2,3},{3,2},{4,5},{5,4},{6,7},{7,6},{8,9},{9,8},{10,11... | collective-permute-start | bytes 98312 | tf_op jit(solution)/shard_map/ppermute | solution.py:38
  19.4 1.2 %collective-permute-start.7 = (bf16[1,32,512]{2,1,0:T(8,128)(2,1)S(1)}, bf16[1,32,512]{2,1,0:T(8,128)(2,1)S(1)}, u32[]{:S(2)}, u32[]{:S(2)}) collective-permute-start(bf16[1,32,512]{2,1,0:T(8,128)(2,1)S(1)} %bitcast.10), channel_id=1, source_target_pairs={{0,1},{1,0},{2,3},{3,2},{4,5},{5,4},{6,7},{7,6},{8,9},{9,8},{10,11... | collective-permute-start | bytes 98312 | tf_op jit(solution)/shard_map/ppermute | solution.py:38
  19.7 6.3 %copy-start = (bf16[8,2,1024,128]{3,2,1,0:T(8,128)(2,1)S(1)}, bf16[8,2,1024,128]{3,2,1,0:T(8,128)(2,1)}, u32[]{:S(2)}) copy-start(bf16[8,2,1024,128]{3,2,1,0:T(8,128)(2,1)} %blocks.5) | copy-start | bytes 12582916
  20.0 6.0 %copy-start.5 = (s32[8,2]{0,1:T(2,128)S(1)}, s32[8,2]{0,1:T(2,128)}, u32[]{:S(2)}) copy-start(s32[8,2]{0,1:T(2,128)} %param.17) | copy-start | bytes 196
  20.9 4.7 %collective-permute-start.8 = (bf16[2,32,512]{2,1,0:T(8,128)(2,1)S(1)}, bf16[2,32,512]{2,1,0:T(8,128)(2,1)S(1)}, u32[]{:S(2)}, u32[]{:S(2)}) collective-permute-start(bf16[2,32,512]{2,1,0:T(8,128)(2,1)S(1)} %get-tuple-element.21.half.rest_0_), channel_id=1, source_target_pairs={{0,29},{1,30},{2,31},{3,28},{4,1},{5,2},{6,3},{7,0},{8,5},{9,6},{1... | collective-permute-start | bytes 196616 | tf_op jit(solution)/shard_map/ppermute | solution.py:38
  22.7 3.7 %collective-permute-start.9 = (bf16[2,32,512]{2,1,0:T(8,128)(2,1)S(1)}, bf16[2,32,512]{2,1,0:T(8,128)(2,1)S(1)}, u32[]{:S(2)}, u32[]{:S(2)}) collective-permute-start(bf16[2,32,512]{2,1,0:T(8,128)(2,1)S(1)} %get-tuple-element.21.half.rest_0_), channel_id=1, source_target_pairs={{0,3},{1,2},{2,1},{3,0},{4,7},{5,6},{6,5},{7,4},{8,11},{9,10},{10,... | collective-permute-start | bytes 196616 | tf_op jit(solution)/shard_map/ppermute | solution.py:38
  25.6 1.3 %collective-permute-start.10 = (bf16[1,2,32,512]{3,2,1,0:T(8,128)(2,1)S(1)}, bf16[1,2,32,512]{3,2,1,0:T(8,128)(2,1)S(1)}, u32[]{:S(2)}, u32[]{:S(2)}) collective-permute-start(bf16[1,2,32,512]{3,2,1,0:T(8,128)(2,1)S(1)} %bitcast.7), channel_id=1, source_target_pairs={{0,1},{1,0},{2,3},{3,2},{4,5},{5,4},{6,7},{7,6},{8,9},{9,8},{10,11... | collective-permute-start | bytes 196616 | tf_op jit(solution)/shard_map/ppermute | solution.py:38
